TPU v7x, 32 devices: a whole 2x2x4 slice. The times are simulated.
32 devices in a mesh: dp: 2 (over core), row: 4 (over y, x), col: 4 (over z).
Axes of the slice: x: 2, y: 2, z: 4, core: 2. Of those that a mesh axis runs over, the one named last changes fastest.
Arguments:
- hidden_in: bfloat16 [768, 4, 1024], P('col', 'dp', 'row')
- segments: int32 [4, 1024], P('dp'), may hold values from 0 to 2, as said below
- w_qkv: bfloat16 [3, 12, 49152], P(None, 'row', 'col'), may hold values from -0.21875 to 0.21875
- b_qkv: bfloat16 [3, 768], P(None, 'row'), may hold values from -3 to 3
- w_dense: bfloat16 [12, 49152], P('row', 'col'), may hold values from -2.5 to 2.5
- b_dense: bfloat16 [768], P('col'), may hold values from -2 to 2
- ln1_gain: bfloat16 [768], P('col'), may hold values from 0.25 to 1.75
- ln1_bias: bfloat16 [768], P('col'), may hold values from -2 to 2
- ln2_gain: bfloat16 [768], P('col'), may hold values from 0.25 to 1.75
- ln2_bias: bfloat16 [768], P('col'), may hold values from -2 to 2
- w_in: bfloat16 [768, 3072], P('col', 'row'), may hold values from -0.21875 to 0.21875
- b_in: bfloat16 [3072], P('row'), may hold values from -3 to 3
- w_out: bfloat16 [768, 3072], P('col', 'row'), may hold values from -0.109375 to 0.109375
- b_out: bfloat16 [768], P('col'), may hold values from -2 to 2
- cotangent: bfloat16 [768, 4, 1024], P('col', 'dp', 'row'), may hold values from -6 to 6
Outputs:
- layer_out: bfloat16 [768, 4, 1024], P('col', 'dp', 'row')
- grad_in: float32 [768, 4, 1024], P('col', 'dp', 'row')
- d_w_qkv: float32 [3, 12, 49152], P(None, 'row', 'col')
- d_b_qkv: float32 [3, 768], P(None, 'row')
- d_w_dense: float32 [12, 49152], P('row', 'col')
- d_b_dense: float32 [768], P('col')
- d_ln1_gain: float32 [768], P('col')
- d_ln1_bias: float32 [768], P('col')
- d_ln2_gain: float32 [768], P('col')
- d_ln2_bias: float32 [768], P('col')
- d_w_in: float32 [768, 3072], P('col', 'row')
- d_b_in: float32 [3072], P('row')
- d_w_out: float32 [768, 3072], P('col', 'row')
- d_b_out: float32 [768], P('col')
Inputs may be any that keep to these rules, and one draw needn't show every extreme that they name: `segments`: within each sequence of 1024 tokens the segment numbers never fall: 0 on its first 1 to 128 tokens, 2 on its last 1 to 128 tokens, 1 on all between.
All inputs are finite; a program needn't handle non-finite values.
Results may differ from a plain program's by a relative error of at most 0.012.
Values may be sent and summed in bfloat16 or wider, within the bound.
No kernel may reach another device: no remote copies, remote signals or barrier semaphores. Data moves between devices by JAX's collectives and lax.ppermute only.
A program may use at most 128 MiB of HBM per device.

v0:
```python
from functools import partial

import jax
import jax.numpy as jnp
from jax import lax
from jax.sharding import PartitionSpec as P

D = 768
HD = 64
ROT = 16


EPS = 1e-05


def for_sending(x):

    def short(part):
        return part.astype(jnp.bfloat16) if part.dtype == jnp.float32 else part

    return jax.tree.map(short, x)


def rotate(vector, places):
    half_rot = ROT // 2
    frequency = 10000.0 ** (-jnp.arange(half_rot, dtype=jnp.float32) * 2.0 / ROT)
    angles = places.astype(jnp.float32)[..., None] * frequency
    cosine = jnp.cos(angles)[..., None, :]
    sine_part = jnp.sin(angles)[..., None, :]
    first_half = vector[..., :half_rot]
    second = vector[..., half_rot:ROT]
    return jnp.concatenate(
        [
            first_half * cosine - second * sine_part,
            second * cosine + first_half * sine_part,
            vector[..., ROT:],
        ],
        axis=-1,
    )


def doc_places(seg_ids):
    positions = jnp.arange(seg_ids.shape[0], dtype=jnp.int32)
    previous = jnp.concatenate([seg_ids[:1], seg_ids[:-1]])
    starts = jnp.where(seg_ids != previous, positions, jnp.zeros_like(positions))
    return positions - lax.cummax(starts, axis=0)


def body(
    hidden_in,
    segments,
    w_qkv,
    b_qkv,
    w_dense,
    b_dense,
    ln1_gain,
    ln1_bias,
    ln2_gain,
    ln2_bias,
    w_in,
    b_in,
    w_out,
    b_out,
    cotangent,
):
    f32 = jnp.float32
    bf16 = jnp.bfloat16
    seq_count = segments.shape[0]
    seq_len = segments.shape[1]
    row_rows = seq_len // lax.axis_size("row")
    col_rows = seq_len // lax.axis_size("col")
    row_at = lax.axis_index("row")
    col_at = lax.axis_index("col")
    col_width = hidden_in.shape[0]
    head_count = w_qkv.shape[1]
    head_width = head_count * HD
    scale = HD ** (-0.5)
    wq_blocks = w_qkv.reshape(3, head_count, col_width, HD)
    dense_blocks = w_dense.reshape(head_count, col_width, HD)
    hidden_feat, cot_feat = (
        lax.all_gather(hidden_in, "row", axis=2, tiled=True),
        lax.all_gather(cotangent, "row", axis=2, tiled=True),
    )
    hidden_all = hidden_feat.transpose(2, 1, 0)
    cot_all = cot_feat.transpose(2, 1, 0)
    hidden_cols = hidden_all.astype(f32)
    sum_vals, square_vals = lax.psum(
        (jnp.sum(hidden_cols, axis=2), jnp.sum(hidden_cols * hidden_cols, axis=2)), "col"
    )
    mean_all = sum_vals / D
    rstd_all = lax.rsqrt(square_vals / D - mean_all * mean_all + EPS)
    normed_cols = (hidden_cols - mean_all[..., None]) * rstd_all[..., None]
    act_one = (normed_cols * ln1_gain.astype(f32) + ln1_bias.astype(f32)).astype(bf16)
    act_two = (normed_cols * ln2_gain.astype(f32) + ln2_bias.astype(f32)).astype(bf16)
    attn_part = jnp.einsum(
        "tnd,shdk->tnshk", act_one, wq_blocks, preferred_element_type=f32
    ).reshape(lax.axis_size("col") * col_rows, seq_count, 3 * head_width)
    ffn_part = jnp.einsum("tnd,df->tnf", act_two, w_in, preferred_element_type=f32)
    mixed_in = lax.psum_scatter(
        jnp.concatenate([attn_part, ffn_part], axis=2), "col", scatter_dimension=0, tiled=True
    )
    qkv_pre = mixed_in[..., : 3 * head_width]
    hidden_pre = mixed_in[..., 3 * head_width :]
    qkv_vals = (qkv_pre + b_qkv.astype(f32).reshape(-1)).reshape(
        col_rows, seq_count, 3, head_count, HD
    )
    hidden_act = hidden_pre + b_in.astype(f32)
    places = jax.vmap(doc_places)(segments).T
    q_places = lax.dynamic_slice_in_dim(places, col_at * col_rows, col_rows, 0)
    q_segs = lax.dynamic_slice_in_dim(segments, col_at * col_rows, col_rows, 1)
    rot_query, rot_back = jax.vjp(lambda vector: rotate(vector, q_places), qkv_vals[:, :, 0])
    queries = rot_query.astype(bf16)
    key_local = (
        rotate(qkv_vals[:, :, 1], q_places).astype(bf16).reshape(col_rows, seq_count, head_width)
    )
    value_local = qkv_vals[:, :, 2].astype(bf16).reshape(col_rows, seq_count, head_width)
    key_all, value_all = (
        lax.all_gather(key_local, "col", axis=0, tiled=True),
        lax.all_gather(value_local, "col", axis=0, tiled=True),
    )
    key_all = key_all.reshape(seq_len, seq_count, head_count, HD)
    value_all = value_all.reshape(seq_len, seq_count, head_count, HD)
    q_index = col_at * col_rows + jnp.arange(col_rows, dtype=jnp.int32)
    k_index = jnp.arange(seq_len, dtype=jnp.int32)
    allowed = (k_index[None, None, :] <= q_index[None, :, None]) & (
        segments[:, None, :] == q_segs[:, :, None]
    )
    scores = jnp.einsum("qnhd,knhd->nhqk", queries, key_all, preferred_element_type=f32) * scale
    scores = jnp.where(allowed[:, None], scores, -1000000000.0)
    row_max = jnp.max(scores, axis=-1, keepdims=True)
    exponent = jnp.exp(scores - row_max)
    attn_probs = exponent / jnp.sum(exponent, axis=-1, keepdims=True)
    probs_low = attn_probs.astype(bf16)
    attended = (
        jnp.einsum("nhqk,knhd->qnhd", probs_low, value_all, preferred_element_type=f32)
        .astype(bf16)
        .reshape(col_rows, seq_count, head_width)
    )
    up_vals, gelu_back = jax.vjp(partial(jax.nn.gelu, approximate=False), hidden_act)
    up_low = up_vals.astype(bf16)
    attended_all, up_all = (
        lax.all_gather(for_sending(attended), "col", axis=0, tiled=True).astype(attended.dtype),
        lax.all_gather(for_sending(up_low), "col", axis=0, tiled=True).astype(up_low.dtype),
    )
    att_rows = attended_all.reshape(row_rows * lax.axis_size("row"), seq_count, head_count, HD)
    up_rows = lax.slice_in_dim(up_all, 0, row_rows * lax.axis_size("row"), axis=0)
    attn_part = jnp.einsum("tnhd,hod->tno", att_rows, dense_blocks, preferred_element_type=f32)
    branch_sum = lax.psum_scatter(
        (attn_part + jnp.einsum("tnf,of->tno", up_rows, w_out, preferred_element_type=f32)).astype(
            jnp.bfloat16
        ),
        "row",
        scatter_dimension=0,
        tiled=True,
    ).astype(jnp.float32)
    hidden_local = hidden_in.astype(f32).transpose(2, 1, 0)
    layer_out = (
        (hidden_local + branch_sum + b_dense.astype(f32) + b_out.astype(f32))
        .astype(bf16)
        .transpose(2, 1, 0)
    )
    grad_bias_out = jnp.sum(cot_all, axis=(0, 1), dtype=f32)
    grad_w_dense = jnp.einsum(
        "tnhd,tno->hod",
        attended_all.reshape(seq_len, seq_count, head_count, HD),
        cot_all,
        preferred_element_type=f32,
    ).reshape(head_count, col_width * HD)
    grad_w_out = jnp.einsum("tnf,tno->of", up_all, cot_all, preferred_element_type=f32)
    att_part = jnp.einsum(
        "tno,hod->tnhd", cot_all, dense_blocks, preferred_element_type=f32
    ).reshape(lax.axis_size("col") * col_rows, seq_count, head_width)
    up_part = jnp.einsum("tno,of->tnf", cot_all, w_out, preferred_element_type=f32)
    back_mix = lax.psum_scatter(
        jnp.concatenate([att_part, up_part], axis=2), "col", scatter_dimension=0, tiled=True
    )
    grad_att_pre = back_mix[..., :head_width]
    grad_up_pre = back_mix[..., head_width:]
    grad_att = grad_att_pre.astype(bf16).reshape(col_rows, seq_count, head_count, HD)
    grad_hidden = gelu_back(grad_up_pre)[0].astype(bf16)
    grad_probs = jnp.einsum("qnhd,knhd->nhqk", grad_att, value_all, preferred_element_type=f32)
    grad_scores = attn_probs * (
        grad_probs - jnp.sum(grad_probs * attn_probs, axis=-1, keepdims=True)
    )
    scores_low = grad_scores.astype(bf16)
    grad_query = (
        jnp.einsum("nhqk,knhd->qnhd", scores_low, key_all, preferred_element_type=f32) * scale
    )
    key_part = (
        jnp.einsum("nhqk,qnhd->knhd", scores_low, queries, preferred_element_type=f32) * scale
    )
    value_part = jnp.einsum("nhqk,qnhd->knhd", probs_low, grad_att, preferred_element_type=f32)
    grad_key, grad_value = (
        lax.psum_scatter(
            key_part.reshape(seq_len, seq_count, head_width).astype(jnp.bfloat16),
            "col",
            scatter_dimension=0,
            tiled=True,
        ).astype(jnp.float32),
        lax.psum_scatter(
            value_part.reshape(seq_len, seq_count, head_width).astype(jnp.bfloat16),
            "col",
            scatter_dimension=0,
            tiled=True,
        ).astype(jnp.float32),
    )
    query_pre = rot_back(grad_query)[0]
    key_pre = rot_back(grad_key.reshape(col_rows, seq_count, head_count, HD))[0]
    grad_qkv = (
        jnp.stack(
            [query_pre, key_pre, grad_value.reshape(col_rows, seq_count, head_count, HD)], axis=2
        )
        .astype(bf16)
        .reshape(col_rows, seq_count, 3 * head_width)
    )
    qkv_grad_all, hidden_grad_all = (
        lax.all_gather(grad_qkv, "col", axis=0, tiled=True),
        lax.all_gather(grad_hidden, "col", axis=0, tiled=True),
    )
    grad_b_qkv = jnp.sum(qkv_grad_all, axis=(0, 1), dtype=f32).reshape(3, head_width)
    grad_b_in = jnp.sum(hidden_grad_all, axis=(0, 1), dtype=f32)
    grad_w_qkv = jnp.einsum(
        "tnd,tnshk->shdk",
        act_one,
        qkv_grad_all.reshape(seq_len, seq_count, 3, head_count, HD),
        preferred_element_type=f32,
    ).reshape(3, head_count, col_width * HD)
    grad_w_in = jnp.einsum("tnd,tnf->df", act_two, hidden_grad_all, preferred_element_type=f32)
    qkv_rows = qkv_grad_all.reshape(row_rows * lax.axis_size("row"), seq_count, 3, head_count, HD)
    first_part = jnp.einsum("tnshk,shdk->tnd", qkv_rows, wq_blocks, preferred_element_type=f32)
    second_part = jnp.einsum("tnf,df->tnd", hidden_grad_all, w_in, preferred_element_type=f32)
    back_norm = lax.psum_scatter(
        jnp.concatenate([first_part, second_part], axis=2).astype(jnp.bfloat16),
        "row",
        scatter_dimension=0,
        tiled=True,
    ).astype(jnp.float32)
    grad_one = back_norm[..., :col_width]
    grad_two = back_norm[..., col_width:]
    mean_rows = lax.dynamic_slice_in_dim(mean_all, row_at * row_rows, row_rows, 0)
    rstd_rows = lax.dynamic_slice_in_dim(rstd_all, row_at * row_rows, row_rows, 0)
    normed_rows = (hidden_local - mean_rows[..., None]) * rstd_rows[..., None]
    grad_normed = grad_one * ln1_gain.astype(f32) + grad_two * ln2_gain.astype(f32)
    sum_hat, sum_cross = lax.psum(
        (jnp.sum(grad_normed, axis=2), jnp.sum(grad_normed * normed_rows, axis=2)), "col"
    )
    grad_rows = cotangent.astype(f32).transpose(2, 1, 0) + rstd_rows[..., None] * (
        grad_normed - sum_hat[..., None] / D - normed_rows * sum_cross[..., None] / D
    )
    grad_in = grad_rows.transpose(2, 1, 0)
    d_ln1_gain, d_ln1_bias, d_ln2_gain, d_ln2_bias = lax.psum(
        (
            jnp.sum(grad_one * normed_rows, axis=(0, 1)),
            jnp.sum(grad_one, axis=(0, 1)),
            jnp.sum(grad_two * normed_rows, axis=(0, 1)),
            jnp.sum(grad_two, axis=(0, 1)),
        ),
        ("dp", "row"),
    )
    d_w_qkv, d_b_qkv, d_w_dense, d_b_shared, d_w_in, d_b_in, d_w_out = (
        lax.psum(grad_w_qkv.astype(jnp.bfloat16), "dp").astype(jnp.float32),
        lax.psum(grad_b_qkv.astype(jnp.bfloat16), "dp").astype(jnp.float32),
        lax.psum(grad_w_dense.astype(jnp.bfloat16), "dp").astype(jnp.float32),
        lax.psum(grad_bias_out.astype(jnp.bfloat16), "dp").astype(jnp.float32),
        lax.psum(grad_w_in.astype(jnp.bfloat16), "dp").astype(jnp.float32),
        lax.psum(grad_b_in.astype(jnp.bfloat16), "dp").astype(jnp.float32),
        lax.psum(grad_w_out.astype(jnp.bfloat16), "dp").astype(jnp.float32),
    )
    return (
        layer_out,
        grad_in,
        d_w_qkv,
        d_b_qkv,
        d_w_dense,
        d_b_shared,
        d_ln1_gain,
        d_ln1_bias,
        d_ln2_gain,
        d_ln2_bias,
        d_w_in,
        d_b_in,
        d_w_out,
        d_b_shared,
    )


def solution(mesh):
    placed = (
        P("col", "dp", "row"),
        P("dp", None),
        P(None, "row", "col"),
        P(None, "row"),
        P("row", "col"),
        P("col"),
        P("col"),
        P("col"),
        P("col"),
        P("col"),
        P("col", "row"),
        P("row"),
        P("col", "row"),
        P("col"),
        P("col", "dp", "row"),
    )
    return jax.shard_map(
        body,
        mesh=mesh,
        in_specs=placed,
        out_specs=(
            P("col", "dp", "row"),
            P("col", "dp", "row"),
            P(None, "row", "col"),
            P(None, "row"),
            P("row", "col"),
            P("col"),
            P("col"),
            P("col"),
            P("col"),
            P("col"),
            P("col", "row"),
            P("row"),
            P("col", "row"),
            P("col"),
        ),
        check_vma=False,
    )
```

profile of v0, /device:TPU:1, one launch (start us, length us, event | category | flops | bytes accessed | tf_op | source)
XLA Modules:
  0.0 773.6 jit_solution(3577110874612753593)
XLA Ops:
  8.2 17.0 %all_gather.29 = bf16[192,2,1024]{2,0,1:T(8,128)(2,1)S(1)} all-gather(bf16[192,2,256]{2,0,1:T(8,128)(2,1)S(1)} %copy.108), channel_id=1, replica_groups=mesh['dp'=2,'row'=4,'col'=4] {'row'}, dimensions={2}, use_global_device_ids=true | all-gather | bytes 983040 | tf_op jit(solution)/shard_map/all_gather | solution.py:82
  25.3 1.2 reshape.163
  27.0 1.0 fusion.41
  28.1 3.9 pad_maximum_fusion.1
  34.3 13.2 %all_gather.24 = bf16[192,2,1024]{2,0,1:T(8,128)(2,1)S(1)} all-gather(bf16[192,2,256]{2,0,1:T(8,128)(2,1)S(1)} %copy.100), channel_id=1, replica_groups=mesh['dp'=2,'row'=4,'col'=4] {'row'}, dimensions={2}, use_global_device_ids=true | all-gather | bytes 983040 | tf_op jit(solution)/shard_map/all_gather | solution.py:81
  47.8 18.9 %all-reduce.8 = (f32[1024,2]{0,1:T(2,128)S(1)}, f32[1024,2]{0,1:T(2,128)S(1)}) all-reduce(f32[1024,2]{0,1:T(2,128)S(1)} %get-tuple-element.77, f32[1024,2]{0,1:T(2,128)S(1)} %get-tuple-element.76), channel_id=1, replica_groups=mesh['dp'=2,'row'=4,'col'=4] {'col'}, use_global_device_ids=true, to_apply=%region_3.0 | all-reduce | flops 4096 | bytes 32768 | tf_op jit(solution)/shard_map/psum | solution.py:87
  66.7 3.1 fusion.82
  69.8 3.7 fusion.67
  73.5 10.9 %pad_maximum_fusion = f32[1024,2,1344]{0,2,1:T(8,128)} fusion(f32[1024,2,768]{0,2,1:T(8,128)} %fusion.67, f32[1024,2,576]{0,2,1:T(8,128)} %fusion.82), kind=kLoop, calls=%fused_computation.1 | loop fusion | flops 2752512 | bytes 22020096 | tf_op jit(solution)/shard_map/concatenate | solution.py:100
  87.1 83.7 %reduce-scatter.11.cloned.1.call-done = f32[256,2,960]{0,2,1:T(8,128)} async-done(((f32[1024,2,960]{0,2,1:T(8,128)}), f32[256,2,960]{0,2,1:T(8,128)}) %reduce-scatter.11.cloned.1.call-update) | async-done | bytes 1966096 | tf_op jit(solution)/shard_map/reduce_scatter | solution.py:174
  170.8 1.0 slice.126
  171.9 188.4 %reduce-scatter.7.cloned.1.call-done = f32[256,2,1344]{0,2,1:T(8,128)} async-done(((f32[1024,2,1344]{0,2,1:T(8,128)}), f32[256,2,1344]{0,2,1:T(8,128)}) %reduce-scatter.7.cloned.1.call-update) | async-done | bytes 2752528 | tf_op jit(solution)/shard_map/reduce_scatter | solution.py:99
  360.2 1.4 slice_add_fusion.1
  361.9 16.8 %all_gather.26 = bf16[1024,2,192]{0,2,1:T(8,128)(2,1)S(1)} all-gather(bf16[256,2,192]{0,2,1:T(8,128)(2,1)S(1)} %bitcast.245), channel_id=1, replica_groups=mesh['dp'=2,'row'=4,'col'=4] {'col'}, dimensions={0}, use_global_device_ids=true | all-gather | bytes 983040 | tf_op jit(solution)/shard_map/all_gather | solution.py:118
  378.6 16.3 %all_gather.25 = bf16[1024,2,192]{0,2,1:T(8,128)(2,1)S(1)} all-gather(bf16[256,2,192]{0,2,1:T(8,128)(2,1)S(1)} %bitcast.244), channel_id=1, replica_groups=mesh['dp'=2,'row'=4,'col'=4] {'col'}, dimensions={0}, use_global_device_ids=true | all-gather | bytes 983040 | tf_op jit(solution)/shard_map/all_gather | solution.py:119
  394.9 5.1 fusion.86
  400.0 3.8 multiply_reduce_fusion
  404.7 1.0 multiply_convert_fusion
  405.7 1.6 multiply_convert_fusion.1
  407.4 4.7 fusion.26
  412.1 6.2 add_convert_fusion
  418.3 1.1 multiply_convert_fusion.2
  420.1 2.2 fusion.31
  423.1 10.8 %reduce-scatter.13.cloned.1.call-done = bf16[256,2,192]{0,2,1:T(8,128)(2,1)} async-done(((bf16[1024,2,192]{0,2,1:T(8,128)(2,1)}), bf16[256,2,192]{0,2,1:T(8,128)(2,1)}) %reduce-scatter.13.cloned.1.call-update) | async-done | bytes 196624 | tf_op jit(solution)/shard_map/reduce_scatter | solution.py:194
  436.6 21.9 %reduce-scatter.15.cloned.1.call-done = bf16[256,2,192]{0,2,1:T(8,128)(2,1)} async-done(((bf16[1024,2,192]{0,2,1:T(8,128)(2,1)}), bf16[256,2,192]{0,2,1:T(8,128)(2,1)}) %reduce-scatter.15.cloned.1.call-update) | async-done | bytes 196624 | tf_op jit(solution)/shard_map/reduce_scatter | solution.py:200
  460.5 4.0 fusion.32
  464.5 25.8 %all_gather.27 = bf16[1024,2,192]{0,2,1:T(8,128)(2,1)S(1)} all-gather(bf16[256,2,192]{0,2,1:T(8,128)(2,1)S(1)} %bitcast.250), channel_id=1, replica_groups=mesh['dp'=2,'row'=4,'col'=4] {'col'}, dimensions={0}, use_global_device_ids=true | all-gather | bytes 983040 | tf_op jit(solution)/shard_map/all_gather | solution.py:142
  491.7 41.9 %all-gather.4.cloned.1.call-done = bf16[1024,2,768]{0,2,1:T(8,128)(2,1)} async-done(((bf16[256,2,768]{0,2,1:T(8,128)(2,1)}), bf16[1024,2,768]{0,2,1:T(8,128)(2,1)}) %all-gather.4.cloned.1.call-update) | async-done | bytes 3145744 | tf_op jit(solution)/shard_map/all_gather | solution.py:143
  533.6 3.8 fusion.35
  537.4 60.9 %all-gather.8.cloned.1.call-done = bf16[1024,2,768]{0,2,1:T(8,128)(2,1)} async-done(((bf16[256,2,768]{0,2,1:T(8,128)(2,1)}), bf16[1024,2,768]{0,2,1:T(8,128)(2,1)}) %all-gather.8.cloned.1.call-update) | async-done | bytes 3145744 | tf_op jit(solution)/shard_map/all_gather | solution.py:218
  598.3 3.9 fusion.29
  602.2 46.6 %all-gather.6.cloned.1.call-done = bf16[1024,2,576]{0,2,1:T(8,128)(2,1)} async-done(((bf16[256,2,576]{0,2,1:T(8,128)(2,1)}), bf16[1024,2,576]{0,2,1:T(8,128)(2,1)}) %all-gather.6.cloned.1.call-update) | async-done | bytes 2359312 | tf_op jit(solution)/shard_map/all_gather | solution.py:217
  648.8 2.5 fusion.5
  651.6 1.1 convert_element_type.204
  652.8 2.8 convolution_convert_fusion
  656.5 1.3 pad_maximum_fusion.2
  659.1 3.7 fusion.8
  663.1 2.5 reduce_sum.138
  666.2 3.0 all-reduce.9
  671.4 1.9 convert_element_type.205
  673.2 1.9 convert_element_type.214
  676.7 29.8 %reduce-scatter.17.cloned.1.call-done = bf16[256,2,384]{0,2,1:T(8,128)(2,1)} async-done(((bf16[1024,2,384]{0,2,1:T(8,128)(2,1)}), bf16[256,2,384]{0,2,1:T(8,128)(2,1)}) %reduce-scatter.17.cloned.1.call-update) | async-done | bytes 393232 | tf_op jit(solution)/shard_map/reduce_scatter | solution.py:232
  706.4 1.0 convert_element_type.201
  707.5 28.0 %reduce-scatter.9.cloned.1.call-done = bf16[256,2,192]{0,2,1:T(8,128)(2,1)} async-done(((bf16[1024,2,192]{0,2,1:T(8,128)(2,1)}), bf16[256,2,192]{0,2,1:T(8,128)(2,1)}) %reduce-scatter.9.cloned.1.call-update) | async-done | bytes 196624 | tf_op jit(solution)/shard_map/reduce_scatter | solution.py:148
  735.5 1.3 slice_reduce_fusion
  736.8 9.7 %all-reduce.7 = (f32[256,2]{0,1:T(2,128)S(1)}, f32[256,2]{0,1:T(2,128)S(1)}) all-reduce(f32[256,2]{0,1:T(2,128)S(1)} %get-tuple-element.100, f32[256,2]{0,1:T(2,128)S(1)} %get-tuple-element.101), channel_id=1, replica_groups=mesh['dp'=2,'row'=4,'col'=4] {'col'}, use_global_device_ids=true, to_apply=%region_18.19 | all-reduce | flops 1024 | bytes 8192 | tf_op jit(solution)/shard_map/psum | solution.py:244
  746.7 1.1 copy.120
  748.6 17.6 %all-reduce.6 = (f32[192]{0:T(256)}, f32[192]{0:T(256)}, f32[192]{0:T(256)}, f32[192]{0:T(256)}) all-reduce(f32[192]{0:T(256)S(1)} %get-tuple-element.74, f32[192]{0:T(256)S(1)} %get-tuple-element.73, f32[192]{0:T(256)S(1)} %get-tuple-element.75, f32[192]{0:T(256)S(1)} %get-tuple-element.72), channel_id=1, replica_groups=mesh['dp'=2,'row'=4,'col'=4] {'dp','row'}, use_global_device_ids=true, to_apply=%region_26.27 | all-reduce | flops 768 | bytes 6144 | tf_op jit(solution)/shard_map/psum | solution.py:251
  (173 shorter events, 23.9 us)
Async XLA Ops:
  7.2 62.6 %copy-start = (bf16[192,768]{1,0:T(8,128)(2,1)S(1)}, bf16[192,768]{1,0:T(8,128)(2,1)}, u32[]{:S(2)}) copy-start(bf16[192,768]{1,0:T(8,128)(2,1)} %param.25) | copy-start | bytes 884740
  7.2 163.6 %reduce-scatter.11.cloned.1.call-start = ((), (), s32[]{:S(2)}) async-start(), calls=%async_computation.9 | async-start | bytes 9830400 | tf_op jit(solution)/shard_map/reduce_scatter | solution.py:174
  25.3 2.8 copy-start.1
  25.3 1.7 copy-start.16
  26.5 1.6 copy-start.14
  32.0 1.0 copy-start.35
  32.0 1.1 copy-start.24
  32.0 1.7 copy-start.36
  32.1 1.7 copy-start.37
  32.1 2.2 copy-start.38
  32.1 328.1 %reduce-scatter.7.cloned.1.call-start = ((), (), s32[]{:S(2)}) async-start(), calls=%async_computation.6 | async-start | bytes 13762560 | tf_op jit(solution)/shard_map/reduce_scatter | solution.py:99
  33.1 33.6 %copy-start.28 = (f32[192]{0:T(256)}, f32[192]{0:T(256)S(1)}, u32[]{:S(2)}) copy-start(f32[192]{0:T(256)S(1)} %convert_element_type.172) | copy-start | bytes 2308
  33.8 36.0 %copy-start.33 = (f32[192]{0:T(256)}, f32[192]{0:T(256)S(1)}, u32[]{:S(2)}) copy-start(f32[192]{0:T(256)S(1)} %convert_element_type.173) | copy-start | bytes 2308
  47.5 22.3 %copy-start.3 = (bf16[192,2,1024]{2,0,1:T(8,128)(2,1)}, bf16[192,2,1024]{2,0,1:T(8,128)(2,1)S(1)}, u32[]{:S(2)}) copy-start(bf16[192,2,1024]{2,0,1:T(8,128)(2,1)S(1)} %all_gather.24) | copy-start | bytes 2359300
  84.4 349.4 %reduce-scatter.13.cloned.1.call-start = ((), (), s32[]{:S(2)}) async-start(), calls=%async_computation.10 | async-start | bytes 983040 | tf_op jit(solution)/shard_map/reduce_scatter | solution.py:194
  171.8 228.1 %copy-start.25 = (bf16[256,2,192]{0,2,1:T(8,128)(2,1)}, bf16[256,2,192]{0,2,1:T(8,128)(2,1)S(1)}, u32[]{:S(2)}) copy-start(bf16[256,2,192]{0,2,1:T(8,128)(2,1)S(1)} %slice.126) | copy-start | bytes 589828
  361.8 38.2 %copy-start.21 = (bf16[256,2,3,48]{0,3,2,1:T(8,128)(2,1)}, bf16[256,2,3,48]{0,3,2,1:T(8,128)(2,1)S(1)}, u32[]{:S(2)}) copy-start(bf16[256,2,3,48]{0,3,2,1:T(8,128)(2,1)S(1)} %slice.129) | copy-start | bytes 442372
  378.6 21.4 %copy-start.6 = (bf16[1024,2,192]{0,2,1:T(8,128)(2,1)}, bf16[1024,2,192]{0,2,1:T(8,128)(2,1)S(1)}, u32[]{:S(2)}) copy-start(bf16[1024,2,192]{0,2,1:T(8,128)(2,1)S(1)} %all_gather.26) | copy-start | bytes 2359300
  394.9 5.1 copy-start.19
  400.0 4.0 slice-start
  400.0 4.7 slice-start.1
  404.7 1.0 copy-start.22
  407.3 4.8 copy-start.31
  407.3 51.2 %reduce-scatter.15.cloned.1.call-start = ((), (), s32[]{:S(2)}) async-start(), calls=%async_computation.11 | async-start | bytes 983040 | tf_op jit(solution)/shard_map/reduce_scatter | solution.py:200
  412.1 121.5 %all-gather.4.cloned.1.call-start = ((), (), s32[]{:S(2)}) async-start(), calls=%async_computation.7 | async-start | bytes 3932160 | tf_op jit(solution)/shard_map/all_gather | solution.py:143
  412.1 6.2 copy-start.5
  419.5 178.9 %all-gather.8.cloned.1.call-start = ((), (), s32[]{:S(2)}) async-start(), calls=%async_computation.13 | async-start | bytes 3932160 | tf_op jit(solution)/shard_map/all_gather | solution.py:218
  420.0 228.7 %all-gather.6.cloned.1.call-start = ((), (), s32[]{:S(2)}) async-start(), calls=%async_computation.12 | async-start | bytes 2949120 | tf_op jit(solution)/shard_map/all_gather | solution.py:217
  423.1 13.5 %slice-start.2 = ((f32[256,2,3,64]{0,3,2,1:T(8,128)}), f32[256,2,3,48]{0,3,2,1:T(8,128)S(1)}, s32[]{:S(2)}) async-start(f32[256,2,3,64]{0,3,2,1:T(8,128)} %copy-done.13), calls=%async_computation.18 | async-start | bytes 589824 | tf_op jit(solution)/shard_map/transpose(jvp())/split | solution.py:32
  436.6 23.9 %copy-start.20 = (bf16[1024,2,192]{0,2,1:T(8,128)(2,1)S(1)}, bf16[1024,2,192]{0,2,1:T(8,128)(2,1)}, u32[]{:S(2)}) copy-start(bf16[1024,2,192]{0,2,1:T(8,128)(2,1)} %copy-done.19) | copy-start | bytes 2359300
  460.4 29.9 %copy-start.2 = (bf16[192,2,1024]{2,0,1:T(8,128)(2,1)S(1)}, bf16[192,2,1024]{2,0,1:T(8,128)(2,1)}, u32[]{:S(2)}) copy-start(bf16[192,2,1024]{2,0,1:T(8,128)(2,1)} %copy-done.1) | copy-start | bytes 2359300
  460.4 210.9 %all-reduce.13.cloned.1.call-start = ((), (), s32[]{:S(2)}) async-start(), calls=%async_computation.15 | async-start | bytes 1966080 | tf_op jit(solution)/shard_map/psum | solution.py:261
  491.7 106.7 %copy-start.4 = (bf16[192,2,1024]{2,0,1:T(8,128)(2,1)S(1)}, bf16[192,2,1024]{2,0,1:T(8,128)(2,1)}, u32[]{:S(2)}) copy-start(bf16[192,2,1024]{2,0,1:T(8,128)(2,1)} %copy-done.3) | copy-start | bytes 2359300
  537.4 111.4 %copy-start.29 = (f32[192]{0:T(256)S(1)}, f32[192]{0:T(256)}, u32[]{:S(2)}) copy-start(f32[192]{0:T(256)} %copy-done.28) | copy-start | bytes 2308
  537.4 111.4 %copy-start.34 = (f32[192]{0:T(256)S(1)}, f32[192]{0:T(256)}, u32[]{:S(2)}) copy-start(f32[192]{0:T(256)} %copy-done.33) | copy-start | bytes 2308
  652.7 2.9 copy-start.12
  652.7 53.7 %reduce-scatter.17.cloned.1.call-start = ((), (), s32[]{:S(2)}) async-start(), calls=%async_computation.14 | async-start | bytes 1966080 | tf_op jit(solution)/shard_map/reduce_scatter | solution.py:232
  652.8 2.9 copy-start.7
  657.8 1.3 copy-start.17
  657.8 77.7 %reduce-scatter.9.cloned.1.call-start = ((), (), s32[]{:S(2)}) async-start(), calls=%async_computation.8 | async-start | bytes 983040 | tf_op jit(solution)/shard_map/reduce_scatter | solution.py:148
  659.1 3.7 copy-start.39
  659.1 3.8 copy-start.40
  663.1 2.6 copy-start.8
  670.4 95.7 %copy-start.32 = (f32[192]{0:T(256)}, f32[192]{0:T(256)S(1)}, u32[]{:S(2)}) copy-start(f32[192]{0:T(256)S(1)} %convert_element_type.212) | copy-start | bytes 2308
  671.4 3.7 copy-start.23
  671.4 4.6 copy-start.26
  673.2 62.3 %copy-start.10 = (bf16[192,2,256]{2,1,0:T(2,128)(2,1)S(1)}, bf16[192,2,256]{2,1,0:T(2,128)(2,1)}, u32[]{:S(2)}) copy-start(bf16[192,2,256]{2,1,0:T(2,128)(2,1)} %param.15) | copy-start | bytes 589828
  676.0 70.6 %copy-start.18 = (bf16[192,2,256]{2,1,0:T(2,128)(2,1)S(1)}, bf16[192,2,256]{2,1,0:T(2,128)(2,1)}, u32[]{:S(2)}) copy-start(bf16[192,2,256]{2,1,0:T(2,128)(2,1)} %param.29) | copy-start | bytes 589828
  (6 other events, 4.8 us)
Sparse Core Ops, SparseCore 0:
  32.2 138.6 reduce-scatter.10
  173.2 186.9 reduce-scatter.6
  407.4 26.3 reduce-scatter.12
  436.0 22.5 reduce-scatter.14
  459.9 73.6 all-gather.3
  535.0 63.2 all-gather.7
  600.5 48.2 all-gather.5
  652.8 18.4 all-reduce.12
  674.6 31.7 reduce-scatter.16
  709.4 26.0 reduce-scatter.8
where the time goes:
time: 774 us
  waiting for transfers between devices  514 us (66%)
  blocking collectives  138 us (18%)
  matrix products  47.8 us (6%)
  other arithmetic  42.9 us (6%)
  local copies, waits for them, and re-layouts  15.9 us (2%)
  between operations  14.9 us (2%)
    reduce_scatter x1, waiting for transfers between devices, body(): lax.psum_scatter(jnp.concatenate([attn_part, ffn_part], axis=2), 'col', s...  188 us
    reduce_scatter x1, waiting for transfers between devices, body(): lax.psum_scatter(jnp.concatenate([att_part, up_part], axis=2), 'col', sca...  83.7 us
    all_gather x1, waiting for transfers between devices, body(): lax.all_gather(grad_hidden, 'col', axis=0, tiled=True)  60.9 us
    all_gather x1, waiting for transfers between devices, body(): lax.all_gather(grad_qkv, 'col', axis=0, tiled=True)  46.6 us
    all_gather x1, waiting for transfers between devices, body(): lax.all_gather(for_sending(up_low), 'col', axis=0, tiled=True)  41.9 us
    reduce_scatter x1, waiting for transfers between devices, body(): lax.psum_scatter(jnp.concatenate([first_part, second_part], axis=2).astyp...  29.8 us
    reduce_scatter x1, waiting for transfers between devices, body(): lax.psum_scatter((attn_part + jnp.einsum('tnf,of->tno', up_rows, w_out, p...  28 us
    all_gather x1, blocking collectives, body(): lax.all_gather(for_sending(attended), 'col', axis=0, tiled=True)  25.8 us
  transfers between devices with their start and end apart: 10, of which 10 were waited for; matrix products, arithmetic and copies ran while one was open for 9% of the time, Pallas kernels for 0%

commit v1 on v0

v1 whole, which is shorter than its diff:
```python
from functools import partial

import jax
import jax.numpy as jnp
from jax import lax
from jax.sharding import PartitionSpec as P

D = 768
HD = 64
ROT = 16
EPS = 1e-05
PAD = 16

f32 = jnp.float32
bf16 = jnp.bfloat16


def xor_peers(axis, shift):
    return [(i, i ^ shift) for i in range(lax.axis_size(axis))]


def turn_peers(shift):
    count = lax.axis_size("dp")
    return [(i, (i + shift) % count) for i in range(count)]


def send(x, axis, shift):
    return lax.ppermute(x, axis, xor_peers(axis, shift))


def gather_xor(x, axis):
    return [x] + [send(x, axis, k) for k in range(1, lax.axis_size(axis))]


def spread_peers(round_of, back=False):
    pairs = []
    cols = lax.axis_size("col")
    for dp in range(lax.axis_size("dp")):
        for col in range(cols):
            half, seq = divmod(col ^ round_of, 2)
            target = (dp // 2 * 2 + half) * cols + 2 * (dp % 2) + seq
            pairs.append((dp * cols + col, target))
    return [(b, a) for a, b in pairs] if back else pairs


def pick(flag, first, second):
    return jnp.where(flag, first, second)


def swap_by(code, parts):
    parts = [pick((code & 1) == 1, parts[j ^ 1], parts[j]) for j in range(4)]
    return [pick((code & 2) == 2, parts[j ^ 2], parts[j]) for j in range(4)]


def sum_parts(parts):
    total = parts[0].astype(f32)
    for part in parts[1:]:
        total = total + part.astype(f32)
    return total


def dot(a, b, contract):
    return lax.dot_general(a, b, (contract, ((), ())), preferred_element_type=f32)


def rotate(vector, cosine, sine):
    a, b = vector[..., : ROT // 2, :], vector[..., ROT // 2 : ROT, :]
    return jnp.concatenate(
        [a * cosine - b * sine, b * cosine + a * sine, vector[..., ROT:, :]], axis=-2
    )


def extend(columns, bias):
    high = lax.reduce_precision(bias, 8, 7)
    rows = jnp.stack([high, bias - high]).astype(bf16)
    rows = jnp.pad(rows, ((0, PAD - 2), (0, 0)))
    return jnp.concatenate([columns.astype(bf16), rows], axis=0)


def body(
    hidden_in,
    segments,
    w_qkv,
    b_qkv,
    w_dense,
    b_dense,
    ln1_gain,
    ln1_bias,
    ln2_gain,
    ln2_bias,
    w_in,
    b_in,
    w_out,
    b_out,
    cotangent,
):
    width, seqs, span = hidden_in.shape
    half_span = span // 2
    cols, rows, dps = lax.axis_size("col"), lax.axis_size("row"), lax.axis_size("dp")
    seq_len = span * rows
    heads = w_qkv.shape[1]
    hw = heads * HD
    ff = w_in.shape[1]
    scale = HD ** (-0.5)
    core = lax.axis_index("dp") % 2
    row = lax.axis_index("row")
    col = lax.axis_index("col")
    first_core = core == 0
    crossed = (core ^ (col >> 1)) == 1
    block = width + PAD

    both = jnp.stack([hidden_in, cotangent])
    pieces = [both[:, :, j % 2, (j // 2) * half_span : (j // 2 + 1) * half_span] for j in range(4)]
    sent = swap_by(col, pieces)
    got = [lax.ppermute(sent[k], ("dp", "col"), spread_peers(k)) for k in range(4)]
    got = [pick(crossed, got[k ^ 2], got[k]) for k in range(4)]
    mine = jnp.concatenate(got, axis=1)
    tokens = jnp.concatenate(gather_xor(mine, "row"), axis=2)

    counts = jnp.stack([jnp.sum(segments < 1, axis=1), jnp.sum(segments < 2, axis=1)], axis=1).astype(f32)
    counts_other = send(counts, "dp", 1)
    counts = pick((col >> 1) == core, counts, counts_other)
    counts = pick((col & 1) == 1, counts[1], counts[0]).astype(jnp.int32)

    gain1, shift1 = ln1_gain.astype(f32), ln1_bias.astype(f32)
    gain2, shift2 = ln2_gain.astype(f32), ln2_bias.astype(f32)
    wq = w_qkv.reshape(3, heads, width, HD).transpose(2, 0, 1, 3).reshape(width, 3 * hw)
    wd = w_dense.reshape(heads, width, HD).transpose(1, 0, 2).reshape(width, hw)
    wq32 = wq.astype(f32)
    bias_q = jnp.sum(wq32 * shift1[:, None], axis=0) + b_qkv.astype(f32).reshape(-1) / cols
    chunk1 = extend(
        jnp.concatenate([wq32 * gain1[:, None], wd.astype(f32)], axis=1),
        jnp.concatenate([bias_q, jnp.zeros((hw,), f32)]),
    )
    part = ff // 2
    own_in = lax.dynamic_slice_in_dim(w_in, core * part, part, 1).astype(f32)
    own_out = lax.dynamic_slice_in_dim(w_out, core * part, part, 1)
    own_b = lax.dynamic_slice_in_dim(b_in, core * part, part, 0).astype(f32)
    bias_f = jnp.sum(own_in * shift2[:, None], axis=0) + own_b / cols
    chunk2 = extend(
        jnp.concatenate([own_in * gain2[:, None], own_out.astype(f32)], axis=1),
        jnp.concatenate([bias_f, jnp.zeros((part,), f32)]),
    )
    own1 = pick(first_core, chunk1[:, : 2 * hw], chunk1[:, 2 * hw :])
    own1 = jnp.concatenate(gather_xor(own1, "col"), axis=0)
    other1 = send(own1, "dp", 1)
    w_qk = pick(first_core, own1, other1)
    w_vd = pick(first_core, other1, own1)
    own2 = jnp.concatenate(gather_xor(chunk2, "col"), axis=0)
    other2 = send(own2, "dp", 1)

    x = tokens[0].astype(f32)
    mean = jnp.mean(x, axis=0, keepdims=True)
    centre = x - mean
    rstd = lax.rsqrt(jnp.mean(centre * centre, axis=0, keepdims=True) + EPS)
    count = x.shape[1]
    normed = (centre * rstd).astype(bf16).reshape(cols, width, count)
    ones = jnp.broadcast_to((jnp.arange(PAD) < 2).astype(bf16)[None, :, None], (cols, PAD, count))
    xn = jnp.concatenate([normed, ones], axis=1).reshape(cols * block, count)
    cot = tokens[1].reshape(cols, width, count)
    cot = jnp.concatenate([cot, jnp.zeros((cols, PAD, count), bf16)], axis=1).reshape(cols * block, count)

    base = jnp.arange(half_span, dtype=jnp.int32)
    def positions(core_of):
        return jnp.concatenate([(row ^ j) * span + core_of * half_span + base for j in range(rows)])
    q_pos = positions(core)
    k_pos = jnp.concatenate([q_pos, positions(1 - core)])
    q_start = jnp.where(q_pos >= counts[1], counts[1], jnp.where(q_pos >= counts[0], counts[0], 0))
    frequency = 10000.0 ** (-jnp.arange(ROT // 2, dtype=f32) * 2.0 / ROT)
    angles = (q_pos - q_start).astype(f32)[None, :] * frequency[:, None]
    cosine, sine = jnp.cos(angles), jnp.sin(angles)

    qk = dot(w_qk, xn, ((0,), (0,))).reshape(2, heads, HD, count)
    qk = rotate(qk, cosine, sine).astype(bf16)
    vals = dot(w_vd[:, :hw], xn, ((0,), (0,))).astype(bf16).reshape(heads, HD, count)
    queries = qk[0]
    kv = jnp.stack([qk[1], vals])
    kv_other = send(kv, "dp", 1)
    keys, values = jnp.concatenate([kv, kv_other], axis=3)
    grad_att = dot(w_vd[:, hw:], cot, ((0,), (0,))).astype(bf16).reshape(heads, HD, count)

    allowed = (k_pos[:, None] <= q_pos[None, :]) & (k_pos[:, None] >= q_start[None, :])
    scores = jnp.einsum("hdk,hdq->hkq", keys, queries, preferred_element_type=f32) * scale
    scores = jnp.where(allowed[None], scores, -1000000000.0)
    top = jnp.max(scores, axis=1, keepdims=True)
    exponent = jnp.exp(scores - top)
    probs = exponent / jnp.sum(exponent, axis=1, keepdims=True)
    probs_low = probs.astype(bf16)
    attended = jnp.einsum("hdk,hkq->hdq", values, probs_low, preferred_element_type=f32).astype(bf16)
    grad_probs = jnp.einsum("hdk,hdq->hkq", values, grad_att, preferred_element_type=f32)
    grad_scores = probs * (grad_probs - jnp.sum(grad_probs * probs, axis=1, keepdims=True))
    scores_low = (grad_scores * scale).astype(bf16)
    grad_q = jnp.einsum("hdk,hkq->hdq", keys, scores_low, preferred_element_type=f32)
    grad_k = jnp.einsum("hdq,hkq->hdk", queries, scores_low, preferred_element_type=f32)
    grad_v = jnp.einsum("hdq,hkq->hdk", grad_att, probs_low, preferred_element_type=f32)
    grad_kv = jnp.stack([grad_k, grad_v])
    grad_kv = grad_kv[..., :count] + send(grad_kv[..., count:].astype(bf16), "dp", 1).astype(f32)
    attended = attended.reshape(hw, count)

    def feed(weights):
        pre = dot(weights[:, :part], xn, ((0,), (0,)))
        up, back = jax.vjp(partial(jax.nn.gelu, approximate=False), pre)
        up = up.astype(bf16)
        grad_up = dot(weights[:, part:], cot, ((0,), (0,)))
        grad_pre = back(grad_up)[0].astype(bf16)
        out = dot(weights[:, part:], up, ((1,), (0,)))
        grad_norm = dot(weights[:, :part], grad_pre, ((1,), (0,)))
        moments = jnp.concatenate(
            [dot(xn, grad_pre, ((1,), (1,))), dot(cot, up, ((1,), (1,)))], axis=1
        ).astype(bf16)
        return out, grad_norm, moments

    out_a, norm_a, mom_a = feed(own2)
    out_b, norm_b, mom_b = feed(other2)

    def scatter_moments(keep, give):
        total = sum_parts([keep, send(give, "dp", 1)]).astype(bf16).reshape(cols, block, -1)
        total = sum_parts([total[0]] + [send(total[k], "col", k) for k in range(1, cols)])
        own = total.astype(bf16)
        for k in range(2, dps, 2):
            total = total + lax.ppermute(own, "dp", turn_peers(k)).astype(f32)
        own = total.astype(bf16)
        other = send(own, "dp", 1)
        return pick(first_core, own, other).astype(f32), pick(first_core, other, own).astype(f32)

    m2_low, m2_high = scatter_moments(mom_a, mom_b)
    m_in = jnp.concatenate([m2_low[:, :part], m2_high[:, :part]], axis=1)
    m_out = jnp.concatenate([m2_low[:, part:], m2_high[:, part:]], axis=1)

    def to_rows(partial_sum):
        low = partial_sum.astype(bf16).reshape(cols, block, count)[:, :width]
        low = [low[..., j * half_span : (j + 1) * half_span] for j in range(rows)]
        return sum_parts([low[0]] + [send(low[j], "row", j) for j in range(1, rows)])

    def to_columns(x):
        x = x.astype(bf16)
        parts = [pick(crossed, x[k ^ 2], x[k]) for k in range(4)]
        parts = [lax.ppermute(parts[k], ("dp", "col"), spread_peers(k, True)) for k in range(4)]
        parts = swap_by(col, parts)
        return jnp.stack(
            [jnp.concatenate([parts[s], parts[2 + s]], axis=1) for s in range(2)], axis=1
        ).astype(f32)

    out_sum = out_a + out_b + dot(w_vd[:, hw:], attended, ((1,), (0,)))
    branch = to_columns(to_rows(out_sum))
    bias_out = b_dense.astype(f32) + b_out.astype(f32)
    layer_out = (hidden_in.astype(f32) + branch + bias_out[:, None, None]).astype(bf16)

    grad_qk = jnp.stack([grad_q, grad_kv[0]])
    grad_qk = rotate(grad_qk, cosine, -sine).astype(bf16).reshape(2 * hw, count)
    grad_val = grad_kv[1].astype(bf16).reshape(hw, count)
    norm_sum = (
        norm_a
        + norm_b
        + dot(w_qk, grad_qk, ((1,), (0,)))
        + dot(w_vd[:, :hw], grad_val, ((1,), (0,)))
    )
    mom_qk = dot(xn, grad_qk, ((1,), (1,))).astype(bf16)
    mom_vd = jnp.concatenate(
        [dot(xn, grad_val, ((1,), (1,))), dot(cot, attended, ((1,), (1,)))], axis=1
    ).astype(bf16)
    m_qk, m_vd = scatter_moments(
        pick(first_core, mom_qk, mom_vd), pick(first_core, mom_vd, mom_qk)
    )
    m_q = jnp.concatenate([m_qk, m_vd[:, :hw]], axis=1)
    m_d = m_vd[:width, hw:]

    grad_normed = to_rows(norm_sum)
    x_row = mine[0].astype(f32).reshape(cols, width, half_span)
    mean_row = jnp.mean(x_row, axis=(0, 1), keepdims=True)
    x_row = x_row - mean_row
    rstd_row = lax.rsqrt(jnp.mean(x_row * x_row, axis=(0, 1), keepdims=True) + EPS)
    n_row = x_row * rstd_row
    grad_x = rstd_row * (
        grad_normed
        - jnp.mean(grad_normed, axis=(0, 1), keepdims=True)
        - n_row * jnp.mean(grad_normed * n_row, axis=(0, 1), keepdims=True)
    )
    grad_in = cotangent.astype(f32) + to_columns(grad_x)

    sum_q, sum_f = m_q[width], m_in[width]
    m_q, m_in, m_out = m_q[:width], m_in[:width], m_out[:width]
    d_wq = m_q * gain1[:, None] + shift1[:, None] * sum_q
    d_w_in = m_in * gain2[:, None] + shift2[:, None] * sum_f
    win32 = w_in.astype(f32)
    small = jnp.stack(
        [
            jnp.sum(wq32 * m_q, axis=1),
            jnp.sum(wq32 * sum_q, axis=1),
            jnp.sum(win32 * m_in, axis=1),
            jnp.sum(win32 * sum_f, axis=1),
            jnp.sum(cotangent.astype(f32), axis=(1, 2)),
        ]
    )
    small = sum_parts(gather_xor(small, "row"))
    d_shared = small[4]
    for k in range(1, dps):
        d_shared = d_shared + lax.ppermute(small[4], "dp", turn_peers(k))
    d_w_qkv = d_wq.reshape(width, 3, heads, HD).transpose(1, 2, 0, 3).reshape(w_qkv.shape)
    d_w_dense = m_d.reshape(width, heads, HD).transpose(1, 0, 2).reshape(w_dense.shape)
    return (
        layer_out,
        grad_in,
        d_w_qkv,
        sum_q.reshape(3, hw),
        d_w_dense,
        d_shared,
        small[0],
        small[1],
        small[2],
        small[3],
        d_w_in,
        sum_f,
        m_out,
        d_shared,
    )


def solution(mesh):
    placed = (
        P("col", "dp", "row"),
        P("dp", None),
        P(None, "row", "col"),
        P(None, "row"),
        P("row", "col"),
        P("col"),
        P("col"),
        P("col"),
        P("col"),
        P("col"),
        P("col", "row"),
        P("row"),
        P("col", "row"),
        P("col"),
        P("col", "dp", "row"),
    )
    return jax.shard_map(
        body,
        mesh=mesh,
        in_specs=placed,
        out_specs=(
            P("col", "dp", "row"),
            P("col", "dp", "row"),
            P(None, "row", "col"),
            P(None, "row"),
            P("row", "col"),
            P("col"),
            P("col"),
            P("col"),
            P("col"),
            P("col"),
            P("col", "row"),
            P("row"),
            P("col", "row"),
            P("col"),
        ),
        check_vma=False,
    )
```

time: 774 us -> 261 us (0.34)
  waiting for transfers between devices: 514 us -> 61.5 us
  blocking collectives: 138 us -> 0 us
  starting transfers between devices: 0.41 us -> 63 us
  matrix products: 47.8 us -> 69 us
  local copies, waits for them, and re-layouts: 15.9 us -> 30.5 us
  other arithmetic: 42.9 us -> 30.3 us
  between operations: 14.9 us -> 2.54 us
    reduce_scatter x6 -> x0, waiting for transfers between devices: 362 us -> none  [the longest x1 188 us: body(): lax.psum_scatter(jnp.concatenate([attn_part, ffn_part], axis=2), 'col', s...]
    all_gather x3 -> x0, waiting for transfers between devices: 149 us -> none  [the longest x1 60.9 us: body(): lax.all_gather(grad_hidden, 'col', axis=0, tiled=True)]
    all_gather x5 -> x0, blocking collectives: 89.1 us -> none  [the longest x1 25.8 us: body(): lax.all_gather(for_sending(attended), 'col', axis=0, tiled=True)]
    ppermute x0 -> x46, starting transfers between devices: none -> 63 us  [the longest x33 29.3 us: send(): return lax.ppermute(x, axis, xor_peers(axis, shift))]
    ppermute x0 -> x46, waiting for transfers between devices: none -> 61.5 us  [the longest x33 56.5 us: send(): return lax.ppermute(x, axis, xor_peers(axis, shift))]
    psum x4 -> x0, blocking collectives: 49.2 us -> none  [the longest x1 18.9 us: body(): lax.psum((jnp.sum(hidden_cols, axis=2), jnp.sum(hidden_cols * hidden_cols...]
    dot_general x17 -> x26, matrix products: 42.7 us -> 62.6 us  [the longest x21 30.7 us: dot(): lax.dot_general(a, b, (contract, ((), ())), preferred_element_type=f32)]
    concatenate x4 -> x12, other arithmetic: 16.1 us -> 7.26 us  [the longest x1 1.41 us: body(): tokens = jnp.concatenate(gather_xor(mine, 'row'), axis=2)]
  transfers between devices with their start and end apart: 10 -> 46, of which waited for: 10 -> 12; matrix products, arithmetic and copies ran while one was open for 9% -> 45% of each run, Pallas kernels for 0% -> 0%
where the time goes in v1:
time: 261 us; the launch traced here: 257 us
  matrix products  69 us (26%)
  starting transfers between devices  63 us (24%)
  waiting for transfers between devices  61.5 us (24%)
  local copies, waits for them, and re-layouts  30.5 us (12%)
  other arithmetic  30.3 us (12%)
    ppermute x33, waiting for transfers between devices, send(): return lax.ppermute(x, axis, xor_peers(axis, shift))  56.5 us
    dot_general x21, matrix products, dot(): lax.dot_general(a, b, (contract, ((), ())), preferred_element_type=f32)  30.7 us
    ppermute x33, starting transfers between devices, send(): return lax.ppermute(x, axis, xor_peers(axis, shift))  29.3 us
    ppermute x8, starting transfers between devices, to_columns(): lax.ppermute(parts[k], ('dp', 'col'), spread_peers(k, True))  18.3 us
    ppermute x4, starting transfers between devices, body(): lax.ppermute(sent[k], ('dp', 'col'), spread_peers(k))  14.1 us
    unnamed x147, local copies, waits for them, and re-layouts  12.7 us
    dot_general x1, matrix products, body(): jnp.einsum('hdq,hkq->hdk', queries, scores_low, preferred_element_type=f32)  11.5 us
    dot_general x1, matrix products, body(): jnp.einsum('hdk,hkq->hdq', keys, scores_low, preferred_element_type=f32)  11.3 us
  transfers between devices with their start and end apart: 46, of which 12 were waited for; matrix products, arithmetic and copies ran while one was open for 45% of the time, Pallas kernels for 0%

profile of v1, /device:TPU:1, one launch (start us, length us, event | category | flops | bytes accessed | tf_op | source)
XLA Modules:
  0.0 256.9 jit_solution(7526635341228100916)
XLA Ops:
  4.9 4.2 %collective-permute-start.13 = (bf16[208,384]{0,1:T(8,128)(2,1)S(1)}, bf16[208,384]{0,1:T(8,128)(2,1)S(1)}, u32[]{:S(2)}, u32[]{:S(2)}) collective-permute-start(bf16[208,384]{0,1:T(8,128)(2,1)S(1)} %slice_select_fusion), channel_id=1, source_target_pairs={{0,3},{1,2},{2,1},{3,0},{4,7},{5,6},{6,5},{7,4},{8,11},{9,10},{10,... | collective-permute-start | bytes 479240 | tf_op jit(solution)/shard_map/ppermute | solution.py:28
  10.3 3.2 %collective-permute-start.5 = (bf16[2,192,128]{2,1,0:T(8,128)(2,1)S(1)}, bf16[2,192,128]{2,1,0:T(8,128)(2,1)S(1)}, u32[]{:S(2)}, u32[]{:S(2)}) collective-permute-start(bf16[2,192,128]{2,1,0:T(8,128)(2,1)S(1)} %get-tuple-element.132), channel_id=1, source_target_pairs={{0,17},{1,16},{2,1},{3,0},{16,19},{17,18},{18,3},{19,2},{4,21},{5,... | collective-permute-start | bytes 294920 | tf_op jit(solution)/shard_map/ppermute | solution.py:115
  19.4 1.5 collective-permute-start.6
  24.8 5.6 %collective-permute-start.3 = (bf16[2,192,128]{2,1,0:T(8,128)(2,1)}, bf16[2,192,128]{2,1,0:T(8,128)(2,1)S(1)}, u32[]{:S(2)}, u32[]{:S(2)}) collective-permute-start(bf16[2,192,128]{2,1,0:T(8,128)(2,1)} %get-tuple-element.97), channel_id=1, source_target_pairs={{0,16},{1,17},{2,0},{3,1},{16,18},{17,19},{18,2},{19,3},{4,20},{5,... | collective-permute-start | bytes 294920 | tf_op jit(solution)/shard_map/ppermute | solution.py:115
  30.4 3.8 %collective-permute-start.4 = (bf16[2,192,128]{2,1,0:T(8,128)(2,1)S(1)}, bf16[2,192,128]{2,1,0:T(8,128)(2,1)S(1)}, u32[]{:S(2)}, u32[]{:S(2)}) collective-permute-start(bf16[2,192,128]{2,1,0:T(8,128)(2,1)S(1)} %get-tuple-element.131), channel_id=1, source_target_pairs={{0,0},{1,1},{2,16},{3,17},{16,2},{17,3},{18,18},{19,19},{4,4},{5,5... | collective-permute-start | bytes 294920 | tf_op jit(solution)/shard_map/ppermute | solution.py:115
  35.0 3.3 %collective-permute-done.4 = bf16[2,192,128]{2,1,0:T(8,128)(2,1)S(1)} collective-permute-done((bf16[2,192,128]{2,1,0:T(8,128)(2,1)S(1)}, bf16[2,192,128]{2,1,0:T(8,128)(2,1)S(1)}, u32[]{:S(2)}, u32[]{:S(2)}) %collective-permute-start.4) | collective-permute-done | bytes 98336 | tf_op jit(solution)/shard_map/ppermute | solution.py:115
  41.2 2.2 collective-permute-start.9
  43.6 5.0 %collective-permute-done = bf16[208,768]{1,0:T(8,128)(2,1)S(1)} collective-permute-done((bf16[208,768]{1,0:T(8,128)(2,1)}, bf16[208,768]{1,0:T(8,128)(2,1)S(1)}, u32[]{:S(2)}, u32[]{:S(2)}) %collective-permute-start) | collective-permute-done | bytes 319520 | tf_op jit(solution)/shard_map/ppermute | solution.py:28
  53.0 1.7 constant_dynamic-update-slice_fusion.2
  54.7 7.9 %collective-permute-done.1 = bf16[208,768]{1,0:T(8,128)(2,1)} collective-permute-done((bf16[208,768]{1,0:T(8,128)(2,1)}, bf16[208,768]{1,0:T(8,128)(2,1)}, u32[]{:S(2)}, u32[]{:S(2)}) %collective-permute-start.1) | collective-permute-done | bytes 319520 | tf_op jit(solution)/shard_map/ppermute | solution.py:28
  62.5 1.7 constant_dynamic-update-slice_fusion.1
  64.2 1.7 constant_dynamic-update-slice_fusion
  69.2 3.2 %multiply_convert_fusion.3 = (bf16[384,512]{1,0:T(8,128)(2,1)S(1)}, f32[384,512]{1,0:T(8,128)S(1)}, f32[384,512]{1,0:T(8,128)S(1)}) fusion(bf16[832,512]{1,0:T(8,128)(2,1)S(1)} %bitcast.161, bf16[832,768]{1,0:T(8,128)(2,1)} %constant_dynamic-update-slice_fusion), kind=kOutput, calls=%fused_computation.77 | convolution fusion | flops 339935232 | bytes 3457024 | tf_op jit(solution)/shard_map/dot_general | solution.py:63
  72.5 2.9 %fusion.75 = f32[832,512]{1,0:T(8,128)} fusion(bf16[384,512]{1,0:T(8,128)(2,1)S(1)} %get-tuple-element.95, bf16[832,768]{1,0:T(8,128)(2,1)} %constant_dynamic-update-slice_fusion), kind=kOutput, calls=%fused_computation.131 | convolution fusion | flops 327155712 | bytes 2736128 | tf_op jit(solution)/shard_map/dot_general | solution.py:63
  76.9 1.9 add_convert_fusion.5
  79.5 2.9 %fusion.69 = f32[832,512]{1,0:T(8,128)} fusion(bf16[384,512]{1,0:T(8,128)(2,1)S(1)} %add_convert_fusion.5, bf16[832,768]{1,0:T(8,128)(2,1)} %constant_dynamic-update-slice_fusion), kind=kOutput, calls=%fused_computation.125 | convolution fusion | flops 327155712 | bytes 2736128 | tf_op jit(solution)/shard_map/dot_general | solution.py:63
  82.4 2.2 copy.97
  84.6 1.8 broadcast_select_fusion.1
  91.3 3.6 %fusion.80 = f32[3,1024,512]{2,1,0:T(8,128)} fusion(bf16[3,64,512]{2,1,0:T(8,128)(2,1)S(1)} %bitcast.200, bf16[2,3,64,1024]{3,2,1,0:T(8,128)(2,1)S(1)} %pad_maximum_fusion.4), kind=kOutput, calls=%fused_computation.158 | convolution fusion | flops 201326592 | bytes 6881280 | tf_op jit(solution)/shard_map/hdk,hdq->hkq/dot_general | solution.py:190
  95.0 6.4 %fusion.129 = (f32[3,512]{1,0:T(4,128)S(1)}, f32[3,1024,512]{2,1,0:T(8,128)}) fusion(pred[1024,512]{1,0:T(8,128)(4,1)} %compare_and_fusion, bf16[2,3,64,1024]{3,2,1,0:T(8,128)(2,1)} %copy-done.13, bf16[2,3,64,512]{3,2,1,0:T(8,128)(2,1)} %copy-done.26), kind=kOutput, calls=%fused_computation.303 | convolution fusion | flops 207619072 | bytes 7411712 | tf_op jit(solution)/shard_map/sub | solution.py:186
  101.4 4.9 %fusion.24 = f32[1,3,64,1024]{3,2,1,0:T(8,128)} fusion(bf16[3,64,512]{2,1,0:T(8,128)(2,1)S(1)} %bitcast.201, f32[3,1024,512]{2,1,0:T(8,128)} %get-tuple-element.180, f32[3,512]{1,0:T(4,128)S(1)} %get-tuple-element.179), kind=kOutput, calls=%fused_computation.36 | convolution fusion | flops 204472320 | bytes 7280640 | tf_op jit(solution)/shard_map/hdq,hkq->hdk/dot_general | solution.py:195
  107.0 11.5 %fusion.21 = f32[1,3,64,1024]{3,2,1,0:T(8,128)} fusion(f32[3,1024,512]{2,1,0:T(8,128)} %fusion.80, bf16[2,3,64,512]{3,2,1,0:T(8,128)(2,1)} %copy-done.26, f32[3,1024,512]{2,1,0:T(8,128)} %get-tuple-element.180, f32[3,512]{1,0:T(4,128)S(1)} %get-tuple-element.179), kind=kOutput, calls=%fused_computation.35 | convolution fusion | flops 212339200 | bytes 26165248 | tf_op jit(solution)/shard_map/hdq,hkq->hdk/dot_general | solution.py:194
  118.4 1.9 fusion.39
  120.8 11.3 %fusion.27 = f32[1,3,64,512]{3,2,1,0:T(8,128)} fusion(f32[3,1024,512]{2,1,0:T(8,128)} %fusion.80, bf16[2,3,64,1024]{3,2,1,0:T(8,128)(2,1)} %copy-done.13, f32[3,1024,512]{2,1,0:T(8,128)} %get-tuple-element.180, f32[3,512]{1,0:T(4,128)S(1)} %get-tuple-element.179), kind=kOutput, calls=%fused_computation.40 | convolution fusion | flops 212339200 | bytes 25968640 | tf_op jit(solution)/shard_map/hdk,hkq->hdq/dot_general | solution.py:193
  135.2 1.7 broadcast_select_fusion
  136.9 2.2 copy.101
  139.1 1.8 fusion.131
  141.0 3.2 %multiply_convert_fusion.2 = (bf16[384,512]{1,0:T(8,128)(2,1)S(1)}, f32[384,512]{1,0:T(8,128)S(1)}, f32[384,512]{1,0:T(8,128)S(1)}) fusion(bf16[832,512]{1,0:T(8,128)(2,1)S(1)} %bitcast.167, bf16[832,768]{1,0:T(8,128)(2,1)} %collective-permute-done.10), kind=kOutput, calls=%fused_computation.64 | convolution fusion | flops 339935232 | bytes 3457024 | tf_op jit(solution)/shard_map/dot_general | solution.py:63
  144.2 1.9 add_convert_fusion.4
  146.1 1.8 fusion.59
  148.5 2.2 collective-permute-start.27
  151.9 2.1 fusion.65
  154.6 2.2 collective-permute-start.19
  157.8 3.6 %collective-permute-done.26 = bf16[4,192,128]{2,1,0:T(8,128)(2,1)S(1)} collective-permute-done((bf16[4,192,128]{2,1,0:T(8,128)(2,1)S(1)}, bf16[4,192,128]{2,1,0:T(8,128)(2,1)S(1)}, u32[]{:S(2)}, u32[]{:S(2)}) %collective-permute-start.26) | collective-permute-done | bytes 196640 | tf_op jit(solution)/shard_map/ppermute | solution.py:28
  163.0 4.5 %collective-permute-start.28 = (bf16[192,128]{1,0:T(8,128)(2,1)S(1)}, bf16[192,128]{1,0:T(8,128)(2,1)S(1)}, u32[]{:S(2)}, u32[]{:S(2)}) collective-permute-start(bf16[192,128]{1,0:T(8,128)(2,1)S(1)} %get-tuple-element.143), channel_id=1, source_target_pairs={{17,0},{16,1},{1,2},{0,3},{19,16},{18,17},{3,18},{2,19},{21,4},{20... | collective-permute-start | bytes 147464 | tf_op jit(solution)/shard_map/ppermute | solution.py:238
  168.9 3.2 %collective-permute-start.30 = (bf16[192,128]{1,0:T(8,128)(2,1)S(1)}, bf16[192,128]{1,0:T(8,128)(2,1)S(1)}, u32[]{:S(2)}, u32[]{:S(2)}) collective-permute-start(bf16[192,128]{1,0:T(8,128)(2,1)S(1)} %get-tuple-element.142), channel_id=1, source_target_pairs={{1,0},{0,1},{17,2},{16,3},{3,16},{2,17},{19,18},{18,19},{5,4},{4,5... | collective-permute-start | bytes 147464 | tf_op jit(solution)/shard_map/ppermute | solution.py:238
  172.0 4.3 %collective-permute-start.31 = (bf16[192,128]{1,0:T(8,128)(2,1)S(1)}, bf16[192,128]{1,0:T(8,128)(2,1)S(1)}, u32[]{:S(2)}, u32[]{:S(2)}) collective-permute-start(bf16[192,128]{1,0:T(8,128)(2,1)S(1)} %get-tuple-element.145), channel_id=1, source_target_pairs={{0,0},{1,1},{16,2},{17,3},{2,16},{3,17},{18,18},{19,19},{4,4},{5,5... | collective-permute-start | bytes 147464 | tf_op jit(solution)/shard_map/ppermute | solution.py:238
  176.6 1.8 collective-permute-start.20
  178.4 1.9 collective-permute-start.23
  180.3 2.6 %collective-permute-start.22 = (bf16[192,128]{1,0:T(8,128)(2,1)S(1)}, bf16[192,128]{1,0:T(8,128)(2,1)S(1)}, u32[]{:S(2)}, u32[]{:S(2)}) collective-permute-start(bf16[192,128]{1,0:T(8,128)(2,1)S(1)} %get-tuple-element.150), channel_id=1, source_target_pairs={{1,0},{0,1},{17,2},{16,3},{3,16},{2,17},{19,18},{18,19},{5,4},{4,5... | collective-permute-start | bytes 147464 | tf_op jit(solution)/shard_map/ppermute | solution.py:238
  188.6 1.9 collective-permute-start.34
  190.5 1.6 collective-permute-start.33
  192.9 3.8 %collective-permute-done.35 = bf16[208,384]{0,1:T(8,128)(2,1)S(1)} collective-permute-done((bf16[208,384]{0,1:T(8,128)(2,1)S(1)}, bf16[208,384]{0,1:T(8,128)(2,1)S(1)}, u32[]{:S(2)}, u32[]{:S(2)}) %collective-permute-start.35) | collective-permute-done | bytes 159776 | tf_op jit(solution)/shard_map/ppermute | solution.py:28
  196.7 11.6 %collective-permute-done.34 = bf16[208,384]{0,1:T(8,128)(2,1)S(1)} collective-permute-done((bf16[208,384]{0,1:T(8,128)(2,1)S(1)}, bf16[208,384]{0,1:T(8,128)(2,1)S(1)}, u32[]{:S(2)}, u32[]{:S(2)}) %collective-permute-start.34) | collective-permute-done | bytes 159776 | tf_op jit(solution)/shard_map/ppermute | solution.py:28
  209.2 1.7 add_convert_fusion
  212.8 2.6 %collective-permute-start.38 = (bf16[208,768]{1,0:T(8,128)(2,1)}, bf16[208,768]{1,0:T(8,128)(2,1)}, u32[]{:S(2)}, u32[]{:S(2)}) collective-permute-start(bf16[208,768]{1,0:T(8,128)(2,1)} %get-tuple-element.106), channel_id=1, source_target_pairs={{0,1},{1,0},{2,3},{3,2},{4,5},{5,4},{6,7},{7,6},{8,9},{9,8},{10,11... | collective-permute-start | bytes 958472 | tf_op jit(solution)/shard_map/ppermute | solution.py:28
  217.3 5.9 %collective-permute-done.40 = bf16[208,768]{1,0:T(8,128)(2,1)} collective-permute-done((bf16[208,768]{1,0:T(8,128)(2,1)}, bf16[208,768]{1,0:T(8,128)(2,1)}, u32[]{:S(2)}, u32[]{:S(2)}) %collective-permute-start.40) | collective-permute-done | bytes 319520 | tf_op jit(solution)/shard_map/ppermute | solution.py:28
  223.2 16.5 %collective-permute-done.39 = bf16[208,768]{1,0:T(8,128)(2,1)} collective-permute-done((bf16[208,768]{1,0:T(8,128)(2,1)}, bf16[208,768]{1,0:T(8,128)(2,1)}, u32[]{:S(2)}, u32[]{:S(2)}) %collective-permute-start.39) | collective-permute-done | bytes 319520 | tf_op jit(solution)/shard_map/ppermute | solution.py:28
  (356 shorter events, 71.4 us)
Async XLA Ops:
  4.9 45.6 %copy-start.11 = (bf16[208,384]{0,1:T(8,128)(2,1)}, bf16[208,384]{0,1:T(8,128)(2,1)S(1)}, u32[]{:S(2)}) copy-start(bf16[208,384]{0,1:T(8,128)(2,1)S(1)} %slice_select_fusion) | copy-start | bytes 479236
  4.9 35.0 %collective-permute-start.13 = (bf16[208,384]{0,1:T(8,128)(2,1)S(1)}, bf16[208,384]{0,1:T(8,128)(2,1)S(1)}, u32[]{:S(2)}, u32[]{:S(2)}) collective-permute-start(bf16[208,384]{0,1:T(8,128)(2,1)S(1)} %slice_select_fusion), channel_id=1, source_target_pairs={{0,3},{1,2},{2,1},{3,0},{4,7},{5,6},{6,5},{7,4},{8,11},{9,10},{10,... | collective-permute-start | bytes 479240 | tf_op jit(solution)/shard_map/ppermute | solution.py:28
  9.1 32.1 %collective-permute-start.12 = (bf16[208,384]{0,1:T(8,128)(2,1)S(1)}, bf16[208,384]{0,1:T(8,128)(2,1)S(1)}, u32[]{:S(2)}, u32[]{:S(2)}) collective-permute-start(bf16[208,384]{0,1:T(8,128)(2,1)S(1)} %slice_select_fusion), channel_id=1, source_target_pairs={{0,2},{1,3},{2,0},{3,1},{4,6},{5,7},{6,4},{7,5},{8,10},{9,11},{10,... | collective-permute-start | bytes 479240 | tf_op jit(solution)/shard_map/ppermute | solution.py:28
  9.1 34.3 %collective-permute-start.11 = (bf16[208,384]{0,1:T(8,128)(2,1)S(1)}, bf16[208,384]{0,1:T(8,128)(2,1)}, u32[]{:S(2)}, u32[]{:S(2)}) collective-permute-start(bf16[208,384]{0,1:T(8,128)(2,1)S(1)} %slice_select_fusion), channel_id=1, source_target_pairs={{0,1},{1,0},{2,3},{3,2},{4,5},{5,4},{6,7},{7,6},{8,9},{9,8},{10,11... | collective-permute-start | bytes 479240 | tf_op jit(solution)/shard_map/ppermute | solution.py:28
  10.3 14.5 %collective-permute-start.5 = (bf16[2,192,128]{2,1,0:T(8,128)(2,1)S(1)}, bf16[2,192,128]{2,1,0:T(8,128)(2,1)S(1)}, u32[]{:S(2)}, u32[]{:S(2)}) collective-permute-start(bf16[2,192,128]{2,1,0:T(8,128)(2,1)S(1)} %get-tuple-element.132), channel_id=1, source_target_pairs={{0,17},{1,16},{2,1},{3,0},{16,19},{17,18},{18,3},{19,2},{4,21},{5,... | collective-permute-start | bytes 294920 | tf_op jit(solution)/shard_map/ppermute | solution.py:115
  13.8 5.6 %collective-permute-start.15 = (f32[2,2]{0,1:T(2,128)S(1)}, f32[2,2]{0,1:T(2,128)S(1)}, u32[]{:S(2)}, u32[]{:S(2)}) collective-permute-start(f32[2,2]{0,1:T(2,128)S(1)} %add_convert_fusion.11), channel_id=1, source_target_pairs={{0,16},{16,0},{1,17},{17,1},{2,18},{18,2},{3,19},{19,3},{4,20},{20... | collective-permute-start | bytes 56 | tf_op jit(solution)/shard_map/ppermute | solution.py:28
  19.4 11.1 %collective-permute-start.6 = (bf16[2,192,128]{2,1,0:T(8,128)(2,1)S(1)}, bf16[2,192,128]{2,1,0:T(8,128)(2,1)S(1)}, u32[]{:S(2)}, u32[]{:S(2)}) collective-permute-start(bf16[2,192,128]{2,1,0:T(8,128)(2,1)S(1)} %get-tuple-element.133), channel_id=1, source_target_pairs={{0,1},{1,0},{2,17},{3,16},{16,3},{17,2},{18,19},{19,18},{4,5},{5,4... | collective-permute-start | bytes 294920 | tf_op jit(solution)/shard_map/ppermute | solution.py:115
  24.8 9.4 %collective-permute-start.3 = (bf16[2,192,128]{2,1,0:T(8,128)(2,1)}, bf16[2,192,128]{2,1,0:T(8,128)(2,1)S(1)}, u32[]{:S(2)}, u32[]{:S(2)}) collective-permute-start(bf16[2,192,128]{2,1,0:T(8,128)(2,1)} %get-tuple-element.97), channel_id=1, source_target_pairs={{0,16},{1,17},{2,0},{3,1},{16,18},{17,19},{18,2},{19,3},{4,20},{5,... | collective-permute-start | bytes 294920 | tf_op jit(solution)/shard_map/ppermute | solution.py:115
  30.4 7.9 %collective-permute-start.4 = (bf16[2,192,128]{2,1,0:T(8,128)(2,1)S(1)}, bf16[2,192,128]{2,1,0:T(8,128)(2,1)S(1)}, u32[]{:S(2)}, u32[]{:S(2)}) collective-permute-start(bf16[2,192,128]{2,1,0:T(8,128)(2,1)S(1)} %get-tuple-element.131), channel_id=1, source_target_pairs={{0,0},{1,1},{2,16},{3,17},{16,2},{17,3},{18,18},{19,19},{4,4},{5,5... | collective-permute-start | bytes 294920 | tf_op jit(solution)/shard_map/ppermute | solution.py:115
  34.3 14.3 %collective-permute-start = (bf16[208,768]{1,0:T(8,128)(2,1)}, bf16[208,768]{1,0:T(8,128)(2,1)S(1)}, u32[]{:S(2)}, u32[]{:S(2)}) collective-permute-start(bf16[208,768]{1,0:T(8,128)(2,1)} %pad_maximum_fusion.11), channel_id=1, source_target_pairs={{0,1},{1,0},{2,3},{3,2},{4,5},{5,4},{6,7},{7,6},{8,9},{9,8},{10,11... | collective-permute-start | bytes 958472 | tf_op jit(solution)/shard_map/ppermute | solution.py:28
  38.3 24.2 %collective-permute-start.1 = (bf16[208,768]{1,0:T(8,128)(2,1)}, bf16[208,768]{1,0:T(8,128)(2,1)}, u32[]{:S(2)}, u32[]{:S(2)}) collective-permute-start(bf16[208,768]{1,0:T(8,128)(2,1)} %pad_maximum_fusion.11), channel_id=1, source_target_pairs={{0,2},{1,3},{2,0},{3,1},{4,6},{5,7},{6,4},{7,5},{8,10},{9,11},{10,... | collective-permute-start | bytes 958472 | tf_op jit(solution)/shard_map/ppermute | solution.py:28
  39.9 24.3 %collective-permute-start.2 = (bf16[208,768]{1,0:T(8,128)(2,1)}, bf16[208,768]{1,0:T(8,128)(2,1)}, u32[]{:S(2)}, u32[]{:S(2)}) collective-permute-start(bf16[208,768]{1,0:T(8,128)(2,1)} %pad_maximum_fusion.11), channel_id=1, source_target_pairs={{0,3},{1,2},{2,1},{3,0},{4,7},{5,6},{6,5},{7,4},{8,11},{9,10},{10,... | collective-permute-start | bytes 958472 | tf_op jit(solution)/shard_map/ppermute | solution.py:28
  41.2 25.3 %collective-permute-start.9 = (bf16[2,768,128]{2,1,0:T(8,128)(2,1)S(1)}, bf16[2,768,128]{2,1,0:T(8,128)(2,1)}, u32[]{:S(2)}, u32[]{:S(2)}) collective-permute-start(bf16[2,768,128]{2,1,0:T(8,128)(2,1)S(1)} %pad_maximum_fusion.8), channel_id=1, source_target_pairs={{0,12},{4,8},{8,4},{12,0},{1,13},{5,9},{9,5},{13,1},{2,14},{6,10},... | collective-permute-start | bytes 1179656 | tf_op jit(solution)/shard_map/ppermute | solution.py:28
  43.4 23.1 %collective-permute-start.8 = (bf16[2,768,128]{2,1,0:T(8,128)(2,1)S(1)}, bf16[2,768,128]{2,1,0:T(8,128)(2,1)}, u32[]{:S(2)}, u32[]{:S(2)}) collective-permute-start(bf16[2,768,128]{2,1,0:T(8,128)(2,1)S(1)} %pad_maximum_fusion.8), channel_id=1, source_target_pairs={{0,8},{4,12},{8,0},{12,4},{1,9},{5,13},{9,1},{13,5},{2,10},{6,14},... | collective-permute-start | bytes 1179656 | tf_op jit(solution)/shard_map/ppermute | solution.py:28
  49.3 17.2 %collective-permute-start.7 = (bf16[2,768,128]{2,1,0:T(8,128)(2,1)S(1)}, bf16[2,768,128]{2,1,0:T(8,128)(2,1)}, u32[]{:S(2)}, u32[]{:S(2)}) collective-permute-start(bf16[2,768,128]{2,1,0:T(8,128)(2,1)S(1)} %pad_maximum_fusion.8), channel_id=1, source_target_pairs={{0,4},{4,0},{8,12},{12,8},{1,5},{5,1},{9,13},{13,9},{2,6},{6,2},{1... | collective-permute-start | bytes 1179656 | tf_op jit(solution)/shard_map/ppermute | solution.py:28
  62.5 19.9 %collective-permute-start.14 = (bf16[832,384]{1,0:T(8,128)(2,1)}, bf16[832,384]{1,0:T(8,128)(2,1)}, u32[]{:S(2)}, u32[]{:S(2)}) collective-permute-start(bf16[832,384]{1,0:T(8,128)(2,1)} %copy.96), channel_id=1, source_target_pairs={{0,16},{16,0},{1,17},{17,1},{2,18},{18,2},{3,19},{19,3},{4,20},{20... | collective-permute-start | bytes 1916936 | tf_op jit(solution)/shard_map/ppermute | solution.py:28
  66.0 75.0 %collective-permute-start.10 = (bf16[832,768]{1,0:T(8,128)(2,1)}, bf16[832,768]{1,0:T(8,128)(2,1)}, u32[]{:S(2)}, u32[]{:S(2)}) collective-permute-start(bf16[832,768]{1,0:T(8,128)(2,1)} %constant_dynamic-update-slice_fusion), channel_id=1, source_target_pairs={{0,16},{16,0},{1,17},{17,1},{2,18},{18,2},{3,19},{19,3},{4,20},{20... | collective-permute-start | bytes 3833864 | tf_op jit(solution)/shard_map/ppermute | solution.py:28
  88.4 1.9 collective-permute-start.16
  120.4 12.3 %collective-permute-start.24 = (bf16[2,3,64,512]{3,2,1,0:T(8,128)(2,1)}, bf16[2,3,64,512]{3,2,1,0:T(8,128)(2,1)}, u32[]{:S(2)}, u32[]{:S(2)}) collective-permute-start(bf16[2,3,64,512]{3,2,1,0:T(8,128)(2,1)} %fusion.39), channel_id=1, source_target_pairs={{0,16},{16,0},{1,17},{17,1},{2,18},{18,2},{3,19},{19,3},{4,20},{20... | collective-permute-start | bytes 1179656 | tf_op jit(solution)/shard_map/ppermute | solution.py:28
  139.1 47.3 %collective-permute-start.32 = (bf16[832,384]{1,0:T(8,128)(2,1)}, bf16[832,384]{1,0:T(8,128)(2,1)}, u32[]{:S(2)}, u32[]{:S(2)}) collective-permute-start(bf16[832,384]{1,0:T(8,128)(2,1)} %copy.101), channel_id=1, source_target_pairs={{0,16},{16,0},{1,17},{17,1},{2,18},{18,2},{3,19},{19,3},{4,20},{20... | collective-permute-start | bytes 1916936 | tf_op jit(solution)/shard_map/ppermute | solution.py:28
  148.5 8.9 %collective-permute-start.27 = (bf16[4,192,128]{2,1,0:T(8,128)(2,1)S(1)}, bf16[4,192,128]{2,1,0:T(8,128)(2,1)S(1)}, u32[]{:S(2)}, u32[]{:S(2)}) collective-permute-start(bf16[4,192,128]{2,1,0:T(8,128)(2,1)S(1)} %get-tuple-element.110), channel_id=1, source_target_pairs={{0,12},{4,8},{8,4},{12,0},{1,13},{5,9},{9,5},{13,1},{2,14},{6,10},... | collective-permute-start | bytes 589832 | tf_op jit(solution)/shard_map/ppermute | solution.py:28
  150.8 10.6 %collective-permute-start.26 = (bf16[4,192,128]{2,1,0:T(8,128)(2,1)S(1)}, bf16[4,192,128]{2,1,0:T(8,128)(2,1)S(1)}, u32[]{:S(2)}, u32[]{:S(2)}) collective-permute-start(bf16[4,192,128]{2,1,0:T(8,128)(2,1)S(1)} %get-tuple-element.111), channel_id=1, source_target_pairs={{0,8},{4,12},{8,0},{12,4},{1,9},{5,13},{9,1},{13,5},{2,10},{6,14},... | collective-permute-start | bytes 589832 | tf_op jit(solution)/shard_map/ppermute | solution.py:28
  151.0 11.6 %collective-permute-start.25 = (bf16[4,192,128]{2,1,0:T(8,128)(2,1)S(1)}, bf16[4,192,128]{2,1,0:T(8,128)(2,1)S(1)}, u32[]{:S(2)}, u32[]{:S(2)}) collective-permute-start(bf16[4,192,128]{2,1,0:T(8,128)(2,1)S(1)} %get-tuple-element.109), channel_id=1, source_target_pairs={{0,4},{4,0},{8,12},{12,8},{1,5},{5,1},{9,13},{13,9},{2,6},{6,2},{1... | collective-permute-start | bytes 589832 | tf_op jit(solution)/shard_map/ppermute | solution.py:28
  154.6 12.9 %collective-permute-start.19 = (bf16[4,192,128]{2,1,0:T(8,128)(2,1)S(1)}, bf16[4,192,128]{2,1,0:T(8,128)(2,1)S(1)}, u32[]{:S(2)}, u32[]{:S(2)}) collective-permute-start(bf16[4,192,128]{2,1,0:T(8,128)(2,1)S(1)} %get-tuple-element.113), channel_id=1, source_target_pairs={{0,12},{4,8},{8,4},{12,0},{1,13},{5,9},{9,5},{13,1},{2,14},{6,10},... | collective-permute-start | bytes 589832 | tf_op jit(solution)/shard_map/ppermute | solution.py:28
  157.5 11.4 %collective-permute-start.18 = (bf16[4,192,128]{2,1,0:T(8,128)(2,1)S(1)}, bf16[4,192,128]{2,1,0:T(8,128)(2,1)S(1)}, u32[]{:S(2)}, u32[]{:S(2)}) collective-permute-start(bf16[4,192,128]{2,1,0:T(8,128)(2,1)S(1)} %get-tuple-element.114), channel_id=1, source_target_pairs={{0,8},{4,12},{8,0},{12,4},{1,9},{5,13},{9,1},{13,5},{2,10},{6,14},... | collective-permute-start | bytes 589832 | tf_op jit(solution)/shard_map/ppermute | solution.py:28
  161.4 10.7 %collective-permute-start.17 = (bf16[4,192,128]{2,1,0:T(8,128)(2,1)S(1)}, bf16[4,192,128]{2,1,0:T(8,128)(2,1)S(1)}, u32[]{:S(2)}, u32[]{:S(2)}) collective-permute-start(bf16[4,192,128]{2,1,0:T(8,128)(2,1)S(1)} %get-tuple-element.112), channel_id=1, source_target_pairs={{0,4},{4,0},{8,12},{12,8},{1,5},{5,1},{9,13},{13,9},{2,6},{6,2},{1... | collective-permute-start | bytes 589832 | tf_op jit(solution)/shard_map/ppermute | solution.py:28
  163.0 13.5 %collective-permute-start.28 = (bf16[192,128]{1,0:T(8,128)(2,1)S(1)}, bf16[192,128]{1,0:T(8,128)(2,1)S(1)}, u32[]{:S(2)}, u32[]{:S(2)}) collective-permute-start(bf16[192,128]{1,0:T(8,128)(2,1)S(1)} %get-tuple-element.143), channel_id=1, source_target_pairs={{17,0},{16,1},{1,2},{0,3},{19,16},{18,17},{3,18},{2,19},{21,4},{20... | collective-permute-start | bytes 147464 | tf_op jit(solution)/shard_map/ppermute | solution.py:238
  167.5 9.0 %collective-permute-start.29 = (bf16[192,128]{1,0:T(8,128)(2,1)S(1)}, bf16[192,128]{1,0:T(8,128)(2,1)S(1)}, u32[]{:S(2)}, u32[]{:S(2)}) collective-permute-start(bf16[192,128]{1,0:T(8,128)(2,1)S(1)} %get-tuple-element.144), channel_id=1, source_target_pairs={{16,0},{17,1},{0,2},{1,3},{18,16},{19,17},{2,18},{3,19},{20,4},{21... | collective-permute-start | bytes 147464 | tf_op jit(solution)/shard_map/ppermute | solution.py:238
  168.9 9.5 %collective-permute-start.30 = (bf16[192,128]{1,0:T(8,128)(2,1)S(1)}, bf16[192,128]{1,0:T(8,128)(2,1)S(1)}, u32[]{:S(2)}, u32[]{:S(2)}) collective-permute-start(bf16[192,128]{1,0:T(8,128)(2,1)S(1)} %get-tuple-element.142), channel_id=1, source_target_pairs={{1,0},{0,1},{17,2},{16,3},{3,16},{2,17},{19,18},{18,19},{5,4},{4,5... | collective-permute-start | bytes 147464 | tf_op jit(solution)/shard_map/ppermute | solution.py:238
  172.0 8.3 %collective-permute-start.31 = (bf16[192,128]{1,0:T(8,128)(2,1)S(1)}, bf16[192,128]{1,0:T(8,128)(2,1)S(1)}, u32[]{:S(2)}, u32[]{:S(2)}) collective-permute-start(bf16[192,128]{1,0:T(8,128)(2,1)S(1)} %get-tuple-element.145), channel_id=1, source_target_pairs={{0,0},{1,1},{16,2},{17,3},{2,16},{3,17},{18,18},{19,19},{4,4},{5,5... | collective-permute-start | bytes 147464 | tf_op jit(solution)/shard_map/ppermute | solution.py:238
  176.5 7.6 %collective-permute-start.21 = (bf16[192,128]{1,0:T(8,128)(2,1)S(1)}, bf16[192,128]{1,0:T(8,128)(2,1)S(1)}, u32[]{:S(2)}, u32[]{:S(2)}) collective-permute-start(bf16[192,128]{1,0:T(8,128)(2,1)S(1)} %get-tuple-element.151), channel_id=1, source_target_pairs={{16,0},{17,1},{0,2},{1,3},{18,16},{19,17},{2,18},{3,19},{20,4},{21... | collective-permute-start | bytes 147464 | tf_op jit(solution)/shard_map/ppermute | solution.py:238
  176.6 7.5 %collective-permute-start.20 = (bf16[192,128]{1,0:T(8,128)(2,1)S(1)}, bf16[192,128]{1,0:T(8,128)(2,1)S(1)}, u32[]{:S(2)}, u32[]{:S(2)}) collective-permute-start(bf16[192,128]{1,0:T(8,128)(2,1)S(1)} %get-tuple-element.153), channel_id=1, source_target_pairs={{17,0},{16,1},{1,2},{0,3},{19,16},{18,17},{3,18},{2,19},{21,4},{20... | collective-permute-start | bytes 147464 | tf_op jit(solution)/shard_map/ppermute | solution.py:238
  178.4 6.7 %collective-permute-start.23 = (bf16[192,128]{1,0:T(8,128)(2,1)S(1)}, bf16[192,128]{1,0:T(8,128)(2,1)S(1)}, u32[]{:S(2)}, u32[]{:S(2)}) collective-permute-start(bf16[192,128]{1,0:T(8,128)(2,1)S(1)} %get-tuple-element.152), channel_id=1, source_target_pairs={{0,0},{1,1},{16,2},{17,3},{2,16},{3,17},{18,18},{19,19},{4,4},{5,5... | collective-permute-start | bytes 147464 | tf_op jit(solution)/shard_map/ppermute | solution.py:238
  180.3 5.4 %collective-permute-start.22 = (bf16[192,128]{1,0:T(8,128)(2,1)S(1)}, bf16[192,128]{1,0:T(8,128)(2,1)S(1)}, u32[]{:S(2)}, u32[]{:S(2)}) collective-permute-start(bf16[192,128]{1,0:T(8,128)(2,1)S(1)} %get-tuple-element.150), channel_id=1, source_target_pairs={{1,0},{0,1},{17,2},{16,3},{3,16},{2,17},{19,18},{18,19},{5,4},{4,5... | collective-permute-start | bytes 147464 | tf_op jit(solution)/shard_map/ppermute | solution.py:238
  184.0 25.1 %collective-permute-start.37 = (bf16[832,768]{1,0:T(8,128)(2,1)}, bf16[832,768]{1,0:T(8,128)(2,1)}, u32[]{:S(2)}, u32[]{:S(2)}) collective-permute-start(bf16[832,768]{1,0:T(8,128)(2,1)} %pad_maximum_fusion.1), channel_id=1, source_target_pairs={{0,16},{16,0},{1,17},{17,1},{2,18},{18,2},{3,19},{19,3},{4,20},{20... | collective-permute-start | bytes 3833864 | tf_op jit(solution)/shard_map/ppermute | solution.py:28
  188.5 8.2 %collective-permute-start.35 = (bf16[208,384]{0,1:T(8,128)(2,1)S(1)}, bf16[208,384]{0,1:T(8,128)(2,1)S(1)}, u32[]{:S(2)}, u32[]{:S(2)}) collective-permute-start(bf16[208,384]{0,1:T(8,128)(2,1)S(1)} %get-tuple-element.118), channel_id=1, source_target_pairs={{0,3},{1,2},{2,1},{3,0},{4,7},{5,6},{6,5},{7,4},{8,11},{9,10},{10,... | collective-permute-start | bytes 479240 | tf_op jit(solution)/shard_map/ppermute | solution.py:28
  188.6 19.7 %collective-permute-start.34 = (bf16[208,384]{0,1:T(8,128)(2,1)S(1)}, bf16[208,384]{0,1:T(8,128)(2,1)S(1)}, u32[]{:S(2)}, u32[]{:S(2)}) collective-permute-start(bf16[208,384]{0,1:T(8,128)(2,1)S(1)} %get-tuple-element.119), channel_id=1, source_target_pairs={{0,2},{1,3},{2,0},{3,1},{4,6},{5,7},{6,4},{7,5},{8,10},{9,11},{10,... | collective-permute-start | bytes 479240 | tf_op jit(solution)/shard_map/ppermute | solution.py:28
  190.5 17.8 %collective-permute-start.33 = (bf16[208,384]{0,1:T(8,128)(2,1)S(1)}, bf16[208,384]{0,1:T(8,128)(2,1)S(1)}, u32[]{:S(2)}, u32[]{:S(2)}) collective-permute-start(bf16[208,384]{0,1:T(8,128)(2,1)S(1)} %get-tuple-element.117), channel_id=1, source_target_pairs={{0,1},{1,0},{2,3},{3,2},{4,5},{5,4},{6,7},{7,6},{8,9},{9,8},{10,11... | collective-permute-start | bytes 479240 | tf_op jit(solution)/shard_map/ppermute | solution.py:28
  208.4 7.6 %collective-permute-start.36 = (bf16[208,384]{0,1:T(8,128)(2,1)S(1)}, bf16[208,384]{0,1:T(8,128)(2,1)S(1)}, u32[]{:S(2)}, u32[]{:S(2)}) collective-permute-start(bf16[208,384]{0,1:T(8,128)(2,1)S(1)} %add_convert_fusion.7), channel_id=1, source_target_pairs={{0,16},{16,0},{1,17},{17,1},{2,18},{18,2},{3,19},{19,3},{4,20},{20... | collective-permute-start | bytes 479240 | tf_op jit(solution)/shard_map/ppermute | solution.py:28
  211.9 11.3 %collective-permute-start.40 = (bf16[208,768]{1,0:T(8,128)(2,1)}, bf16[208,768]{1,0:T(8,128)(2,1)}, u32[]{:S(2)}, u32[]{:S(2)}) collective-permute-start(bf16[208,768]{1,0:T(8,128)(2,1)} %get-tuple-element.107), channel_id=1, source_target_pairs={{0,3},{1,2},{2,1},{3,0},{4,7},{5,6},{6,5},{7,4},{8,11},{9,10},{10,... | collective-permute-start | bytes 958472 | tf_op jit(solution)/shard_map/ppermute | solution.py:28
  212.8 26.9 %collective-permute-start.39 = (bf16[208,768]{1,0:T(8,128)(2,1)}, bf16[208,768]{1,0:T(8,128)(2,1)}, u32[]{:S(2)}, u32[]{:S(2)}) collective-permute-start(bf16[208,768]{1,0:T(8,128)(2,1)} %get-tuple-element.108), channel_id=1, source_target_pairs={{0,2},{1,3},{2,0},{3,1},{4,6},{5,7},{6,4},{7,5},{8,10},{9,11},{10,... | collective-permute-start | bytes 958472 | tf_op jit(solution)/shard_map/ppermute | solution.py:28
  212.8 26.9 %collective-permute-start.38 = (bf16[208,768]{1,0:T(8,128)(2,1)}, bf16[208,768]{1,0:T(8,128)(2,1)}, u32[]{:S(2)}, u32[]{:S(2)}) collective-permute-start(bf16[208,768]{1,0:T(8,128)(2,1)} %get-tuple-element.106), channel_id=1, source_target_pairs={{0,1},{1,0},{2,3},{3,2},{4,5},{5,4},{6,7},{7,6},{8,9},{9,8},{10,11... | collective-permute-start | bytes 958472 | tf_op jit(solution)/shard_map/ppermute | solution.py:28
  216.9 25.2 %copy-start.61 = (f32[192]{0:T(256)S(1)}, f32[192]{0:T(256)}, u32[]{:S(2)}) copy-start(f32[192]{0:T(256)} %copy-done.60) | copy-start | bytes 2308
  241.0 2.1 collective-permute-start.41
  245.2 8.0 %collective-permute-start.44 = (f32[5,192]{1,0:T(8,128)S(1)}, f32[5,192]{1,0:T(8,128)S(1)}, u32[]{:S(2)}, u32[]{:S(2)}) collective-permute-start(f32[5,192]{1,0:T(8,128)S(1)} %stack.125), channel_id=1, source_target_pairs={{0,12},{4,8},{8,4},{12,0},{1,13},{5,9},{9,5},{13,1},{2,14},{6,10},... | collective-permute-start | bytes 11528 | tf_op jit(solution)/shard_map/ppermute | solution.py:28
  246.7 6.5 %collective-permute-start.43 = (f32[5,192]{1,0:T(8,128)S(1)}, f32[5,192]{1,0:T(8,128)S(1)}, u32[]{:S(2)}, u32[]{:S(2)}) collective-permute-start(f32[5,192]{1,0:T(8,128)S(1)} %stack.125), channel_id=1, source_target_pairs={{0,8},{4,12},{8,0},{12,4},{1,9},{5,13},{9,1},{13,5},{2,10},{6,14},... | collective-permute-start | bytes 11528 | tf_op jit(solution)/shard_map/ppermute | solution.py:28
  247.7 5.5 %collective-permute-start.42 = (f32[5,192]{1,0:T(8,128)S(1)}, f32[5,192]{1,0:T(8,128)S(1)}, u32[]{:S(2)}, u32[]{:S(2)}) collective-permute-start(f32[5,192]{1,0:T(8,128)S(1)} %stack.125), channel_id=1, source_target_pairs={{0,4},{4,0},{8,12},{12,8},{1,5},{5,1},{9,13},{13,9},{2,6},{6,2},{1... | collective-permute-start | bytes 11528 | tf_op jit(solution)/shard_map/ppermute | solution.py:28
  253.8 2.1 collective-permute-start.45
  (68 other events, 368.7 us)

commit v2 on v1

v2 whole, which is shorter than its diff:
```python
from functools import partial

import jax
import jax.numpy as jnp
from jax import lax
from jax.experimental import pallas as pl
from jax.experimental.pallas import tpu as pltpu
from jax.sharding import PartitionSpec as P

D = 768
HD = 64
ROT = 16
EPS = 1e-05
PAD = 16

f32 = jnp.float32
bf16 = jnp.bfloat16


def xor_peers(axis, shift):
    return [(i, i ^ shift) for i in range(lax.axis_size(axis))]


def turn_peers(shift):
    count = lax.axis_size("dp")
    return [(i, (i + shift) % count) for i in range(count)]


def send(x, axis, shift):
    return lax.ppermute(x, axis, xor_peers(axis, shift))


def send_near(x):
    pairs = []
    cols = lax.axis_size("col")
    for dp in range(lax.axis_size("dp")):
        pairs += [(dp * cols + c, dp * cols + (c ^ (3 - dp % 2))) for c in range(cols)]
    return lax.ppermute(x, ("dp", "col"), pairs)


def gather_xor(x, axis):
    return [x] + [send(x, axis, k) for k in range(1, lax.axis_size(axis))]


def after(x, others):
    return lax.optimization_barrier((x, others))[0]


def spread_peers(round_of, back=False):
    pairs = []
    cols = lax.axis_size("col")
    for dp in range(lax.axis_size("dp")):
        for col in range(cols):
            half, seq = divmod(col ^ round_of, 2)
            target = (dp // 2 * 2 + half) * cols + 2 * (dp % 2) + seq
            pairs.append((dp * cols + col, target))
    return [(b, a) for a, b in pairs] if back else pairs


def pick(flag, first, second):
    return jnp.where(flag, first, second)


def swap_by(code, parts):
    parts = [pick((code & 1) == 1, parts[j ^ 1], parts[j]) for j in range(4)]
    return [pick((code & 2) == 2, parts[j ^ 2], parts[j]) for j in range(4)]


def sum_parts(parts):
    total = parts[0].astype(f32)
    for part in parts[1:]:
        total = total + part.astype(f32)
    return total


def dot(a, b, contract):
    return lax.dot_general(a, b, (contract, ((), ())), preferred_element_type=f32)


def extend(columns, bias):
    high = lax.reduce_precision(bias, 8, 7)
    rows = jnp.stack([high, bias - high]).astype(bf16)
    rows = jnp.pad(rows, ((0, PAD - 2), (0, 0)))
    return jnp.concatenate([columns.astype(bf16), rows], axis=0)


def call(kernel, outs, args, scalars=None):
    specs = [pl.BlockSpec(memory_space=pltpu.VMEM) for _ in args]
    if scalars is not None:
        specs = [pl.BlockSpec(memory_space=pltpu.SMEM)] + specs
        args = [scalars, *args]
    return pl.pallas_call(
        kernel,
        out_shape=outs,
        in_specs=specs,
        out_specs=[pl.BlockSpec(memory_space=pltpu.VMEM) for _ in outs],
        compiler_params=pltpu.CompilerParams(vmem_limit_bytes=48 * 2**20),
        cost_estimate=pl.CostEstimate(flops=0, bytes_accessed=0, transcendentals=0),
    )(*args)


def shaped(shape, dtype):
    return jax.ShapeDtypeStruct(shape, dtype)


def place_kernel(scal, *refs):
    parts, (xn_ref, cot_ref) = refs[:4], refs[4:]
    block = xn_ref.shape[0] // 4
    width, span = parts[0].shape[2:]
    row, crossed = scal[0], scal[2]
    for j in range(4):
        ref = parts[j]
        at = pl.multiple_of((row ^ j) * span, span)
        x = ref[:, 0].astype(f32)
        x = x - jnp.mean(x, axis=(0, 1), keepdims=True)
        x = (x * lax.rsqrt(jnp.mean(x * x, axis=(0, 1), keepdims=True) + EPS)).astype(bf16)
        for k in range(4):
            to = pl.multiple_of((k ^ (2 * crossed)) * block, PAD)
            xn_ref[pl.ds(to, width), pl.ds(at, span)] = x[k]
            cot_ref[pl.ds(to, width), pl.ds(at, span)] = ref[k, 1]
    rest = (lax.broadcasted_iota(jnp.int32, (PAD, xn_ref.shape[1]), 0) < 2).astype(f32).astype(bf16)
    for k in range(4):
        xn_ref[k * block + width : (k + 1) * block, :] = rest
        cot_ref[k * block + width : (k + 1) * block, :] = jnp.zeros_like(rest)


def turn(x, cosine, sine):
    half = ROT // 2
    a, b = x[:half], x[half:ROT]
    return jnp.concatenate([a * cosine - b * sine, b * cosine + a * sine, x[ROT:]], axis=0)


def dot00(a, b):
    return dot(a, b, ((0,), (0,)))


def dot11(a, b):
    return dot(a, b, ((1,), (1,)))


def dot10(a, b):
    return dot(a, b, ((1,), (0,)))


def weight(parts, i, u):
    own, near, near_other, far, far_other = parts
    if i == 3:
        return (far, far_other)[u][...]
    half = far.shape[1]
    side = 1 - u if i == 2 else u
    return (own, near, near_other)[i][:, side * half : (side + 1) * half]


def blocks_of(core, size):
    return [pl.ds(pl.multiple_of(b * size, PAD), size) for b in (0, 3 - core, 2 + core, 1)]


def qkv_kernel(heads, scal, tables, xn, cot, *refs):
    weights, (q_ref, kv_ref, ga_ref) = refs[:5], refs[5:]
    sub = HD // 2
    at_blocks = blocks_of(scal[1], weights[0].shape[0])
    third = heads * sub
    for u in range(2):
        w = [weight(weights, i, u) for i in range(4)]
        pre = sum(dot00(w[i], xn[at_blocks[i], :]) for i in range(4))
        grad = sum(dot00(w[i][:, 2 * 128 :], cot[at_blocks[i], :]) for i in range(4))
        cosine, sine = tables[2 * u], tables[2 * u + 1]
        for h in range(heads):
            dims = slice(u * sub, (u + 1) * sub)
            at = h * sub
            q_ref[h, dims, :] = turn(pre[at : at + sub], cosine, sine).astype(bf16)
            at += third
            kv_ref[0, h, dims, :] = turn(pre[at : at + sub], cosine, sine).astype(bf16)
            at += third
            kv_ref[1, h, dims, :] = pre[at : at + sub].astype(bf16)
            at += third - 2 * 128
            ga_ref[h, dims, :] = grad[at : at + sub].astype(bf16)


def put_sums(keep, give, i, u, value):
    half = value.shape[1]
    if i == 1:
        keep[:, u * half : (u + 1) * half] = value
    elif i == 2:
        give[:, (1 - u) * half : (2 - u) * half] = value
    else:
        at = (2 if i == 3 else 3) * half
        (keep, give)[u][:, at : at + half] = value


def swapped(x):
    sub = HD // 2
    return jnp.concatenate([x[sub:], x[:sub]], axis=0)


def attention_kernel(
    span, scal, start, q_ref, kv_ref, kv_other, ga_ref, att_ref, gq_ref, gkv_ref, gkv_other, kc, vc, gk, gv
):
    count = q_ref.shape[2]
    rows = 2 * count // span
    half = span // 2
    core = scal[1]
    for rr in range(rows):
        mine, lanes = slice(rr * half, (rr + 1) * half), rr * span
        for ref, at in ((kc, 0), (vc, 1)):
            ref[:, lanes : lanes + half] = kv_ref[at, 0, :, mine]
            ref[:, lanes + half : lanes + span] = swapped(kv_other[at, 0, :, mine])
    kt, vt = kc[...].T, vc[...].T
    gk[...] = jnp.zeros_like(gk)
    gv[...] = jnp.zeros_like(gv)
    scale = HD ** (-0.5)
    for a in range(rows):
        size = (a + 1) * span
        mine = slice(a * half, (a + 1) * half)
        q, ga = q_ref[0, :, mine], ga_ref[0, :, mine]
        key = lax.broadcasted_iota(jnp.int32, (size, 1), 0)
        at = key % span
        key = key - at + jnp.where((at >= half) == (core == 0), half, 0) + at % half
        query = lax.broadcasted_iota(jnp.int32, (1, half), 1) + (a * span + core * half)
        first = start[:, mine]
        allowed = (key <= query) & (key >= first)
        scores = jnp.where(allowed, dot10(kt[:size], q) * scale, -1000000000.0)
        top = jnp.max(scores, axis=0, keepdims=True)
        exponent = jnp.exp(scores - top)
        probs = exponent * (1.0 / jnp.sum(exponent, axis=0, keepdims=True))
        low = probs.astype(bf16)
        att_ref[0, :, mine] = dot10(vc[:, :size], low).astype(bf16)
        grad = dot10(vt[:size], ga)
        total = jnp.sum(grad * probs, axis=0, keepdims=True)
        grad = (probs * (grad - total) * scale).astype(bf16)
        gq_ref[0, :, mine] = dot10(kc[:, :size], grad)
        gk[:, :size] += dot11(q, grad)
        gv[:, :size] += dot11(ga, low)
    for rr in range(rows):
        mine, lanes = slice(rr * half, (rr + 1) * half), rr * span
        for ref, at in ((gk, 0), (gv, 1)):
            gkv_ref[at, 0, :, mine] = ref[:, lanes : lanes + half]
            gkv_other[at, 0, :, mine] = ref[:, lanes + half : lanes + span].astype(bf16)


def qkv_grad_kernel(heads, scal, tables, gq_ref, gkv_ref, gk_other, gv_other, att_ref, xn, cot, *outs):
    sub = HD // 2
    third = heads * sub
    keep, give = outs[4:]
    at_blocks = blocks_of(scal[1], keep.shape[0])
    zeros = jnp.zeros((third, xn.shape[1]), bf16)
    for u in range(2):
        grads_ref, att_out = outs[2 * u : 2 * u + 2]
        cosine, sine = tables[2 * u], tables[2 * u + 1]
        dims = slice(u * sub, (u + 1) * sub)
        swap = slice((1 - u) * sub, (2 - u) * sub)
        for h in range(heads):
            at = h * sub
            grads_ref[at : at + sub, :] = turn(gq_ref[h, dims, :], cosine, -sine).astype(bf16)
            g = gkv_ref[0, h, dims, :] + gk_other[0, h, swap, :].astype(f32)
            at += third
            grads_ref[at : at + sub, :] = turn(g, cosine, -sine).astype(bf16)
            g = gkv_ref[1, h, dims, :] + gv_other[0, h, swap, :].astype(f32)
            at += third
            grads_ref[at : at + sub, :] = g.astype(bf16)
            at += third
            att_out[at : at + sub, :] = att_ref[h, dims, :]
        grads_ref[3 * third :, :] = zeros
        for s in range(3):
            att_out[s * third : (s + 1) * third, :] = zeros
        for i in range(4):
            total = dot11(xn[at_blocks[i], :], grads_ref[...]) + dot11(cot[at_blocks[i], :], att_out[...])
            put_sums(keep, give, i, u, total.astype(bf16))


def feed_kernel(scal, xn, cot, *refs):
    weights, acts, (keep, give) = refs[:5], refs[5:9], refs[9:]
    at_blocks = blocks_of(scal[1], weights[0].shape[0])
    part = acts[0].shape[0]
    for u in range(2):
        up_ref, grad_ref = acts[2 * u : 2 * u + 2]
        w = [weight(weights, i, u) for i in range(4)]
        pre = sum(dot00(w[i][:, :part], xn[at_blocks[i], :]) for i in range(4))
        phi = 0.5 * (1.0 + lax.erf(pre * (0.5**0.5)))
        slope = phi + pre * (jnp.exp(-0.5 * pre * pre) * 0.3989422804014327)
        up_ref[...] = (pre * phi).astype(bf16)
        grad = sum(dot00(w[i][:, part:], cot[at_blocks[i], :]) for i in range(4))
        grad_ref[...] = (grad * slope).astype(bf16)
        for i in range(4):
            total = jnp.concatenate(
                [
                    dot11(xn[at_blocks[i], :], grad_ref[...]).astype(bf16),
                    dot11(cot[at_blocks[i], :], up_ref[...]).astype(bf16),
                ],
                axis=1,
            )
            put_sums(keep, give, i, u, total)


def back_kernel(scal, *refs):
    w1, w2, acts, outs = refs[:5], refs[5:10], refs[10:18], refs[18:]
    part = acts[4].shape[0]
    rows, (_, _, width, span) = len(outs), outs[0].shape
    row, core = scal[0], scal[1]
    for i, to in enumerate((0, 3 - core, 2 + core, 1)):
        for way in range(2):
            side = slice((1 - way) * part, (2 - way) * part)
            total = sum(dot10(weight(w1, i, u), acts[2 * way + u][...]) for u in range(2))
            total += sum(dot10(weight(w2, i, u)[:, side], acts[4 + 2 * way + u][...]) for u in range(2))
            total = total[:width].astype(bf16)
            for j, out in enumerate(outs):
                value = total[:, :span]
                for rr in range(1, rows):
                    value = jnp.where((row ^ j) == rr, total[:, rr * span : (rr + 1) * span], value)
                out[to, way] = value


def pair_kernel(*refs):
    near, far, own = refs[4:]
    to = 0
    for keep, got in (refs[:2], refs[2:4]):
        size = keep.shape[1] // 4
        total = keep[...].astype(f32) + got[...].astype(f32)
        near[:, 2 * to : 2 * to + 2 * size] = total[:, : 2 * size].astype(bf16)
        far[:, to : to + size] = total[:, 2 * size : 3 * size].astype(bf16)
        own[:, to : to + size] = total[:, 3 * size :]
        to += size


def total_kernel(near, far, own, out):
    third = far.shape[1] // 3
    for at, size in ((0, third), (third, 2 * third)):
        mine = slice(at, at + size)
        total = near[:, 2 * at : 2 * at + size].astype(f32) + far[:, mine].astype(f32) + own[:, mine]
        out[:, 2 * at : 2 * at + size] = total.astype(bf16)
        out[:, 2 * at + size : 2 * (at + size)] = near[:, 2 * at + size : 2 * (at + size)]


def final_kernel(scal, here, there, scales, wq_ref, win_ref, d_wq, d_wd, d_win, d_wout, d_bq, d_bf, small):
    heads, width, _ = d_wd.shape
    sub = HD // 2
    tail = d_win.shape[1]
    part = tail // 2
    third = heads * sub
    mine_first = scal[1] == 0
    gain1, shift1, gain2, shift2 = (scales[:, i : i + 1] for i in range(4))

    def both(at, size):
        lo, hi = slice(at, at + size), slice(at + size, at + 2 * size)
        mine = here[:, lo].astype(f32) + there[:, hi].astype(f32)
        theirs = here[:, hi].astype(f32) + there[:, lo].astype(f32)
        return jnp.where(mine_first, mine, theirs), jnp.where(mine_first, theirs, mine)

    sums = [jnp.zeros((width, 1), f32) for _ in range(4)]
    for a, m in enumerate(both(0, 4 * third)):
        dims = slice(a * sub, (a + 1) * sub)
        row = m[width : width + 1, : 3 * third]
        w = wq_ref[a].astype(f32)
        sums[0] += jnp.sum(w * m[:width, : 3 * third], axis=1, keepdims=True)
        sums[1] += jnp.sum(w * row, axis=1, keepdims=True)
        d_bq[a : a + 1, :] = row
        grad = m[:width, : 3 * third] * gain1 + shift1 * row
        for s in range(3):
            for h in range(heads):
                at = (s * heads + h) * sub
                d_wq[s, h, :, dims] = grad[:, at : at + sub]
        for h in range(heads):
            at = 3 * third + h * sub
            d_wd[h, :, dims] = m[:width, at : at + sub]
    for a, m in enumerate(both(8 * third, tail)):
        cols = slice(a * part, (a + 1) * part)
        row = m[width : width + 1, :part]
        w = win_ref[:, cols].astype(f32)
        sums[2] += jnp.sum(w * m[:width, :part], axis=1, keepdims=True)
        sums[3] += jnp.sum(w * row, axis=1, keepdims=True)
        d_bf[a : a + 1, :] = row
        d_win[:, cols] = m[:width, :part] * gain2 + shift2 * row
        d_wout[:, cols] = m[:width, part:]
    small[...] = jnp.concatenate(sums, axis=1)


def row_kernel(scal, x_ref, *refs):
    parts, outs = refs[:4], refs[4:]
    crossed = scal[2]
    x = x_ref[:, 0].astype(f32)
    x = x - jnp.mean(x, axis=(0, 1), keepdims=True)
    rstd = lax.rsqrt(jnp.mean(x * x, axis=(0, 1), keepdims=True) + EPS)
    x = x * rstd
    sums = []
    for way in range(2):
        total = sum(p[:, way].astype(f32) for p in parts)
        sums.append([jnp.where(crossed == 1, total[k ^ 2], total[k]) for k in range(4)])
    grad = jnp.stack(sums[1])
    grad = rstd * (
        grad
        - jnp.mean(grad, axis=(0, 1), keepdims=True)
        - x * jnp.mean(grad * x, axis=(0, 1), keepdims=True)
    )
    for k in range(4):
        outs[k][0] = sums[0][k].astype(bf16)
        outs[k][1] = grad[k].astype(bf16)


def body(
    hidden_in,
    segments,
    w_qkv,
    b_qkv,
    w_dense,
    b_dense,
    ln1_gain,
    ln1_bias,
    ln2_gain,
    ln2_bias,
    w_in,
    b_in,
    w_out,
    b_out,
    cotangent,
):
    width, seqs, span = hidden_in.shape
    half_span = span // 2
    cols, rows, dps = lax.axis_size("col"), lax.axis_size("row"), lax.axis_size("dp")
    heads = w_qkv.shape[1]
    hw = heads * HD
    sub = HD // 2
    ff = w_in.shape[1]
    core = lax.axis_index("dp") % 2
    row = lax.axis_index("row")
    col = lax.axis_index("col")
    first_core = core == 0
    crossed = (core ^ (col >> 1)) == 1
    block = width + PAD
    count = rows * half_span

    both = jnp.stack([hidden_in, cotangent])
    pieces = [both[:, :, j % 2, (j // 2) * half_span : (j // 2 + 1) * half_span] for j in range(4)]
    sent = swap_by(col, pieces)
    got = [lax.ppermute(sent[k], ("dp", "col"), spread_peers(k)) for k in range(4)]
    mine = jnp.stack(got)
    tokens = gather_xor(mine, "row")

    counts = jnp.stack([jnp.sum(segments < 1, axis=1), jnp.sum(segments < 2, axis=1)], axis=1).astype(f32)
    counts_other = send(counts, "dp", 1)
    counts = pick((col >> 1) == core, counts, counts_other)
    counts = pick((col & 1) == 1, counts[1], counts[0]).astype(jnp.int32)
    scalars = jnp.stack([row, core, crossed.astype(jnp.int32)])

    gain1, shift1 = ln1_gain.astype(f32), ln1_bias.astype(f32)
    gain2, shift2 = ln2_gain.astype(f32), ln2_bias.astype(f32)

    def in_order(halves):
        low, high = halves
        return jnp.concatenate([pick(first_core, low, high), pick(first_core, high, low)], axis=-1)

    wq = w_qkv.reshape(3, heads, width, 2, sub).transpose(3, 2, 0, 1, 4).reshape(2, width, -1)
    wd = w_dense.reshape(heads, width, 2, sub).transpose(2, 1, 0, 3).reshape(2, width, -1)
    bias_q = b_qkv.reshape(3, heads, 2, sub).transpose(2, 0, 1, 3).reshape(2, -1).astype(f32) / cols
    part = ff // 2
    bias_f = b_in.reshape(2, part).astype(f32) / cols
    halves1, halves2 = [], []
    for u in range(2):
        w = wq[u].astype(f32)
        bias = jnp.sum(w * shift1[:, None], axis=0) + bias_q[u]
        halves1.append(
            extend(
                jnp.concatenate([w * gain1[:, None], wd[u].astype(f32)], axis=1),
                jnp.concatenate([bias, jnp.zeros((heads * sub,), f32)]),
            )
        )
        w = w_in[:, u * part : (u + 1) * part].astype(f32)
        bias = jnp.sum(w * shift2[:, None], axis=0) + bias_f[u]
        halves2.append(
            extend(
                jnp.concatenate([w * gain2[:, None], w_out[:, u * part : (u + 1) * part].astype(f32)], axis=1),
                jnp.concatenate([bias, jnp.zeros((part,), f32)]),
            )
        )

    head, tail = 2 * hw, 2 * part
    own1, own2 = in_order(halves1), in_order(halves2)
    near1 = send_near(after(own1, [sent, counts_other]))
    far = send(jnp.concatenate([own1[:, :head], own2[:, :tail]], axis=1), "col", 1)
    near2 = send_near(after(own2, [near1, far, tokens[1:]]))
    far_other = send(far, "dp", 1)
    w1 = [own1, near1, send(near1, "dp", 1), far[:, :head], far_other[:, :head]]

    base = jnp.arange(half_span, dtype=jnp.int32)
    q_pos = jnp.concatenate([rr * span + core * half_span + base for rr in range(rows)])
    q_start = jnp.where(q_pos >= counts[1], counts[1], jnp.where(q_pos >= counts[0], counts[0], 0))
    frequency = 10000.0 ** (-jnp.arange(ROT // 2, dtype=f32) * 2.0 / ROT)
    angles = (q_pos - q_start).astype(f32)[None, :] * frequency[:, None]
    cosine, sine = jnp.cos(angles), jnp.sin(angles)
    unit, nil = jnp.ones_like(cosine), jnp.zeros_like(sine)
    tables = jnp.stack(
        [
            pick(first_core, cosine, unit),
            pick(first_core, sine, nil),
            pick(first_core, unit, cosine),
            pick(first_core, nil, sine),
        ]
    )

    grid_shape = (cols * block, count)
    xn, cot = call(place_kernel, [shaped(grid_shape, bf16)] * 2, tokens, scalars)
    queries, kv, grad_att = call(
        partial(qkv_kernel, heads),
        [
            shaped((heads, HD, count), bf16),
            shaped((2, heads, HD, count), bf16),
            shaped((heads, HD, count), bf16),
        ],
        [tables, xn, cot, *w1],
        scalars,
    )
    kv_other = send(kv, "dp", 1)

    by_head = pl.BlockSpec((1, HD, count), lambda h: (h, 0, 0))
    by_head2 = pl.BlockSpec((2, 1, HD, count), lambda h: (0, h, 0, 0))
    attended, grad_q, grad_kv, grad_kv_other = pl.pallas_call(
        partial(attention_kernel, span),
        grid=(heads,),
        in_specs=[
            pl.BlockSpec(memory_space=pltpu.SMEM),
            pl.BlockSpec((1, count), lambda h: (0, 0)),
            by_head,
            by_head2,
            by_head2,
            by_head,
        ],
        out_specs=[by_head, by_head, by_head2, by_head2],
        out_shape=[
            shaped((heads, HD, count), bf16),
            shaped((heads, HD, count), f32),
            shaped((2, heads, HD, count), f32),
            shaped((2, heads, HD, count), bf16),
        ],
        scratch_shapes=[
            pltpu.VMEM((HD, 2 * count), bf16),
            pltpu.VMEM((HD, 2 * count), bf16),
            pltpu.VMEM((HD, 2 * count), f32),
            pltpu.VMEM((HD, 2 * count), f32),
        ],
        compiler_params=pltpu.CompilerParams(vmem_limit_bytes=48 * 2**20),
        cost_estimate=pl.CostEstimate(
            flops=0, bytes_accessed=0, transcendentals=0
        ),
    )(scalars, q_start[None, :], queries, kv, kv_other, grad_att)
    grad_kv_got = [send(grad_kv_other[:1], "dp", 1), send(grad_kv_other[1:], "dp", 1)]

    near2 = after(near2, [attended])
    w2 = [own2, near2, send(near2, "dp", 1), far[:, head:], far_other[:, head:]]
    act = shaped((part, count), bf16)
    sums2 = shaped((block, 4 * tail), bf16)
    up_a, hid_a, up_b, hid_b, keep2, give2 = call(
        feed_kernel, [act] * 4 + [sums2] * 2, [xn, cot, *w2], scalars
    )
    got2 = send(give2, "dp", 1)

    half_act = shaped((head, count), bf16)
    sums1 = shaped((block, 4 * head), bf16)
    grads_a, att_a, grads_b, att_b, keep1, give1 = call(
        partial(qkv_grad_kernel, heads),
        [half_act] * 4 + [sums1] * 2,
        [tables, grad_q, grad_kv, *grad_kv_got, after(attended, keep2), xn, cot],
        scalars,
    )
    got1 = send(give1, "dp", 1)
    low_near, low_far, own_sum = call(
        pair_kernel,
        [
            shaped((block, 2 * (head + tail)), bf16),
            shaped((block, head + tail), bf16),
            shaped((block, head + tail), f32),
        ],
        [keep1, got1, keep2, got2],
    )
    sum_near = send_near(low_near)
    sum_far = send(low_far, "col", 1)

    strip = shaped((cols, 2, width, half_span), bf16)
    sums = call(
        back_kernel,
        [strip] * rows,
        [*w1, *w2, *after([att_a, att_b, grads_a, grads_b, up_a, up_b, hid_a, hid_b], [low_near])],
        scalars,
    )
    sums = [sums[0]] + [send(sums[j], "row", j) for j in range(1, rows)]
    piece = shaped((2, width, half_span), bf16)
    back = call(row_kernel, [piece] * cols, [mine, *sums], scalars)
    back = [lax.ppermute(back[k], ("dp", "col"), spread_peers(k, True)) for k in range(4)]
    back = swap_by(col, back)
    branch, grad_x = jnp.stack(
        [jnp.concatenate([back[s], back[2 + s]], axis=2) for s in range(2)], axis=2
    ).astype(f32)
    bias_out = b_dense.astype(f32) + b_out.astype(f32)
    layer_out = (hidden_in.astype(f32) + branch + bias_out[:, None, None]).astype(bf16)
    grad_in = cotangent.astype(f32) + grad_x

    total = call(total_kernel, [shaped((block, 2 * (head + tail)), bf16)], [sum_near, sum_far, own_sum])[0]
    wide = total.astype(f32)
    for k in range(2, dps, 2):
        wide = wide + lax.ppermute(total, "dp", turn_peers(k)).astype(f32)
    total = wide.astype(bf16)
    other = send(total, "dp", 1)

    scales = jnp.stack([gain1, shift1, gain2, shift2], axis=1)
    d_wq, d_wd, d_w_in, d_w_out, d_bq, d_bf, small = call(
        final_kernel,
        [
            shaped((3, heads, width, HD), f32),
            shaped((heads, width, HD), f32),
            shaped((width, ff), f32),
            shaped((width, ff), f32),
            shaped((2, 3 * heads * sub), f32),
            shaped((2, part), f32),
            shaped((width, 4), f32),
        ],
        [total, other, scales, wq, w_in],
        scalars,
    )
    c_sum = jnp.sum(cotangent.astype(f32), axis=(1, 2))
    small = jnp.concatenate([small.T, c_sum[None]])
    small = sum_parts(gather_xor(small, "row"))
    d_shared = small[4]
    for k in range(1, dps):
        d_shared = d_shared + lax.ppermute(small[4], "dp", turn_peers(k))
    return (
        layer_out,
        grad_in,
        d_wq.reshape(w_qkv.shape),
        d_bq.reshape(2, 3, heads, sub).transpose(1, 2, 0, 3).reshape(3, hw),
        d_wd.reshape(w_dense.shape),
        d_shared,
        small[0],
        small[1],
        small[2],
        small[3],
        d_w_in,
        d_bf.reshape(ff),
        d_w_out,
        d_shared,
    )


def solution(mesh):
    placed = (
        P("col", "dp", "row"),
        P("dp", None),
        P(None, "row", "col"),
        P(None, "row"),
        P("row", "col"),
        P("col"),
        P("col"),
        P("col"),
        P("col"),
        P("col"),
        P("col", "row"),
        P("row"),
        P("col", "row"),
        P("col"),
        P("col", "dp", "row"),
    )
    return jax.shard_map(
        body,
        mesh=mesh,
        in_specs=placed,
        out_specs=(
            P("col", "dp", "row"),
            P("col", "dp", "row"),
            P(None, "row", "col"),
            P(None, "row"),
            P("row", "col"),
            P("col"),
            P("col"),
            P("col"),
            P("col"),
            P("col"),
            P("col", "row"),
            P("row"),
            P("col", "row"),
            P("col"),
        ),
        check_vma=False,
    )
```

time: 261 us -> 164 us (0.63); the launches traced: 257 us -> 163 us
  matrix products: 69 us -> 0 us
  Pallas kernels: 0 us -> 34.5 us
  starting transfers between devices: 63 us -> 38.5 us
  other arithmetic: 30.3 us -> 6.91 us
  local copies, waits for them, and re-layouts: 30.5 us -> 17.1 us
  waiting for transfers between devices: 61.5 us -> 65 us
    dot_general x26 -> x0, matrix products: 62.6 us -> none  [the longest x21 30.7 us: dot(): lax.dot_general(a, b, (contract, ((), ())), preferred_element_type=f32)]
    pallas_call x0 -> x10, Pallas kernels: none -> 34.5 us  [the longest x9 23.8 us: call(): pl.pallas_call(kernel, out_shape=outs, in_specs=specs, out_specs=[pl.Bloc...]
    ppermute x8 -> x7, waiting for transfers between devices: 1.67 us -> 25.2 us  [the longest x3 21.3 us: send_near(): return lax.ppermute(x, ('dp', 'col'), pairs)]
    ppermute x33 -> x21, waiting for transfers between devices: 56.5 us -> 39.9 us  [send(): return lax.ppermute(x, axis, xor_peers(axis, shift))]
    ppermute x33 -> x21, starting transfers between devices: 29.3 us -> 14.5 us  [send(): return lax.ppermute(x, axis, xor_peers(axis, shift))]
    concatenate x12 -> x6, other arithmetic: 7.26 us -> 0.14 us  [the longest x2 0.07 us: in_order(): jnp.concatenate([pick(first_core, low, high), pick(first_core, high, low)...]
    sub x1 -> x0, matrix products: 6.36 us -> none  [body(): exponent = jnp.exp(scores - top)]
    ppermute x4, starting transfers between devices: 14.1 us -> 7.8 us  [body(): lax.ppermute(sent[k], ('dp', 'col'), spread_peers(k))]
  transfers between devices with their start and end apart: 46 -> 33, of which waited for: 12 -> 15; matrix products, arithmetic and copies ran while one was open for 45% -> 11% of each run, Pallas kernels for 0% -> 15%
where the time goes in v2:
time: 164 us; the launch traced here: 163 us
  waiting for transfers between devices  65 us (40%)
  starting transfers between devices  38.5 us (23%)
  Pallas kernels  34.5 us (21%)
  local copies, waits for them, and re-layouts  17.1 us (10%)
  other arithmetic  6.91 us (4%)
    ppermute x21, waiting for transfers between devices, send(): return lax.ppermute(x, axis, xor_peers(axis, shift))  39.9 us
    pallas_call x9, Pallas kernels, call(): pl.pallas_call(kernel, out_shape=outs, in_specs=specs, out_specs=[pl.Bloc...  23.8 us
    ppermute x3, waiting for transfers between devices, send_near(): return lax.ppermute(x, ('dp', 'col'), pairs)  21.3 us
    ppermute x21, starting transfers between devices, send(): return lax.ppermute(x, axis, xor_peers(axis, shift))  14.5 us
    ppermute x4, starting transfers between devices, body(): lax.ppermute(back[k], ('dp', 'col'), spread_peers(k, True))  11.5 us
    pallas_call x1, Pallas kernels, body(): pl.pallas_call(partial(attention_kernel, span), grid=(heads,), in_specs=[...  10.6 us
    ppermute x4, starting transfers between devices, body(): lax.ppermute(sent[k], ('dp', 'col'), spread_peers(k))  7.8 us
    unnamed x57, local copies, waits for them, and re-layouts  7.01 us
  transfers between devices with their start and end apart: 33, of which 15 were waited for; matrix products, arithmetic and copies ran while one was open for 11% of the time, Pallas kernels for 15%

profile of v2, /device:TPU:1, one launch (start us, length us, event | category | flops | bytes accessed | tf_op | source)
XLA Modules:
  0.0 163.5 jit_solution(5511283714949834886)
XLA Ops:
  0.7 1.1 copy_bitcast_fusion
  2.6 3.1 %collective-permute-start.2 = (bf16[2,192,128]{2,1,0:T(8,128)(2,1)}, bf16[2,192,128]{2,1,0:T(8,128)(2,1)S(1)}, u32[]{:S(2)}, u32[]{:S(2)}) collective-permute-start(bf16[2,192,128]{2,1,0:T(8,128)(2,1)} %get-tuple-element.212), channel_id=1, source_target_pairs={{0,16},{1,17},{2,0},{3,1},{16,18},{17,19},{18,2},{19,3},{4,20},{5,... | collective-permute-start | bytes 294920 | tf_op jit(solution)/shard_map/ppermute | solution.py:434
  5.8 1.7 %collective-permute-start.3 = (bf16[2,192,128]{2,1,0:T(8,128)(2,1)}, bf16[2,192,128]{2,1,0:T(8,128)(2,1)S(1)}, u32[]{:S(2)}, u32[]{:S(2)}) collective-permute-start(bf16[2,192,128]{2,1,0:T(8,128)(2,1)} %get-tuple-element.213), channel_id=1, source_target_pairs={{0,17},{1,16},{2,1},{3,0},{16,19},{17,18},{18,3},{19,2},{4,21},{5,... | collective-permute-start | bytes 294920 | tf_op jit(solution)/shard_map/ppermute | solution.py:434
  7.7 2.7 %collective-permute-start = (bf16[2,192,128]{2,1,0:T(8,128)(2,1)S(1)}, bf16[2,192,128]{2,1,0:T(8,128)(2,1)S(1)}, u32[]{:S(2)}, u32[]{:S(2)}) collective-permute-start(bf16[2,192,128]{2,1,0:T(8,128)(2,1)S(1)} %get-tuple-element.194), channel_id=1, source_target_pairs={{0,0},{1,1},{2,16},{3,17},{16,2},{17,3},{18,18},{19,19},{4,4},{5,5... | collective-permute-start | bytes 294920 | tf_op jit(solution)/shard_map/ppermute | solution.py:434
  15.3 2.8 %collective-permute-start.7 = (bf16[208,1152]{1,0:T(8,128)(2,1)S(1)}, bf16[208,1152]{1,0:T(8,128)(2,1)S(1)}, u32[]{:S(2)}, u32[]{:S(2)}) collective-permute-start(bf16[208,1152]{1,0:T(8,128)(2,1)S(1)} %pad_maximum_fusion.1), channel_id=1, source_target_pairs={{0,1},{1,0},{2,3},{3,2},{4,5},{5,4},{6,7},{7,6},{8,9},{9,8},{10,11... | collective-permute-start | bytes 1437704 | tf_op jit(solution)/shard_map/ppermute | solution.py:30
  18.3 1.3 collective-permute-start.10
  19.6 1.2 collective-permute-start.11
  21.1 13.4 %collective-permute-done.7 = bf16[208,1152]{1,0:T(8,128)(2,1)S(1)} collective-permute-done((bf16[208,1152]{1,0:T(8,128)(2,1)S(1)}, bf16[208,1152]{1,0:T(8,128)(2,1)S(1)}, u32[]{:S(2)}, u32[]{:S(2)}) %collective-permute-start.7) | collective-permute-done | bytes 479264 | tf_op jit(solution)/shard_map/ppermute | solution.py:30
  34.5 1.6 collective-permute-start.8
  36.6 1.3 subtract_convert_fusion
  38.0 3.1 %collective-permute-start.12 = (bf16[208,1536]{1,0:T(8,128)(2,1)S(1)}, bf16[208,1536]{1,0:T(8,128)(2,1)S(1)}, u32[]{:S(2)}, u32[]{:S(2)}) collective-permute-start(bf16[208,1536]{1,0:T(8,128)(2,1)S(1)} %pad_maximum_fusion.refs_0_.refs_5_), channel_id=1, source_target_pairs={{0,3},{1,2},{2,1},{3,0},{16,18},{17,19},{18,16},{19,17},{4,7},{5,6... | collective-permute-start | bytes 1916936 | tf_op jit(solution)/shard_map/ppermute | solution.py:38
  41.3 1.3 shard_map.254
  42.6 1.8 %shard_map.255 = (bf16[3,64,512]{2,1,0:T(8,128)(2,1)S(1)}, bf16[2,3,64,512]{3,2,1,0:T(8,128)(2,1)S(1)}, bf16[3,64,512]{2,1,0:T(8,128)(2,1)S(1)}) custom-call(s32[3]{0:T(128)S(1)} %pad_add_fusion.1.scal, f32[4,8,512]{2,1,0:T(8,128)S(1)} %pad_maximum_fusion.9.tables, bf16[832,512]{1,0:T(8,128)(2,1)S(1)} %get-tuple-element.67.xn, ...), custom_call_target="tpu_custom_call" | custom-call | tf_op jit(solution)/shard_map/pallas_call | solution.py:92
  45.3 1.3 compare_select_fusion.1.start
  46.6 10.6 %shard_map.256 = (bf16[3,64,512]{2,1,0:T(8,128)(2,1)S(1)}, f32[3,64,512]{2,1,0:T(8,128)S(1)}, f32[2,3,64,512]{3,2,1,0:T(8,128)S(1)}, bf16[2,3,64,512]{3,2,1,0:T(8,128)(2,1)S(1)}) custom-call(s32[3]{0:T(128)S(1)} %pad_add_fusion.1.scal, s32[1,512]{1,0:T(1,128)S(1)} %compare_select_fusion.1.start, bf16[3,64,512]{2,1,0:T(8,128)(2,1)S(1)} %get-tuple-element.69.q_ref, ...), custom_call_target="tpu_custom_call" | custom-call | tf_op jit(solution)/shard_map/pallas_call | solution.py:515
  57.3 11.5 %collective-permute-done.12.refs_1_.refs_6_ = bf16[208,1536]{1,0:T(8,128)(2,1)S(1)} collective-permute-done((bf16[208,1536]{1,0:T(8,128)(2,1)S(1)}, bf16[208,1536]{1,0:T(8,128)(2,1)S(1)}, u32[]{:S(2)}, u32[]{:S(2)}) %collective-permute-start.12) | collective-permute-done | bytes 639008 | tf_op jit(solution)/shard_map/ppermute | solution.py:38
  68.9 2.0 %collective-permute-done.14.refs_2_.refs_7_ = bf16[208,1536]{1,0:T(8,128)(2,1)S(1)} collective-permute-done((bf16[208,1536]{1,0:T(8,128)(2,1)S(1)}, bf16[208,1536]{1,0:T(8,128)(2,1)S(1)}, u32[]{:S(2)}, u32[]{:S(2)}) %collective-permute-start.14) | collective-permute-done | bytes 639008 | tf_op jit(solution)/shard_map/ppermute | solution.py:30
  70.9 6.0 %shard_map.257 = (bf16[384,512]{1,0:T(8,128)(2,1)S(1)}, bf16[384,512]{1,0:T(8,128)(2,1)S(1)}, bf16[384,512]{1,0:T(8,128)(2,1)S(1)}, bf16[384,512]{1,0:T(8,128)(2...) custom-call(s32[3]{0:T(128)S(1)} %pad_add_fusion.1.scal, bf16[832,512]{1,0:T(8,128)(2,1)S(1)} %get-tuple-element.67.xn, ...), custom_call_target="tpu_custom_call" | custom-call | tf_op jit(solution)/shard_map/pallas_call | solution.py:92
  77.7 2.5 %collective-permute-done.15.gk_other = bf16[1,3,64,512]{3,2,1,0:T(8,128)(2,1)S(1)} collective-permute-done((bf16[1,3,64,512]{3,2,1,0:T(8,128)(2,1)S(1)}, bf16[1,3,64,512]{3,2,1,0:T(8,128)(2,1)S(1)}, u32[]{:S(2)}, u32[]{:S(2)}) %collective-permute-start.15) | collective-permute-done | bytes 196640 | tf_op jit(solution)/shard_map/ppermute | solution.py:30
  80.5 3.5 %shard_map.258 = (bf16[384,512]{1,0:T(8,128)(2,1)S(1)}, bf16[384,512]{1,0:T(8,128)(2,1)S(1)}, bf16[384,512]{1,0:T(8,128)(2,1)S(1)}, bf16[384,512]{1,0:T(8,128)(2...) custom-call(s32[3]{0:T(128)S(1)} %pad_add_fusion.1.scal, ...), custom_call_target="tpu_custom_call" | custom-call | tf_op jit(solution)/shard_map/pallas_call | solution.py:92
  84.3 1.9 %collective-permute-done.17.refs_1_ = bf16[208,1536]{1,0:T(8,128)(2,1)S(1)} collective-permute-done((bf16[208,1536]{1,0:T(8,128)(2,1)S(1)}, bf16[208,1536]{1,0:T(8,128)(2,1)S(1)}, u32[]{:S(2)}, u32[]{:S(2)}) %collective-permute-start.17) | collective-permute-done | bytes 639008 | tf_op jit(solution)/shard_map/ppermute | solution.py:30
  86.2 1.1 copy-done.11
  87.3 1.8 %shard_map.259 = (bf16[208,2304]{1,0:T(8,128)(2,1)S(1)}, bf16[208,1152]{1,0:T(8,128)(2,1)S(1)}, f32[208,1152]{1,0:T(8,128)S(1)}) custom-call(bf16[208,1536]{1,0:T(8,128)(2,1)S(1)} %get-tuple-element.87.refs_0_, bf16[208,1536]{1,0:T(8,128)(2,1)S(1)} %collective-permute-done.17.refs_1_, bf16[208,3072]{1,0:T(8,128)(2,1)S(1)} %copy-done.4, ...), custom_call_target="tpu_custom_call" | custom-call | tf_op jit(solution)/shard_map/pallas_call | solution.py:92
  89.1 1.5 collective-permute-start.26
  90.6 5.4 %shard_map.260 = (bf16[4,2,192,128]{3,2,1,0:T(8,128)(2,1)S(1)}, bf16[4,2,192,128]{3,2,1,0:T(8,128)(2,1)S(1)}, bf16[4,2,192,128]{3,2,1,0:T(8,128)(2,1)S(1)}, bf16[4,2,192,128]{3,2,1,0:T(8,128)(2,1)S(1)}) custom-call(s32[3]{0:T(128)S(1)} %pad_add_fusion.1.scal, bf16[208,768]{1,0:T(8,128)(2,1)S(1)} %pad_maximum_fusion.3.refs_0_, ...), custom_call_target="tpu_custom_call" | custom-call | tf_op jit(solution)/shard_map/pallas_call | solution.py:92
  96.0 1.3 collective-permute-start.19
  97.3 1.2 collective-permute-start.20
  98.7 6.7 %collective-permute-done.19.refs_1_ = bf16[4,2,192,128]{3,2,1,0:T(8,128)(2,1)S(1)} collective-permute-done((bf16[4,2,192,128]{3,2,1,0:T(8,128)(2,1)S(1)}, bf16[4,2,192,128]{3,2,1,0:T(8,128)(2,1)S(1)}, u32[]{:S(2)}, u32[]{:S(2)}) %collective-permute-start.19) | collective-permute-done | bytes 393248 | tf_op jit(solution)/shard_map/ppermute | solution.py:30
  105.5 0.9 collective-permute-done.20.refs_2_
  106.4 8.5 %collective-permute-done.21.refs_3_ = bf16[4,2,192,128]{3,2,1,0:T(8,128)(2,1)S(1)} collective-permute-done((bf16[4,2,192,128]{3,2,1,0:T(8,128)(2,1)S(1)}, bf16[4,2,192,128]{3,2,1,0:T(8,128)(2,1)S(1)}, u32[]{:S(2)}, u32[]{:S(2)}) %collective-permute-start.21) | collective-permute-done | bytes 393248 | tf_op jit(solution)/shard_map/ppermute | solution.py:30
  114.9 1.1 shard_map.261
  116.0 3.8 %collective-permute-start.22 = (bf16[2,192,128]{2,1,0:T(8,128)(2,1)S(1)}, bf16[2,192,128]{2,1,0:T(8,128)(2,1)S(1)}, u32[]{:S(2)}, u32[]{:S(2)}) collective-permute-start(bf16[2,192,128]{2,1,0:T(8,128)(2,1)S(1)} %get-tuple-element.103), channel_id=1, source_target_pairs={{17,0},{16,1},{1,2},{0,3},{19,16},{18,17},{3,18},{2,19},{21,4},{20... | collective-permute-start | bytes 294920 | tf_op jit(solution)/shard_map/ppermute | solution.py:586
  119.8 1.0 collective-permute-start.23
  121.1 6.7 %collective-permute-start.25 = (bf16[2,192,128]{2,1,0:T(8,128)(2,1)S(1)}, bf16[2,192,128]{2,1,0:T(8,128)(2,1)}, u32[]{:S(2)}, u32[]{:S(2)}) collective-permute-start(bf16[2,192,128]{2,1,0:T(8,128)(2,1)S(1)} %get-tuple-element.106), channel_id=1, source_target_pairs={{0,0},{1,1},{16,2},{17,3},{2,16},{3,17},{18,18},{19,19},{4,4},{5,5... | collective-permute-start | bytes 294920 | tf_op jit(solution)/shard_map/ppermute | solution.py:586
  127.7 9.7 %collective-permute-done.26.near = bf16[208,2304]{1,0:T(8,128)(2,1)S(1)} collective-permute-done((bf16[208,2304]{1,0:T(8,128)(2,1)S(1)}, bf16[208,2304]{1,0:T(8,128)(2,1)S(1)}, u32[]{:S(2)}, u32[]{:S(2)}) %collective-permute-start.26) | collective-permute-done | bytes 958496 | tf_op jit(solution)/shard_map/ppermute | solution.py:38
  138.1 3.5 %collective-permute-done.23 = bf16[2,192,128]{2,1,0:T(8,128)(2,1)S(1)} collective-permute-done((bf16[2,192,128]{2,1,0:T(8,128)(2,1)S(1)}, bf16[2,192,128]{2,1,0:T(8,128)(2,1)S(1)}, u32[]{:S(2)}, u32[]{:S(2)}) %collective-permute-start.23) | collective-permute-done | bytes 98336 | tf_op jit(solution)/shard_map/ppermute | solution.py:586
  142.0 1.0 broadcast_select_fusion.15
  143.2 0.8 convert_add_fusion
  144.0 2.7 %shard_map.263 = (f32[3,3,192,64]{3,2,1,0:T(8,128)S(1)}, f32[3,192,64]{2,1,0:T(8,128)S(1)}, f32[192,768]{1,0:T(8,128)}, f32[192,768]{1,0:T(8,128)}, f32[2,288]{1...) custom-call(s32[3]{0:T(128)S(1)} %pad_add_fusion.1.scal, bf16[208,2304]{1,0:T(8,128)(2,1)S(1)} %shard_map.262.here, ...), custom_call_target="tpu_custom_call" | custom-call | tf_op jit(solution)/shard_map/pallas_call | solution.py:92
  148.1 1.0 copy.114
  149.1 1.3 collective-permute-start.29
  150.3 1.2 collective-permute-start.30
  151.8 1.2 collective-permute-done.30
  153.0 2.0 %collective-permute-done.31 = f32[5,192]{1,0:T(8,128)S(1)} collective-permute-done((f32[5,192]{1,0:T(8,128)S(1)}, f32[5,192]{1,0:T(8,128)S(1)}, u32[]{:S(2)}, u32[]{:S(2)}) %collective-permute-start.31) | collective-permute-done | bytes 3872 | tf_op jit(solution)/shard_map/ppermute | solution.py:30
  155.6 2.1 %copy.116 = f32[192,2,256]{2,1,0:T(2,128)} copy(f32[192,2,256]{2,0,1:T(8,128)} %get-tuple-element.199) | data formatting | bytes 786432
  157.7 1.8 %copy.115 = bf16[192,2,256]{2,1,0:T(2,128)(2,1)} copy(bf16[192,2,256]{2,0,1:T(8,128)(2,1)} %get-tuple-element.200) | data formatting | bytes 393216
  159.5 1.2 reshape.440
  160.7 0.8 reshape.443
  (178 shorter events, 14.6 us)
Async XLA Ops:
  0.6 9.8 %copy-start.17 = (s32[2,1024]{1,0:T(2,128)S(1)}, s32[2,1024]{1,0:T(2,128)}, u32[]{:S(2)}) copy-start(s32[2,1024]{1,0:T(2,128)} %param.16) | copy-start | bytes 24580
  0.7 10.1 %copy-start.23 = (bf16[192]{0:T(256)(128)(2,1)S(1)}, bf16[192]{0:T(256)(128)(2,1)}, u32[]{:S(2)}) copy-start(bf16[192]{0:T(256)(128)(2,1)} %param.23) | copy-start | bytes 1156
  0.7 10.1 %copy-start.24 = (bf16[192]{0:T(256)(128)(2,1)S(1)}, bf16[192]{0:T(256)(128)(2,1)}, u32[]{:S(2)}) copy-start(bf16[192]{0:T(256)(128)(2,1)} %param.24) | copy-start | bytes 1156
  0.7 10.1 %copy-start.19 = (bf16[768]{0:T(1024)(128)(2,1)S(1)}, bf16[768]{0:T(1024)(128)(2,1)}, u32[]{:S(2)}) copy-start(bf16[768]{0:T(1024)(128)(2,1)} %param.26) | copy-start | bytes 4612
  0.7 10.1 %copy-start.5 = (bf16[192,768]{1,0:T(8,128)(2,1)S(1)}, bf16[192,768]{1,0:T(8,128)(2,1)}, u32[]{:S(2)}) copy-start(bf16[192,768]{1,0:T(8,128)(2,1)} %win_ref.1) | copy-start | bytes 884740
  1.8 9.3 %copy-start.14 = (bf16[192,768]{1,0:T(8,128)(2,1)S(1)}, bf16[192,768]{1,0:T(8,128)(2,1)}, u32[]{:S(2)}) copy-start(bf16[192,768]{1,0:T(8,128)(2,1)} %param.27) | copy-start | bytes 884740
  1.8 9.3 %copy-start.15 = (bf16[3,3,12288]{2,1,0:T(4,128)(2,1)S(1)}, bf16[3,3,12288]{2,1,0:T(4,128)(2,1)}, u32[]{:S(2)}) copy-start(bf16[3,3,12288]{2,1,0:T(4,128)(2,1)} %param.17) | copy-start | bytes 663556
  2.6 15.4 %collective-permute-start.2 = (bf16[2,192,128]{2,1,0:T(8,128)(2,1)}, bf16[2,192,128]{2,1,0:T(8,128)(2,1)S(1)}, u32[]{:S(2)}, u32[]{:S(2)}) collective-permute-start(bf16[2,192,128]{2,1,0:T(8,128)(2,1)} %get-tuple-element.212), channel_id=1, source_target_pairs={{0,16},{1,17},{2,0},{3,1},{16,18},{17,19},{18,2},{19,3},{4,20},{5,... | collective-permute-start | bytes 294920 | tf_op jit(solution)/shard_map/ppermute | solution.py:434
  5.8 12.4 %collective-permute-start.3 = (bf16[2,192,128]{2,1,0:T(8,128)(2,1)}, bf16[2,192,128]{2,1,0:T(8,128)(2,1)S(1)}, u32[]{:S(2)}, u32[]{:S(2)}) collective-permute-start(bf16[2,192,128]{2,1,0:T(8,128)(2,1)} %get-tuple-element.213), channel_id=1, source_target_pairs={{0,17},{1,16},{2,1},{3,0},{16,19},{17,18},{18,3},{19,2},{4,21},{5,... | collective-permute-start | bytes 294920 | tf_op jit(solution)/shard_map/ppermute | solution.py:434
  7.5 10.7 %collective-permute-start.1 = (bf16[2,192,128]{2,1,0:T(8,128)(2,1)S(1)}, bf16[2,192,128]{2,1,0:T(8,128)(2,1)S(1)}, u32[]{:S(2)}, u32[]{:S(2)}) collective-permute-start(bf16[2,192,128]{2,1,0:T(8,128)(2,1)S(1)} %get-tuple-element.211), channel_id=1, source_target_pairs={{0,1},{1,0},{2,17},{3,16},{16,3},{17,2},{18,19},{19,18},{4,5},{5,4... | collective-permute-start | bytes 294920 | tf_op jit(solution)/shard_map/ppermute | solution.py:434
  7.7 10.5 %collective-permute-start = (bf16[2,192,128]{2,1,0:T(8,128)(2,1)S(1)}, bf16[2,192,128]{2,1,0:T(8,128)(2,1)S(1)}, u32[]{:S(2)}, u32[]{:S(2)}) collective-permute-start(bf16[2,192,128]{2,1,0:T(8,128)(2,1)S(1)} %get-tuple-element.194), channel_id=1, source_target_pairs={{0,0},{1,1},{2,16},{3,17},{16,2},{17,3},{18,18},{19,19},{4,4},{5,5... | collective-permute-start | bytes 294920 | tf_op jit(solution)/shard_map/ppermute | solution.py:434
  10.6 4.6 %collective-permute-start.4 = (f32[2,2]{0,1:T(2,128)S(1)}, f32[2,2]{0,1:T(2,128)S(1)}, u32[]{:S(2)}, u32[]{:S(2)}) collective-permute-start(f32[2,2]{0,1:T(2,128)S(1)} %add_convert_fusion), channel_id=1, source_target_pairs={{0,16},{16,0},{1,17},{17,1},{2,18},{18,2},{3,19},{19,3},{4,20},{20... | collective-permute-start | bytes 56 | tf_op jit(solution)/shard_map/ppermute | solution.py:30
  15.2 55.8 %copy-start.1 = (bf16[208,1536]{1,0:T(8,128)(2,1)}, bf16[208,1536]{1,0:T(8,128)(2,1)S(1)}, u32[]{:S(2)}) copy-start(bf16[208,1536]{1,0:T(8,128)(2,1)S(1)} %pad_maximum_fusion.refs_0_.refs_5_) | copy-start | bytes 1916932
  15.3 19.2 %collective-permute-start.7 = (bf16[208,1152]{1,0:T(8,128)(2,1)S(1)}, bf16[208,1152]{1,0:T(8,128)(2,1)S(1)}, u32[]{:S(2)}, u32[]{:S(2)}) collective-permute-start(bf16[208,1152]{1,0:T(8,128)(2,1)S(1)} %pad_maximum_fusion.1), channel_id=1, source_target_pairs={{0,1},{1,0},{2,3},{3,2},{4,5},{5,4},{6,7},{7,6},{8,9},{9,8},{10,11... | collective-permute-start | bytes 1437704 | tf_op jit(solution)/shard_map/ppermute | solution.py:30
  18.1 19.8 %collective-permute-start.5 = (bf16[208,768]{1,0:T(8,128)(2,1)S(1)}, bf16[208,768]{1,0:T(8,128)(2,1)S(1)}, u32[]{:S(2)}, u32[]{:S(2)}) collective-permute-start(bf16[208,768]{1,0:T(8,128)(2,1)S(1)} %pad_maximum_fusion.3.refs_0_), channel_id=1, source_target_pairs={{0,3},{1,2},{2,1},{3,0},{16,18},{17,19},{18,16},{19,17},{4,7},{5,6... | collective-permute-start | bytes 958472 | tf_op jit(solution)/shard_map/ppermute | solution.py:38
  18.3 19.7 %collective-permute-start.10 = (bf16[4,2,192,128]{3,2,1,0:T(8,128)(2,1)S(1)}, bf16[4,2,192,128]{3,2,1,0:T(8,128)(2,1)S(1)}, u32[]{:S(2)}, u32[]{:S(2)}) collective-permute-start(bf16[4,2,192,128]{3,2,1,0:T(8,128)(2,1)S(1)} %pad_maximum_fusion.2.refs_0_.x_ref), channel_id=1, source_target_pairs={{0,8},{4,12},{8,0},{12,4},{1,9},{5,13},{9,1},{13,5},{2,10},{6,14},... | collective-permute-start | bytes 1179656 | tf_op jit(solution)/shard_map/ppermute | solution.py:30
  19.6 18.4 %collective-permute-start.11 = (bf16[4,2,192,128]{3,2,1,0:T(8,128)(2,1)S(1)}, bf16[4,2,192,128]{3,2,1,0:T(8,128)(2,1)S(1)}, u32[]{:S(2)}, u32[]{:S(2)}) collective-permute-start(bf16[4,2,192,128]{3,2,1,0:T(8,128)(2,1)S(1)} %pad_maximum_fusion.2.refs_0_.x_ref), channel_id=1, source_target_pairs={{0,12},{4,8},{8,4},{12,0},{1,13},{5,9},{9,5},{13,1},{2,14},{6,10},... | collective-permute-start | bytes 1179656 | tf_op jit(solution)/shard_map/ppermute | solution.py:30
  20.7 17.3 %collective-permute-start.9 = (bf16[4,2,192,128]{3,2,1,0:T(8,128)(2,1)S(1)}, bf16[4,2,192,128]{3,2,1,0:T(8,128)(2,1)S(1)}, u32[]{:S(2)}, u32[]{:S(2)}) collective-permute-start(bf16[4,2,192,128]{3,2,1,0:T(8,128)(2,1)S(1)} %pad_maximum_fusion.2.refs_0_.x_ref), channel_id=1, source_target_pairs={{0,4},{4,0},{8,12},{12,8},{1,5},{5,1},{9,13},{13,9},{2,6},{6,2},{1... | collective-permute-start | bytes 1179656 | tf_op jit(solution)/shard_map/ppermute | solution.py:30
  34.5 8.1 %collective-permute-start.8 = (bf16[208,1152]{1,0:T(8,128)(2,1)S(1)}, bf16[208,1152]{1,0:T(8,128)(2,1)S(1)}, u32[]{:S(2)}, u32[]{:S(2)}) collective-permute-start(bf16[208,1152]{1,0:T(8,128)(2,1)S(1)} %collective-permute-done.7), channel_id=1, source_target_pairs={{0,16},{16,0},{1,17},{17,1},{2,18},{18,2},{3,19},{19,3},{4,20},{20... | collective-permute-start | bytes 1437704 | tf_op jit(solution)/shard_map/ppermute | solution.py:30
  37.9 4.7 %collective-permute-start.6 = (bf16[208,768]{1,0:T(8,128)(2,1)S(1)}, bf16[208,768]{1,0:T(8,128)(2,1)S(1)}, u32[]{:S(2)}, u32[]{:S(2)}) collective-permute-start(bf16[208,768]{1,0:T(8,128)(2,1)S(1)} %collective-permute-done.5.refs_1_), channel_id=1, source_target_pairs={{0,16},{16,0},{1,17},{17,1},{2,18},{18,2},{3,19},{19,3},{4,20},{20... | collective-permute-start | bytes 958472 | tf_op jit(solution)/shard_map/ppermute | solution.py:30
  38.0 30.8 %collective-permute-start.12 = (bf16[208,1536]{1,0:T(8,128)(2,1)S(1)}, bf16[208,1536]{1,0:T(8,128)(2,1)S(1)}, u32[]{:S(2)}, u32[]{:S(2)}) collective-permute-start(bf16[208,1536]{1,0:T(8,128)(2,1)S(1)} %pad_maximum_fusion.refs_0_.refs_5_), channel_id=1, source_target_pairs={{0,3},{1,2},{2,1},{3,0},{16,18},{17,19},{18,16},{19,17},{4,7},{5,6... | collective-permute-start | bytes 1916936 | tf_op jit(solution)/shard_map/ppermute | solution.py:38
  42.6 28.3 %copy-start = (bf16[832,512]{1,0:T(8,128)(2,1)}, bf16[832,512]{1,0:T(8,128)(2,1)S(1)}, u32[]{:S(2)}) copy-start(bf16[832,512]{1,0:T(8,128)(2,1)S(1)} %get-tuple-element.68.cot) | copy-start | bytes 2555908
  44.5 2.1 %collective-permute-start.13 = (bf16[2,3,64,512]{3,2,1,0:T(8,128)(2,1)S(1)}, bf16[2,3,64,512]{3,2,1,0:T(8,128)(2,1)S(1)}, u32[]{:S(2)}, u32[]{:S(2)}) collective-permute-start(bf16[2,3,64,512]{3,2,1,0:T(8,128)(2,1)S(1)} %get-tuple-element.70.kv_ref), channel_id=1, source_target_pairs={{0,16},{16,0},{1,17},{17,1},{2,18},{18,2},{3,19},{19,3},{4,20},{20... | collective-permute-start | bytes 1179656 | tf_op jit(solution)/shard_map/ppermute | solution.py:30
  68.8 8.1 %copy-start.2 = (bf16[208,1536]{1,0:T(8,128)(2,1)}, bf16[208,1536]{1,0:T(8,128)(2,1)S(1)}, u32[]{:S(2)}) copy-start(bf16[208,1536]{1,0:T(8,128)(2,1)S(1)} %collective-permute-done.12.refs_1_.refs_6_) | copy-start | bytes 1916932
  68.8 2.1 %collective-permute-start.14 = (bf16[208,1536]{1,0:T(8,128)(2,1)S(1)}, bf16[208,1536]{1,0:T(8,128)(2,1)S(1)}, u32[]{:S(2)}, u32[]{:S(2)}) collective-permute-start(bf16[208,1536]{1,0:T(8,128)(2,1)S(1)} %collective-permute-done.12.refs_1_.refs_6_), channel_id=1, source_target_pairs={{0,16},{16,0},{1,17},{17,1},{2,18},{18,2},{3,19},{19,3},{4,20},{20... | collective-permute-start | bytes 1916936 | tf_op jit(solution)/shard_map/ppermute | solution.py:30
  76.9 7.2 %copy-start.6 = (bf16[384,512]{1,0:T(8,128)(2,1)}, bf16[384,512]{1,0:T(8,128)(2,1)S(1)}, u32[]{:S(2)}) copy-start(bf16[384,512]{1,0:T(8,128)(2,1)S(1)} %get-tuple-element.97.refs_16_) | copy-start | bytes 1179652
  76.9 7.2 %copy-start.7 = (bf16[384,512]{1,0:T(8,128)(2,1)}, bf16[384,512]{1,0:T(8,128)(2,1)S(1)}, u32[]{:S(2)}) copy-start(bf16[384,512]{1,0:T(8,128)(2,1)S(1)} %get-tuple-element.98.refs_17_) | copy-start | bytes 1179652
  76.9 9.3 %collective-permute-start.18 = (bf16[208,3072]{1,0:T(8,128)(2,1)}, bf16[208,3072]{1,0:T(8,128)(2,1)S(1)}, u32[]{:S(2)}, u32[]{:S(2)}) collective-permute-start(bf16[208,3072]{1,0:T(8,128)(2,1)} %get-tuple-element.89), channel_id=1, source_target_pairs={{0,16},{16,0},{1,17},{17,1},{2,18},{18,2},{3,19},{19,3},{4,20},{20... | collective-permute-start | bytes 3833864 | tf_op jit(solution)/shard_map/ppermute | solution.py:30
  77.2 3.1 %collective-permute-start.15 = (bf16[1,3,64,512]{3,2,1,0:T(8,128)(2,1)S(1)}, bf16[1,3,64,512]{3,2,1,0:T(8,128)(2,1)S(1)}, u32[]{:S(2)}, u32[]{:S(2)}) collective-permute-start(bf16[1,3,64,512]{3,2,1,0:T(8,128)(2,1)S(1)} %get-tuple-element.210), channel_id=1, source_target_pairs={{0,16},{16,0},{1,17},{17,1},{2,18},{18,2},{3,19},{19,3},{4,20},{20... | collective-permute-start | bytes 589832 | tf_op jit(solution)/shard_map/ppermute | solution.py:30
  77.6 2.9 %collective-permute-start.16 = (bf16[1,3,64,512]{3,2,1,0:T(8,128)(2,1)S(1)}, bf16[1,3,64,512]{3,2,1,0:T(8,128)(2,1)S(1)}, u32[]{:S(2)}, u32[]{:S(2)}) collective-permute-start(bf16[1,3,64,512]{3,2,1,0:T(8,128)(2,1)S(1)} %get-tuple-element.209), channel_id=1, source_target_pairs={{0,16},{16,0},{1,17},{17,1},{2,18},{18,2},{3,19},{19,3},{4,20},{20... | collective-permute-start | bytes 589832 | tf_op jit(solution)/shard_map/ppermute | solution.py:30
  80.5 6.7 %copy-start.4 = (bf16[208,3072]{1,0:T(8,128)(2,1)S(1)}, bf16[208,3072]{1,0:T(8,128)(2,1)}, u32[]{:S(2)}) copy-start(bf16[208,3072]{1,0:T(8,128)(2,1)} %get-tuple-element.77.refs_2_) | copy-start | bytes 3833860
  84.1 2.1 %collective-permute-start.17 = (bf16[208,1536]{1,0:T(8,128)(2,1)S(1)}, bf16[208,1536]{1,0:T(8,128)(2,1)S(1)}, u32[]{:S(2)}, u32[]{:S(2)}) collective-permute-start(bf16[208,1536]{1,0:T(8,128)(2,1)S(1)} %get-tuple-element.88), channel_id=1, source_target_pairs={{0,16},{16,0},{1,17},{17,1},{2,18},{18,2},{3,19},{19,3},{4,20},{20... | collective-permute-start | bytes 1916936 | tf_op jit(solution)/shard_map/ppermute | solution.py:30
  89.1 48.4 %collective-permute-start.26 = (bf16[208,2304]{1,0:T(8,128)(2,1)S(1)}, bf16[208,2304]{1,0:T(8,128)(2,1)S(1)}, u32[]{:S(2)}, u32[]{:S(2)}) collective-permute-start(bf16[208,2304]{1,0:T(8,128)(2,1)S(1)} %get-tuple-element.90), channel_id=1, source_target_pairs={{0,3},{1,2},{2,1},{3,0},{16,18},{17,19},{18,16},{19,17},{4,7},{5,6... | collective-permute-start | bytes 2875400 | tf_op jit(solution)/shard_map/ppermute | solution.py:38
  90.5 30.5 %collective-permute-start.27 = (bf16[208,1152]{1,0:T(8,128)(2,1)S(1)}, bf16[208,1152]{1,0:T(8,128)(2,1)S(1)}, u32[]{:S(2)}, u32[]{:S(2)}) collective-permute-start(bf16[208,1152]{1,0:T(8,128)(2,1)S(1)} %get-tuple-element.107), channel_id=1, source_target_pairs={{0,1},{1,0},{2,3},{3,2},{4,5},{5,4},{6,7},{7,6},{8,9},{9,8},{10,11... | collective-permute-start | bytes 1437704 | tf_op jit(solution)/shard_map/ppermute | solution.py:30
  90.5 8.2 %copy-start.21 = (bf16[192]{0:T(256)(128)(2,1)S(1)}, bf16[192]{0:T(256)(128)(2,1)}, u32[]{:S(2)}) copy-start(bf16[192]{0:T(256)(128)(2,1)} %param.28) | copy-start | bytes 1156
  90.6 8.2 %copy-start.22 = (bf16[192]{0:T(256)(128)(2,1)S(1)}, bf16[192]{0:T(256)(128)(2,1)}, u32[]{:S(2)}) copy-start(bf16[192]{0:T(256)(128)(2,1)} %param.20) | copy-start | bytes 1156
  96.0 9.5 %collective-permute-start.19 = (bf16[4,2,192,128]{3,2,1,0:T(8,128)(2,1)S(1)}, bf16[4,2,192,128]{3,2,1,0:T(8,128)(2,1)S(1)}, u32[]{:S(2)}, u32[]{:S(2)}) collective-permute-start(bf16[4,2,192,128]{3,2,1,0:T(8,128)(2,1)S(1)} %get-tuple-element.100), channel_id=1, source_target_pairs={{0,4},{4,0},{8,12},{12,8},{1,5},{5,1},{9,13},{13,9},{2,6},{6,2},{1... | collective-permute-start | bytes 1179656 | tf_op jit(solution)/shard_map/ppermute | solution.py:30
  97.3 9.1 %collective-permute-start.20 = (bf16[4,2,192,128]{3,2,1,0:T(8,128)(2,1)S(1)}, bf16[4,2,192,128]{3,2,1,0:T(8,128)(2,1)S(1)}, u32[]{:S(2)}, u32[]{:S(2)}) collective-permute-start(bf16[4,2,192,128]{3,2,1,0:T(8,128)(2,1)S(1)} %get-tuple-element.101), channel_id=1, source_target_pairs={{0,8},{4,12},{8,0},{12,4},{1,9},{5,13},{9,1},{13,5},{2,10},{6,14},... | collective-permute-start | bytes 1179656 | tf_op jit(solution)/shard_map/ppermute | solution.py:30
  98.5 16.4 %collective-permute-start.21 = (bf16[4,2,192,128]{3,2,1,0:T(8,128)(2,1)S(1)}, bf16[4,2,192,128]{3,2,1,0:T(8,128)(2,1)S(1)}, u32[]{:S(2)}, u32[]{:S(2)}) collective-permute-start(bf16[4,2,192,128]{3,2,1,0:T(8,128)(2,1)S(1)} %get-tuple-element.102), channel_id=1, source_target_pairs={{0,12},{4,8},{8,4},{12,0},{1,13},{5,9},{9,5},{13,1},{2,14},{6,10},... | collective-permute-start | bytes 1179656 | tf_op jit(solution)/shard_map/ppermute | solution.py:30
  116.0 22.1 %collective-permute-start.22 = (bf16[2,192,128]{2,1,0:T(8,128)(2,1)S(1)}, bf16[2,192,128]{2,1,0:T(8,128)(2,1)S(1)}, u32[]{:S(2)}, u32[]{:S(2)}) collective-permute-start(bf16[2,192,128]{2,1,0:T(8,128)(2,1)S(1)} %get-tuple-element.103), channel_id=1, source_target_pairs={{17,0},{16,1},{1,2},{0,3},{19,16},{18,17},{3,18},{2,19},{21,4},{20... | collective-permute-start | bytes 294920 | tf_op jit(solution)/shard_map/ppermute | solution.py:586
  119.8 21.9 %collective-permute-start.23 = (bf16[2,192,128]{2,1,0:T(8,128)(2,1)S(1)}, bf16[2,192,128]{2,1,0:T(8,128)(2,1)S(1)}, u32[]{:S(2)}, u32[]{:S(2)}) collective-permute-start(bf16[2,192,128]{2,1,0:T(8,128)(2,1)S(1)} %get-tuple-element.104), channel_id=1, source_target_pairs={{16,0},{17,1},{0,2},{1,3},{18,16},{19,17},{2,18},{3,19},{20,4},{21... | collective-permute-start | bytes 294920 | tf_op jit(solution)/shard_map/ppermute | solution.py:586
  120.8 20.8 %collective-permute-start.24 = (bf16[2,192,128]{2,1,0:T(8,128)(2,1)S(1)}, bf16[2,192,128]{2,1,0:T(8,128)(2,1)}, u32[]{:S(2)}, u32[]{:S(2)}) collective-permute-start(bf16[2,192,128]{2,1,0:T(8,128)(2,1)S(1)} %get-tuple-element.105), channel_id=1, source_target_pairs={{1,0},{0,1},{17,2},{16,3},{3,16},{2,17},{19,18},{18,19},{5,4},{4,5... | collective-permute-start | bytes 294920 | tf_op jit(solution)/shard_map/ppermute | solution.py:586
  121.1 21.0 %collective-permute-start.25 = (bf16[2,192,128]{2,1,0:T(8,128)(2,1)S(1)}, bf16[2,192,128]{2,1,0:T(8,128)(2,1)}, u32[]{:S(2)}, u32[]{:S(2)}) collective-permute-start(bf16[2,192,128]{2,1,0:T(8,128)(2,1)S(1)} %get-tuple-element.106), channel_id=1, source_target_pairs={{0,0},{1,1},{16,2},{17,3},{2,16},{3,17},{18,18},{19,19},{4,4},{5,5... | collective-permute-start | bytes 294920 | tf_op jit(solution)/shard_map/ppermute | solution.py:586
  137.7 6.3 %collective-permute-start.28 = (bf16[208,2304]{1,0:T(8,128)(2,1)S(1)}, bf16[208,2304]{1,0:T(8,128)(2,1)S(1)}, u32[]{:S(2)}, u32[]{:S(2)}) collective-permute-start(bf16[208,2304]{1,0:T(8,128)(2,1)S(1)} %shard_map.262.here), channel_id=1, source_target_pairs={{0,16},{16,0},{1,17},{17,1},{2,18},{18,2},{3,19},{19,3},{4,20},{20... | collective-permute-start | bytes 2875400 | tf_op jit(solution)/shard_map/ppermute | solution.py:30
  149.1 2.7 %collective-permute-start.29 = (f32[5,192]{1,0:T(8,128)S(1)}, f32[5,192]{1,0:T(8,128)S(1)}, u32[]{:S(2)}, u32[]{:S(2)}) collective-permute-start(f32[5,192]{1,0:T(8,128)S(1)} %pad_maximum_fusion.10), channel_id=1, source_target_pairs={{0,4},{4,0},{8,12},{12,8},{1,5},{5,1},{9,13},{13,9},{2,6},{6,2},{1... | collective-permute-start | bytes 11528 | tf_op jit(solution)/shard_map/ppermute | solution.py:30
  150.3 2.6 %collective-permute-start.30 = (f32[5,192]{1,0:T(8,128)S(1)}, f32[5,192]{1,0:T(8,128)S(1)}, u32[]{:S(2)}, u32[]{:S(2)}) collective-permute-start(f32[5,192]{1,0:T(8,128)S(1)} %pad_maximum_fusion.10), channel_id=1, source_target_pairs={{0,8},{4,12},{8,0},{12,4},{1,9},{5,13},{9,1},{13,5},{2,10},{6,14},... | collective-permute-start | bytes 11528 | tf_op jit(solution)/shard_map/ppermute | solution.py:30
  151.6 3.4 %collective-permute-start.31 = (f32[5,192]{1,0:T(8,128)S(1)}, f32[5,192]{1,0:T(8,128)S(1)}, u32[]{:S(2)}, u32[]{:S(2)}) collective-permute-start(f32[5,192]{1,0:T(8,128)S(1)} %pad_maximum_fusion.10), channel_id=1, source_target_pairs={{0,12},{4,8},{8,4},{12,0},{1,13},{5,9},{9,5},{13,1},{2,14},{6,10},... | collective-permute-start | bytes 11528 | tf_op jit(solution)/shard_map/ppermute | solution.py:30
  155.6 7.3 %collective-permute-start.32 = (f32[192]{0:T(256)S(1)}, f32[192]{0:T(256)S(1)}, u32[]{:S(2)}, u32[]{:S(2)}) collective-permute-start(f32[192]{0:T(256)S(1)} %bitcast.94), channel_id=1, source_target_pairs={{0,16},{16,0},{1,17},{17,1},{2,18},{18,2},{3,19},{19,3},{4,20},{20... | collective-permute-start | bytes 2312 | tf_op jit(solution)/shard_map/ppermute | solution.py:622
  (12 other events, 28.6 us)

commit v3 on v2

--- a/solution.py
+++ b/solution.py
@@ -84,7 +84,7 @@
     return jnp.concatenate([columns.astype(bf16), rows], axis=0)
 
 
-def call(kernel, outs, args, scalars=None):
+def call(kernel, outs, args, scalars=None, cost=0):
     specs = [pl.BlockSpec(memory_space=pltpu.VMEM) for _ in args]
     if scalars is not None:
         specs = [pl.BlockSpec(memory_space=pltpu.SMEM)] + specs
@@ -95,7 +95,7 @@
         in_specs=specs,
         out_specs=[pl.BlockSpec(memory_space=pltpu.VMEM) for _ in outs],
         compiler_params=pltpu.CompilerParams(vmem_limit_bytes=48 * 2**20),
-        cost_estimate=pl.CostEstimate(flops=0, bytes_accessed=0, transcendentals=0),
+        cost_estimate=pl.CostEstimate(flops=cost, bytes_accessed=0, transcendentals=0),
     )(*args)
 
 
@@ -143,12 +143,9 @@
 
 
 def weight(parts, i, u):
-    own, near, near_other, far, far_other = parts
-    if i == 3:
-        return (far, far_other)[u][...]
-    half = far.shape[1]
+    half = parts[i].shape[1] // 2
     side = 1 - u if i == 2 else u
-    return (own, near, near_other)[i][:, side * half : (side + 1) * half]
+    return parts[i][:, side * half : (side + 1) * half]
 
 
 def blocks_of(core, size):
@@ -156,7 +153,7 @@
 
 
 def qkv_kernel(heads, scal, tables, xn, cot, *refs):
-    weights, (q_ref, kv_ref, ga_ref) = refs[:5], refs[5:]
+    weights, (q_ref, kv_ref, ga_ref) = refs[:4], refs[4:]
     sub = HD // 2
     at_blocks = blocks_of(scal[1], weights[0].shape[0])
     third = heads * sub
@@ -177,15 +174,21 @@
             ga_ref[h, dims, :] = grad[at : at + sub].astype(bf16)
 
 
-def put_sums(keep, give, i, u, value):
+def put_sums(refs, i, u, value):
+    own, keep, give, far = refs
     half = value.shape[1]
-    if i == 1:
-        keep[:, u * half : (u + 1) * half] = value
-    elif i == 2:
-        give[:, (1 - u) * half : (2 - u) * half] = value
-    else:
-        at = (2 if i == 3 else 3) * half
-        (keep, give)[u][:, at : at + half] = value
+    side = 1 - u if i == 2 else u
+    (own, keep, give, far)[i][:, side * half : (side + 1) * half] = value.astype(own.dtype if i == 0 else bf16)
+
+
+def rows_at(first, *rows):
+    at = lax.broadcasted_iota(jnp.int32, (PAD, rows[0].shape[1]), 0)
+    return sum(jnp.where(at == first + i, row, 0.0) for i, row in enumerate(rows))
+
+
+def add_below(ref, rows):
+    size = rows.shape[1]
+    ref[-PAD:, :size] = (ref[-PAD:, :size].astype(f32) + rows).astype(ref.dtype)
 
 
 def swapped(x):
@@ -194,7 +197,7 @@
 
 
 def attention_kernel(
-    span, scal, start, q_ref, kv_ref, kv_other, ga_ref, att_ref, gq_ref, gkv_ref, gkv_other, kc, vc, gk, gv
+    span, scal, start, q_ref, kv_ref, k_other, v_other, ga_ref, att_ref, gq_ref, gkv_ref, gkv_other, kc, vc, gk, gv
 ):
     count = q_ref.shape[2]
     rows = 2 * count // span
@@ -202,9 +205,9 @@
     core = scal[1]
     for rr in range(rows):
         mine, lanes = slice(rr * half, (rr + 1) * half), rr * span
-        for ref, at in ((kc, 0), (vc, 1)):
+        for at, ref, other in ((0, kc, k_other), (1, vc, v_other)):
             ref[:, lanes : lanes + half] = kv_ref[at, 0, :, mine]
-            ref[:, lanes + half : lanes + span] = swapped(kv_other[at, 0, :, mine])
+            ref[:, lanes + half : lanes + span] = swapped(other[0, 0, :, mine])
     kt, vt = kc[...].T, vc[...].T
     gk[...] = jnp.zeros_like(gk)
     gv[...] = jnp.zeros_like(gv)
@@ -238,11 +241,11 @@
             gkv_other[at, 0, :, mine] = ref[:, lanes + half : lanes + span].astype(bf16)
 
 
-def qkv_grad_kernel(heads, scal, tables, gq_ref, gkv_ref, gk_other, gv_other, att_ref, xn, cot, *outs):
+def qkv_grad_kernel(heads, scal, tables, gq_ref, gkv_ref, gk_other, gv_other, att_ref, xn, cot, *refs):
     sub = HD // 2
     third = heads * sub
-    keep, give = outs[4:]
-    at_blocks = blocks_of(scal[1], keep.shape[0])
+    outs, sums = refs[:4], refs[4:]
+    at_blocks = blocks_of(scal[1], sums[0].shape[0])
     zeros = jnp.zeros((third, xn.shape[1]), bf16)
     for u in range(2):
         grads_ref, att_out = outs[2 * u : 2 * u + 2]
@@ -265,11 +268,11 @@
             att_out[s * third : (s + 1) * third, :] = zeros
         for i in range(4):
             total = dot11(xn[at_blocks[i], :], grads_ref[...]) + dot11(cot[at_blocks[i], :], att_out[...])
-            put_sums(keep, give, i, u, total.astype(bf16))
+            put_sums(sums, i, u, total)
 
 
 def feed_kernel(scal, xn, cot, *refs):
-    weights, acts, (keep, give) = refs[:5], refs[5:9], refs[9:]
+    weights, acts, sums = refs[:4], refs[4:8], refs[8:]
     at_blocks = blocks_of(scal[1], weights[0].shape[0])
     part = acts[0].shape[0]
     for u in range(2):
@@ -282,18 +285,12 @@
         grad = sum(dot00(w[i][:, part:], cot[at_blocks[i], :]) for i in range(4))
         grad_ref[...] = (grad * slope).astype(bf16)
         for i in range(4):
-            total = jnp.concatenate(
-                [
-                    dot11(xn[at_blocks[i], :], grad_ref[...]).astype(bf16),
-                    dot11(cot[at_blocks[i], :], up_ref[...]).astype(bf16),
-                ],
-                axis=1,
-            )
-            put_sums(keep, give, i, u, total)
+            total = [dot11(xn[at_blocks[i], :], grad_ref[...]), dot11(cot[at_blocks[i], :], up_ref[...])]
+            put_sums(sums, i, u, jnp.concatenate(total, axis=1))
 
 
 def back_kernel(scal, *refs):
-    w1, w2, acts, outs = refs[:5], refs[5:10], refs[10:18], refs[18:]
+    w1, w2, acts, outs = refs[:4], refs[4:8], refs[8:16], refs[16:]
     part = acts[4].shape[0]
     rows, (_, _, width, span) = len(outs), outs[0].shape
     row, core = scal[0], scal[1]
@@ -310,68 +307,84 @@
                 out[to, way] = value
 
 
-def pair_kernel(*refs):
-    near, far, own = refs[4:]
-    to = 0
-    for keep, got in (refs[:2], refs[2:4]):
-        size = keep.shape[1] // 4
-        total = keep[...].astype(f32) + got[...].astype(f32)
-        near[:, 2 * to : 2 * to + 2 * size] = total[:, : 2 * size].astype(bf16)
-        far[:, to : to + size] = total[:, 2 * size : 3 * size].astype(bf16)
-        own[:, to : to + size] = total[:, 3 * size :]
-        to += size
-
-
-def total_kernel(near, far, own, out):
-    third = far.shape[1] // 3
-    for at, size in ((0, third), (third, 2 * third)):
-        mine = slice(at, at + size)
-        total = near[:, 2 * at : 2 * at + size].astype(f32) + far[:, mine].astype(f32) + own[:, mine]
-        out[:, 2 * at : 2 * at + size] = total.astype(bf16)
-        out[:, 2 * at + size : 2 * (at + size)] = near[:, 2 * at + size : 2 * (at + size)]
-
-
-def final_kernel(scal, here, there, scales, wq_ref, win_ref, d_wq, d_wd, d_win, d_wout, d_bq, d_bf, small):
+def pair_kernel(keep, *refs):
+    near, size = refs[-1], refs[0].shape[1]
+    for j, got in enumerate(refs[:-1]):
+        cols = slice(j * size, (j + 1) * size)
+        near[:, cols] = (keep[:, cols].astype(f32) + got[...].astype(f32)).astype(bf16)
+
+
+def total_kernel(near1, far1, own1, near2, far2, own2, c_sum, out):
+    at = own1.shape[1]
+    out[:, :at] = (near1[...].astype(f32) + far1[...].astype(f32) + own1[...]).astype(bf16)
+    out[:, at:] = (near2[...].astype(f32) + far2[...].astype(f32) + own2[...]).astype(bf16)
+    add_below(out, rows_at(4, c_sum[...]))
+
+
+def halves_of(here, there, at, size):
+    def theirs(cols):
+        piece = there[cols // there[0].shape[1]]
+        cols = cols % there[0].shape[1]
+        return piece[:, cols : cols + size].astype(f32)
+
+    mine = here[:, at : at + size].astype(f32) + theirs(at + size)
+    return mine, here[:, at + size : at + 2 * size].astype(f32) + theirs(at)
+
+
+def small_kernel(here, there0, there1, there2, own1, own2, out):
+    there = (there0, there1, there2)
+    width = out.shape[1]
+    rows, at = [], 0
+    for own, used in ((own1, 3 * own1.shape[1] // 8), (own2, own2.shape[1] // 4)):
+        half = own.shape[1] // 2
+        gain = bias = 0.0
+        for u, m in enumerate(halves_of(here, there, at, half)):
+            w = own[:width, u * half : u * half + used]
+            ones = jnp.ones((8, used), bf16)
+            gain += dot11(ones, (m[:width, :used] * w.astype(f32)).astype(bf16))
+            bias += dot11(jnp.broadcast_to(m[width : width + 1, :used], ones.shape).astype(bf16), w)
+        rows += [gain[:1], bias[:1]]
+        at += 2 * half
+    cols = slice(0, width)
+    rows.append(here[width:, cols].astype(f32)[4:5] + there0[width:, cols].astype(f32)[4:5])
+    out[...] = jnp.concatenate(rows + [jnp.zeros((3, width), f32)], axis=0)
+
+
+def final_kernel(scal, here, there0, there1, there2, scales, d_wq, d_wd, d_win, d_wout, d_bq, d_bf):
+    there = (there0, there1, there2)
     heads, width, _ = d_wd.shape
     sub = HD // 2
     tail = d_win.shape[1]
     part = tail // 2
     third = heads * sub
-    mine_first = scal[1] == 0
-    gain1, shift1, gain2, shift2 = (scales[:, i : i + 1] for i in range(4))
-
-    def both(at, size):
-        lo, hi = slice(at, at + size), slice(at + size, at + 2 * size)
-        mine = here[:, lo].astype(f32) + there[:, hi].astype(f32)
-        theirs = here[:, hi].astype(f32) + there[:, lo].astype(f32)
-        return jnp.where(mine_first, mine, theirs), jnp.where(mine_first, theirs, mine)
-
-    sums = [jnp.zeros((width, 1), f32) for _ in range(4)]
-    for a, m in enumerate(both(0, 4 * third)):
+    core = scal[1]
+    at = lax.broadcasted_iota(jnp.int32, (8, 128), 0)
+    eye = (at == lax.broadcasted_iota(jnp.int32, (8, 128), 1)).astype(f32).astype(bf16)
+    columns = dot00(scales[...], eye)
+    gain1, shift1, gain2, shift2 = (columns[:, i : i + 1] for i in range(4))
+
+    def in_order(pair):
+        mine, theirs = pair
+        return jnp.where(core == 0, mine, theirs), jnp.where(core == 0, theirs, mine)
+
+    for a, m in enumerate(in_order(halves_of(here, there, 0, 4 * third))):
         dims = slice(a * sub, (a + 1) * sub)
         row = m[width : width + 1, : 3 * third]
-        w = wq_ref[a].astype(f32)
-        sums[0] += jnp.sum(w * m[:width, : 3 * third], axis=1, keepdims=True)
-        sums[1] += jnp.sum(w * row, axis=1, keepdims=True)
-        d_bq[a : a + 1, :] = row
         grad = m[:width, : 3 * third] * gain1 + shift1 * row
         for s in range(3):
             for h in range(heads):
                 at = (s * heads + h) * sub
                 d_wq[s, h, :, dims] = grad[:, at : at + sub]
+                d_bq[s : s + 1, h * HD + a * sub : h * HD + (a + 1) * sub] = row[:, at : at + sub]
         for h in range(heads):
             at = 3 * third + h * sub
             d_wd[h, :, dims] = m[:width, at : at + sub]
-    for a, m in enumerate(both(8 * third, tail)):
+    for a, m in enumerate(in_order(halves_of(here, there, 8 * third, tail))):
         cols = slice(a * part, (a + 1) * part)
         row = m[width : width + 1, :part]
-        w = win_ref[:, cols].astype(f32)
-        sums[2] += jnp.sum(w * m[:width, :part], axis=1, keepdims=True)
-        sums[3] += jnp.sum(w * row, axis=1, keepdims=True)
-        d_bf[a : a + 1, :] = row
+        d_bf[:, cols] = row
         d_win[:, cols] = m[:width, :part] * gain2 + shift2 * row
         d_wout[:, cols] = m[:width, part:]
-    small[...] = jnp.concatenate(sums, axis=1)
 
 
 def row_kernel(scal, x_ref, *refs):
@@ -428,17 +441,20 @@
     block = width + PAD
     count = rows * half_span
 
-    both = jnp.stack([hidden_in, cotangent])
-    pieces = [both[:, :, j % 2, (j // 2) * half_span : (j // 2 + 1) * half_span] for j in range(4)]
+    counts = jnp.stack([jnp.sum(segments < 1, axis=1), jnp.sum(segments < 2, axis=1)], axis=1)
+    counts = jnp.stack([counts // 256, counts % 256], axis=2).reshape(seqs, 4).astype(bf16)
+    counts = jnp.pad(counts[:, None], ((0, 0), (0, PAD - 1), (0, half_span - 4)))
+    pieces = []
+    for j in range(4):
+        at, where = j % 2, slice((j // 2) * half_span, (j // 2 + 1) * half_span)
+        pieces.append(jnp.concatenate([hidden_in[:, at, where], cotangent[:, at, where], counts[at]]))
     sent = swap_by(col, pieces)
     got = [lax.ppermute(sent[k], ("dp", "col"), spread_peers(k)) for k in range(4)]
-    mine = jnp.stack(got)
+    counts = got[0][2 * width, :4].astype(jnp.int32)
+    counts = [256 * counts[0] + counts[1], 256 * counts[2] + counts[3]]
+    mine = jnp.stack([g[: 2 * width].reshape(2, width, half_span) for g in got])
     tokens = gather_xor(mine, "row")
 
-    counts = jnp.stack([jnp.sum(segments < 1, axis=1), jnp.sum(segments < 2, axis=1)], axis=1).astype(f32)
-    counts_other = send(counts, "dp", 1)
-    counts = pick((col >> 1) == core, counts, counts_other)
-    counts = pick((col & 1) == 1, counts[1], counts[0]).astype(jnp.int32)
     scalars = jnp.stack([row, core, crossed.astype(jnp.int32)])
 
     gain1, shift1 = ln1_gain.astype(f32), ln1_bias.astype(f32)
@@ -474,11 +490,11 @@
 
     head, tail = 2 * hw, 2 * part
     own1, own2 = in_order(halves1), in_order(halves2)
-    near1 = send_near(after(own1, [sent, counts_other]))
-    far = send(jnp.concatenate([own1[:, :head], own2[:, :tail]], axis=1), "col", 1)
-    near2 = send_near(after(own2, [near1, far, tokens[1:]]))
-    far_other = send(far, "dp", 1)
-    w1 = [own1, near1, send(near1, "dp", 1), far[:, :head], far_other[:, :head]]
+    own1 = after(own1, got[:2])
+    near1, far1 = send_near(own1), send(own1, "col", 1)
+    near2 = send_near(after(own2, [near1]))
+    w1 = [own1, near1, send(near1, "dp", 1), far1]
+    far2 = send(after(own2, [far1, w1[2]]), "col", 1)
 
     base = jnp.arange(half_span, dtype=jnp.int32)
     q_pos = jnp.concatenate([rr * span + core * half_span + base for rr in range(rows)])
@@ -508,9 +524,10 @@
         [tables, xn, cot, *w1],
         scalars,
     )
-    kv_other = send(kv, "dp", 1)
+    kv_other = [send(kv[:1], "dp", 1), send(kv[1:], "dp", 1)]
 
     by_head = pl.BlockSpec((1, HD, count), lambda h: (h, 0, 0))
+    by_head1 = pl.BlockSpec((1, 1, HD, count), lambda h: (0, h, 0, 0))
     by_head2 = pl.BlockSpec((2, 1, HD, count), lambda h: (0, h, 0, 0))
     attended, grad_q, grad_kv, grad_kv_other = pl.pallas_call(
         partial(attention_kernel, span),
@@ -520,7 +537,8 @@
             pl.BlockSpec((1, count), lambda h: (0, 0)),
             by_head,
             by_head2,
-            by_head2,
+            by_head1,
+            by_head1,
             by_head,
         ],
         out_specs=[by_head, by_head, by_head2, by_head2],
@@ -540,50 +558,81 @@
         cost_estimate=pl.CostEstimate(
             flops=0, bytes_accessed=0, transcendentals=0
         ),
-    )(scalars, q_start[None, :], queries, kv, kv_other, grad_att)
+    )(scalars, q_start[None, :], queries, kv, *kv_other, grad_att)
     grad_kv_got = [send(grad_kv_other[:1], "dp", 1), send(grad_kv_other[1:], "dp", 1)]
 
-    near2 = after(near2, [attended])
-    w2 = [own2, near2, send(near2, "dp", 1), far[:, head:], far_other[:, head:]]
+    def sums(size):
+        return [shaped((block, size), f32)] + [shaped((block, size), bf16)] * 3
+
+    half_act = shaped((head, count), bf16)
+    grads_a, att_a, grads_b, att_b, sum1, keep1, give1, far_sum1 = call(
+        partial(qkv_grad_kernel, heads),
+        [half_act] * 4 + sums(2 * head),
+        [tables, grad_q, grad_kv, *grad_kv_got, attended, xn, cot],
+        scalars,
+    )
+    got1 = send(give1, "dp", 1)
+    low_near1 = call(pair_kernel, [shaped((block, 2 * head), bf16)], [keep1, got1])[0]
+    sum_near1 = send_near(low_near1)
+    sum_far1 = send(far_sum1, "col", 1)
+
+    near2, far2 = after([near2, far2], [keep1])
+    near2 = after(near2, [far2])
+    w2 = [own2, near2, send(near2, "dp", 1), far2]
     act = shaped((part, count), bf16)
-    sums2 = shaped((block, 4 * tail), bf16)
-    up_a, hid_a, up_b, hid_b, keep2, give2 = call(
-        feed_kernel, [act] * 4 + [sums2] * 2, [xn, cot, *w2], scalars
-    )
-    got2 = send(give2, "dp", 1)
-
-    half_act = shaped((head, count), bf16)
-    sums1 = shaped((block, 4 * head), bf16)
-    grads_a, att_a, grads_b, att_b, keep1, give1 = call(
-        partial(qkv_grad_kernel, heads),
-        [half_act] * 4 + [sums1] * 2,
-        [tables, grad_q, grad_kv, *grad_kv_got, after(attended, keep2), xn, cot],
-        scalars,
-    )
-    got1 = send(give1, "dp", 1)
-    low_near, low_far, own_sum = call(
-        pair_kernel,
-        [
-            shaped((block, 2 * (head + tail)), bf16),
-            shaped((block, head + tail), bf16),
-            shaped((block, head + tail), f32),
-        ],
-        [keep1, got1, keep2, got2],
-    )
-    sum_near = send_near(low_near)
-    sum_far = send(low_far, "col", 1)
+    up_a, hid_a, up_b, hid_b, sum2, keep2, give2, far_sum2 = call(
+        feed_kernel, [act] * 4 + sums(2 * tail), [after(xn, low_near1), cot, *w2], scalars
+    )
+    third = 2 * tail // 3
+    got2 = [send(give2[:, j * third : (j + 1) * third], "dp", 1) for j in range(3)]
+    low_near2 = call(pair_kernel, [shaped((block, 2 * tail), bf16)], [keep2, *got2])[0]
+    low_near2, far_sum2 = after([low_near2, far_sum2], [sum_near1, sum_far1])
+    sum_near2 = send_near(low_near2)
+    sum_far2 = send(far_sum2, "col", 1)
 
     strip = shaped((cols, 2, width, half_span), bf16)
     sums = call(
         back_kernel,
         [strip] * rows,
-        [*w1, *w2, *after([att_a, att_b, grads_a, grads_b, up_a, up_b, hid_a, hid_b], [low_near])],
+        [*w1, *w2, att_a, att_b, grads_a, grads_b, up_a, up_b, hid_a, hid_b],
         scalars,
     )
+    sums = after(sums, [sum_near1, sum_far1])
     sums = [sums[0]] + [send(sums[j], "row", j) for j in range(1, rows)]
     piece = shaped((2, width, half_span), bf16)
     back = call(row_kernel, [piece] * cols, [mine, *sums], scalars)
+    back = after(back, [sum_near2, sum_far2])
     back = [lax.ppermute(back[k], ("dp", "col"), spread_peers(k, True)) for k in range(4)]
+    c_sum = jnp.sum(cotangent.astype(f32), axis=(1, 2))[None]
+    total = call(
+        total_kernel,
+        [shaped((block, 2 * (head + tail)), bf16)],
+        [sum_near1, sum_far1, sum1, sum_near2, sum_far2, sum2, c_sum],
+    )[0]
+    wide = total.astype(f32)
+    for k in range(2, dps, 2):
+        wide = wide + lax.ppermute(total, "dp", turn_peers(k)).astype(f32)
+    total = wide.astype(bf16)
+    third = (head + tail) * 2 // 3
+    other = [send(total[:, j * third : (j + 1) * third], "dp", 1) for j in range(3)]
+    small = call(small_kernel, [shaped((8, width), f32)], [total, *other, own1, own2])[0]
+    small = small + send(small, "row", 1)
+    small = small + send(small, "row", 2)
+    scales = jnp.pad(jnp.stack([ln1_gain, ln1_bias, ln2_gain, ln2_bias]), ((0, 4), (0, 0)))
+    d_wq, d_wd, d_w_in, d_w_out, d_bq, d_bf = call(
+        final_kernel,
+        [
+            shaped((3, heads, width, HD), f32),
+            shaped((heads, width, HD), f32),
+            shaped((width, ff), f32),
+            shaped((width, ff), f32),
+            shaped((3, hw), f32),
+            shaped((1, ff), f32),
+        ],
+        [total, *other, scales],
+        scalars,
+    )
+    back = after(back, d_bf)
     back = swap_by(col, back)
     branch, grad_x = jnp.stack(
         [jnp.concatenate([back[s], back[2 + s]], axis=2) for s in range(2)], axis=2
@@ -592,49 +641,21 @@
     layer_out = (hidden_in.astype(f32) + branch + bias_out[:, None, None]).astype(bf16)
     grad_in = cotangent.astype(f32) + grad_x
 
-    total = call(total_kernel, [shaped((block, 2 * (head + tail)), bf16)], [sum_near, sum_far, own_sum])[0]
-    wide = total.astype(f32)
-    for k in range(2, dps, 2):
-        wide = wide + lax.ppermute(total, "dp", turn_peers(k)).astype(f32)
-    total = wide.astype(bf16)
-    other = send(total, "dp", 1)
-
-    scales = jnp.stack([gain1, shift1, gain2, shift2], axis=1)
-    d_wq, d_wd, d_w_in, d_w_out, d_bq, d_bf, small = call(
-        final_kernel,
-        [
-            shaped((3, heads, width, HD), f32),
-            shaped((heads, width, HD), f32),
-            shaped((width, ff), f32),
-            shaped((width, ff), f32),
-            shaped((2, 3 * heads * sub), f32),
-            shaped((2, part), f32),
-            shaped((width, 4), f32),
-        ],
-        [total, other, scales, wq, w_in],
-        scalars,
-    )
-    c_sum = jnp.sum(cotangent.astype(f32), axis=(1, 2))
-    small = jnp.concatenate([small.T, c_sum[None]])
-    small = sum_parts(gather_xor(small, "row"))
-    d_shared = small[4]
-    for k in range(1, dps):
-        d_shared = d_shared + lax.ppermute(small[4], "dp", turn_peers(k))
     return (
         layer_out,
         grad_in,
         d_wq.reshape(w_qkv.shape),
-        d_bq.reshape(2, 3, heads, sub).transpose(1, 2, 0, 3).reshape(3, hw),
+        d_bq,
         d_wd.reshape(w_dense.shape),
-        d_shared,
-        small[0],
-        small[1],
-        small[2],
-        small[3],
+        small[4],
+        small[0] / gain1,
+        small[1] / gain1,
+        small[2] / gain2,
+        small[3] / gain2,
         d_w_in,
         d_bf.reshape(ff),
         d_w_out,
-        d_shared,
+        small[4],
     )
 
 

time: 164 us -> 146 us (0.89)
  waiting for transfers between devices: 65 us -> 51.5 us
  local copies, waits for them, and re-layouts: 17.1 us -> 10.7 us
  between operations: 1.53 us -> 4.14 us
  other arithmetic: 6.91 us -> 4.51 us
  starting transfers between devices: 38.5 us -> 40.5 us
    ppermute x21 -> x25, waiting for transfers between devices: 39.9 us -> 12.7 us  [send(): return lax.ppermute(x, axis, xor_peers(axis, shift))]
    ppermute x3 -> x4, waiting for transfers between devices: 21.3 us -> 34.6 us  [send_near(): return lax.ppermute(x, ('dp', 'col'), pairs)]
    ppermute x21 -> x25, starting transfers between devices: 14.5 us -> 21.3 us  [send(): return lax.ppermute(x, axis, xor_peers(axis, shift))]
    ppermute x4, starting transfers between devices: 11.5 us -> 7.04 us  [body(): lax.ppermute(back[k], ('dp', 'col'), spread_peers(k, True))]
    unnamed x57 -> x52, local copies, waits for them, and re-layouts: 7.01 us -> 4.57 us
    ppermute x3 -> x4, starting transfers between devices: 4.72 us -> 3.5 us  [send_near(): return lax.ppermute(x, ('dp', 'col'), pairs)]
    pallas_call x9 -> x11, Pallas kernels: 23.8 us -> 23.1 us  [call(): pl.pallas_call(kernel, out_shape=outs, in_specs=specs, out_specs=[pl.Bloc...]
  transfers between devices with their start and end apart: 33 -> 37, of which waited for: 15 -> 19; matrix products, arithmetic and copies ran while one was open for 11% -> 7% of each run, Pallas kernels for 15% -> 23%
where the time goes in v3:
time: 146 us; the launch traced here: 145 us
  waiting for transfers between devices  51.5 us (35%)
  starting transfers between devices  40.5 us (28%)
  Pallas kernels  33.8 us (23%)
  local copies, waits for them, and re-layouts  10.7 us (7%)
  other arithmetic  4.51 us (3%)
  between operations  4.14 us (3%)
    ppermute x4, waiting for transfers between devices, send_near(): return lax.ppermute(x, ('dp', 'col'), pairs)  34.6 us
    pallas_call x11, Pallas kernels, call(): pl.pallas_call(kernel, out_shape=outs, in_specs=specs, out_specs=[pl.Bloc...  23.1 us
    ppermute x25, starting transfers between devices, send(): return lax.ppermute(x, axis, xor_peers(axis, shift))  21.3 us
    ppermute x25, waiting for transfers between devices, send(): return lax.ppermute(x, axis, xor_peers(axis, shift))  12.7 us
    pallas_call x1, Pallas kernels, body(): pl.pallas_call(partial(attention_kernel, span), grid=(heads,), in_specs=[...  10.6 us
    ppermute x4, starting transfers between devices, body(): lax.ppermute(sent[k], ('dp', 'col'), spread_peers(k))  8.72 us
    ppermute x4, starting transfers between devices, body(): lax.ppermute(back[k], ('dp', 'col'), spread_peers(k, True))  7.04 us
    unnamed x52, local copies, waits for them, and re-layouts  4.57 us
  transfers between devices with their start and end apart: 37, of which 19 were waited for; matrix products, arithmetic and copies ran while one was open for 7% of the time, Pallas kernels for 23%

profile of v3, /device:TPU:1, one launch (start us, length us, event | category | flops | bytes accessed | tf_op | source)
XLA Modules:
  0.0 145.2 jit_solution(13069060587284509547)
XLA Ops:
  0.7 0.8 fusion.23
  1.7 1.0 copy.66
  2.6 1.0 copy.64
  3.8 4.2 %collective-permute-start.3 = (bf16[400,128]{1,0:T(8,128)(2,1)S(1)}, bf16[400,128]{1,0:T(8,128)(2,1)S(1)}, u32[]{:S(2)}, u32[]{:S(2)}) collective-permute-start(bf16[400,128]{1,0:T(8,128)(2,1)S(1)} %broadcast_select_fusion.8), channel_id=1, source_target_pairs={{0,17},{1,16},{2,1},{3,0},{16,19},{17,18},{18,3},{19,2},{4,21},{5,... | collective-permute-start | bytes 307208 | tf_op jit(solution)/shard_map/ppermute | solution.py:452
  8.0 0.9 collective-permute-start.2
  9.2 3.5 %collective-permute-start = (bf16[400,128]{1,0:T(8,128)(2,1)S(1)}, bf16[400,128]{1,0:T(8,128)(2,1)S(1)}, u32[]{:S(2)}, u32[]{:S(2)}) collective-permute-start(bf16[400,128]{1,0:T(8,128)(2,1)S(1)} %broadcast_select_fusion.11), channel_id=1, source_target_pairs={{0,0},{1,1},{2,16},{3,17},{16,2},{17,3},{18,18},{19,19},{4,4},{5,5... | collective-permute-start | bytes 307208 | tf_op jit(solution)/shard_map/ppermute | solution.py:452
  17.3 0.7 collective-permute-done
  18.0 1.6 %collective-permute-start.6 = (bf16[208,768]{1,0:T(8,128)(2,1)S(1)}, bf16[208,768]{1,0:T(8,128)(2,1)S(1)}, u32[]{:S(2)}, u32[]{:S(2)}) collective-permute-start(bf16[208,768]{1,0:T(8,128)(2,1)S(1)} %pad_maximum_fusion.2.refs_0_.own1), channel_id=1, source_target_pairs={{0,1},{1,0},{2,3},{3,2},{4,5},{5,4},{6,7},{7,6},{8,9},{9,8},{10,11... | collective-permute-start | bytes 958472 | tf_op jit(solution)/shard_map/ppermute | solution.py:30
  19.7 1.3 collective-permute-start.9
  21.0 1.2 collective-permute-start.10
  25.7 8.0 %collective-permute-done.4.refs_1_ = bf16[208,768]{1,0:T(8,128)(2,1)S(1)} collective-permute-done((bf16[208,768]{1,0:T(8,128)(2,1)S(1)}, bf16[208,768]{1,0:T(8,128)(2,1)S(1)}, u32[]{:S(2)}, u32[]{:S(2)}) %collective-permute-start.4) | collective-permute-done | bytes 319520 | tf_op jit(solution)/shard_map/ppermute | solution.py:38
  33.9 2.1 %collective-permute-start.7 = (bf16[208,1536]{1,0:T(8,128)(2,1)S(1)}, bf16[208,1536]{1,0:T(8,128)(2,1)S(1)}, u32[]{:S(2)}, u32[]{:S(2)}) collective-permute-start(bf16[208,1536]{1,0:T(8,128)(2,1)S(1)} %pad_maximum_fusion.refs_0_.refs_4_.own2), channel_id=1, source_target_pairs={{0,3},{1,2},{2,1},{3,0},{16,18},{17,19},{18,16},{19,17},{4,7},{5,6... | collective-permute-start | bytes 1916936 | tf_op jit(solution)/shard_map/ppermute | solution.py:38
  35.9 2.6 %collective-permute-done.11.refs_3_ = bf16[4,2,192,128]{3,2,1,0:T(8,128)(2,1)S(1)} collective-permute-done((bf16[4,2,192,128]{3,2,1,0:T(8,128)(2,1)S(1)}, bf16[4,2,192,128]{3,2,1,0:T(8,128)(2,1)S(1)}, u32[]{:S(2)}, u32[]{:S(2)}) %collective-permute-start.11) | collective-permute-done | bytes 393248 | tf_op jit(solution)/shard_map/ppermute | solution.py:30
  38.6 1.3 shard_map.254
  40.0 1.8 %shard_map.255 = (bf16[3,64,512]{2,1,0:T(8,128)(2,1)S(1)}, bf16[2,3,64,512]{3,2,1,0:T(8,128)(2,1)S(1)}, bf16[3,64,512]{2,1,0:T(8,128)(2,1)S(1)}) custom-call(s32[3]{0:T(128)S(1)} %pad_add_fusion.2.scal, f32[4,8,512]{2,1,0:T(8,128)S(1)} %pad_maximum_fusion.11.tables, bf16[832,512]{1,0:T(8,128)(2,1)S(1)} %get-tuple-element.95.xn, ...), custom_call_target="tpu_custom_call" | custom-call | tf_op jit(solution)/shard_map/pallas_call | solution.py:92
  41.9 2.8 %collective-permute-start.12 = (bf16[1,3,64,512]{3,2,1,0:T(8,128)(2,1)S(1)}, bf16[1,3,64,512]{3,2,1,0:T(8,128)(2,1)S(1)}, u32[]{:S(2)}, u32[]{:S(2)}) collective-permute-start(bf16[1,3,64,512]{3,2,1,0:T(8,128)(2,1)S(1)} %get-tuple-element.205), channel_id=1, source_target_pairs={{0,16},{16,0},{1,17},{17,1},{2,18},{18,2},{3,19},{19,3},{4,20},{20... | collective-permute-start | bytes 589832 | tf_op jit(solution)/shard_map/ppermute | solution.py:30
  44.7 1.0 collective-permute-done.12.k_other
  46.1 10.6 %shard_map.256 = (bf16[3,64,512]{2,1,0:T(8,128)(2,1)S(1)}, f32[3,64,512]{2,1,0:T(8,128)S(1)}, f32[2,3,64,512]{3,2,1,0:T(8,128)S(1)}, bf16[2,3,64,512]{3,2,1,0:T(8,128)(2,1)S(1)}) custom-call(s32[3]{0:T(128)S(1)} %pad_add_fusion.2.scal, s32[1,512]{1,0:T(1,128)S(1)} %compare_select_fusion.1.start, bf16[3,64,512]{2,1,0:T(8,128)(2,1)S(1)} %get-tuple-element.79.q_ref, ...), custom_call_target="tpu_custom_call" | custom-call | tf_op jit(solution)/shard_map/pallas_call | solution.py:532
  57.3 0.9 collective-permute-done.14.gk_other
  58.6 3.4 %shard_map.257 = (bf16[384,512]{1,0:T(8,128)(2,1)S(1)}, bf16[384,512]{1,0:T(8,128)(2,1)S(1)}, bf16[384,512]{1,0:T(8,128)(2,1)S(1)}, bf16[384,512]{1,0:T(8,128)(2...) custom-call(s32[3]{0:T(128)S(1)} %pad_add_fusion.2.scal, ...), custom_call_target="tpu_custom_call" | custom-call | tf_op jit(solution)/shard_map/pallas_call | solution.py:92
  61.9 2.5 %collective-permute-done.7.refs_1_.refs_5_ = bf16[208,1536]{1,0:T(8,128)(2,1)S(1)} collective-permute-done((bf16[208,1536]{1,0:T(8,128)(2,1)S(1)}, bf16[208,1536]{1,0:T(8,128)(2,1)S(1)}, u32[]{:S(2)}, u32[]{:S(2)}) %collective-permute-start.7) | collective-permute-done | bytes 639008 | tf_op jit(solution)/shard_map/ppermute | solution.py:38
  64.5 2.3 %collective-permute-done.8.refs_3_.refs_7_ = bf16[208,1536]{1,0:T(8,128)(2,1)S(1)} collective-permute-done((bf16[208,1536]{1,0:T(8,128)(2,1)S(1)}, bf16[208,1536]{1,0:T(8,128)(2,1)S(1)}, u32[]{:S(2)}, u32[]{:S(2)}) %collective-permute-start.8) | collective-permute-done | bytes 639008 | tf_op jit(solution)/shard_map/ppermute | solution.py:30
  66.8 1.9 %collective-permute-start.16 = (bf16[208,1536]{1,0:T(8,128)(2,1)S(1)}, bf16[208,1536]{1,0:T(8,128)(2,1)S(1)}, u32[]{:S(2)}, u32[]{:S(2)}) collective-permute-start(bf16[208,1536]{1,0:T(8,128)(2,1)S(1)} %collective-permute-done.7.refs_1_.refs_5_), channel_id=1, source_target_pairs={{0,16},{16,0},{1,17},{17,1},{2,18},{18,2},{3,19},{19,3},{4,20},{20... | collective-permute-start | bytes 1916936 | tf_op jit(solution)/shard_map/ppermute | solution.py:30
  68.7 2.2 %collective-permute-done.17.refs_0_ = bf16[208,768]{1,0:T(8,128)(2,1)S(1)} collective-permute-done((bf16[208,768]{1,0:T(8,128)(2,1)S(1)}, bf16[208,768]{1,0:T(8,128)(2,1)S(1)}, u32[]{:S(2)}, u32[]{:S(2)}) %collective-permute-start.17) | collective-permute-done | bytes 319520 | tf_op jit(solution)/shard_map/ppermute | solution.py:30
  70.9 1.4 collective-permute-start.18
  72.4 6.1 %shard_map.259 = (bf16[384,512]{1,0:T(8,128)(2,1)S(1)}, bf16[384,512]{1,0:T(8,128)(2,1)S(1)}, bf16[384,512]{1,0:T(8,128)(2,1)S(1)}, bf16[384,512]{1,0:T(8,128)(2...) custom-call(s32[3]{0:T(128)S(1)} %pad_add_fusion.2.scal, ...), custom_call_target="tpu_custom_call" | custom-call | tf_op jit(solution)/shard_map/pallas_call | solution.py:92
  78.5 2.6 %collective-permute-start.23 = (bf16[208,512]{1,0:T(8,128)(2,1)S(1)}, bf16[208,512]{1,0:T(8,128)(2,1)S(1)}, u32[]{:S(2)}, u32[]{:S(2)}) collective-permute-start(bf16[208,512]{1,0:T(8,128)(2,1)S(1)} %get-tuple-element.193), channel_id=1, source_target_pairs={{0,16},{16,0},{1,17},{17,1},{2,18},{18,2},{3,19},{19,3},{4,20},{20... | collective-permute-start | bytes 638984 | tf_op jit(solution)/shard_map/ppermute | solution.py:30
  83.1 4.9 %collective-permute-done.18.near1 = bf16[208,768]{1,0:T(8,128)(2,1)S(1)} collective-permute-done((bf16[208,768]{1,0:T(8,128)(2,1)S(1)}, bf16[208,768]{1,0:T(8,128)(2,1)S(1)}, u32[]{:S(2)}, u32[]{:S(2)}) %collective-permute-start.18) | collective-permute-done | bytes 319520 | tf_op jit(solution)/shard_map/ppermute | solution.py:38
  88.0 2.9 %collective-permute-start.27 = (bf16[208,1536]{1,0:T(8,128)(2,1)S(1)}, bf16[208,1536]{1,0:T(8,128)(2,1)S(1)}, u32[]{:S(2)}, u32[]{:S(2)}) collective-permute-start(bf16[208,1536]{1,0:T(8,128)(2,1)S(1)} %get-tuple-element.117), channel_id=1, source_target_pairs={{0,1},{1,0},{2,3},{3,2},{4,5},{5,4},{6,7},{7,6},{8,9},{9,8},{10,11... | collective-permute-start | bytes 1916936 | tf_op jit(solution)/shard_map/ppermute | solution.py:30
  90.9 5.5 %shard_map.260 = (bf16[4,2,192,128]{3,2,1,0:T(8,128)(2,1)S(1)}, bf16[4,2,192,128]{3,2,1,0:T(8,128)(2,1)S(1)}, bf16[4,2,192,128]{3,2,1,0:T(8,128)(2,1)S(1)}, bf16[4,2,192,128]{3,2,1,0:T(8,128)(2,1)S(1)}) custom-call(s32[3]{0:T(128)S(1)} %pad_add_fusion.2.scal, bf16[208,768]{1,0:T(8,128)(2,1)S(1)} %pad_maximum_fusion.2.refs_0_.own1, ...), custom_call_target="tpu_custom_call" | custom-call | tf_op jit(solution)/shard_map/pallas_call | solution.py:92
  96.4 0.9 collective-permute-start.20
  97.4 1.2 collective-permute-start.21
  99.3 19.1 %collective-permute-done.26.near2 = bf16[208,1536]{1,0:T(8,128)(2,1)S(1)} collective-permute-done((bf16[208,1536]{1,0:T(8,128)(2,1)S(1)}, bf16[208,1536]{1,0:T(8,128)(2,1)S(1)}, u32[]{:S(2)}, u32[]{:S(2)}) %collective-permute-start.26) | collective-permute-done | bytes 639008 | tf_op jit(solution)/shard_map/ppermute | solution.py:38
  118.7 0.7 shard_map.263.here
  120.6 1.1 shard_map.261
  121.7 2.9 %collective-permute-start.28 = (bf16[2,192,128]{2,1,0:T(8,128)(2,1)S(1)}, bf16[2,192,128]{2,1,0:T(8,128)(2,1)S(1)}, u32[]{:S(2)}, u32[]{:S(2)}) collective-permute-start(bf16[2,192,128]{2,1,0:T(8,128)(2,1)S(1)} %get-tuple-element.118), channel_id=1, source_target_pairs={{0,0},{1,1},{16,2},{17,3},{2,16},{3,17},{18,18},{19,19},{4,4},{5,5... | collective-permute-start | bytes 294920 | tf_op jit(solution)/shard_map/ppermute | solution.py:605
  124.6 2.1 %collective-permute-start.29 = (bf16[2,192,128]{2,1,0:T(8,128)(2,1)S(1)}, bf16[2,192,128]{2,1,0:T(8,128)(2,1)S(1)}, u32[]{:S(2)}, u32[]{:S(2)}) collective-permute-start(bf16[2,192,128]{2,1,0:T(8,128)(2,1)S(1)} %get-tuple-element.119), channel_id=1, source_target_pairs={{1,0},{0,1},{17,2},{16,3},{3,16},{2,17},{19,18},{18,19},{5,4},{4,5... | collective-permute-start | bytes 294920 | tf_op jit(solution)/shard_map/ppermute | solution.py:605
  126.8 2.0 %collective-permute-start.31 = (bf16[2,192,128]{2,1,0:T(8,128)(2,1)S(1)}, bf16[2,192,128]{2,1,0:T(8,128)(2,1)S(1)}, u32[]{:S(2)}, u32[]{:S(2)}) collective-permute-start(bf16[2,192,128]{2,1,0:T(8,128)(2,1)S(1)} %get-tuple-element.121), channel_id=1, source_target_pairs={{17,0},{16,1},{1,2},{0,3},{19,16},{18,17},{3,18},{2,19},{21,4},{20... | collective-permute-start | bytes 294920 | tf_op jit(solution)/shard_map/ppermute | solution.py:605
  128.8 2.4 %shard_map.264 = (f32[3,3,192,64]{3,2,1,0:T(8,128)S(1)}, f32[3,192,64]{2,1,0:T(8,128)S(1)}, f32[192,768]{1,0:T(8,128)}, f32[192,768]{1,0:T(8,128)}, f32[3,192]{1,0:T(4,128)}, /*index=5*/f32[1,768]{1,0:T(1,128)S(1)}) custom-call(s32[3]{0:T(128)S(1)} %pad_add_fusion.2.scal, bf16[208,2304]{1,0:T(8,128)(2,1)S(1)} %shard_map.263.here, ...), custom_call_target="tpu_custom_call" | custom-call | tf_op jit(solution)/shard_map/pallas_call | solution.py:92
  131.3 1.7 %collective-permute-done.28 = bf16[2,192,128]{2,1,0:T(8,128)(2,1)S(1)} collective-permute-done((bf16[2,192,128]{2,1,0:T(8,128)(2,1)S(1)}, bf16[2,192,128]{2,1,0:T(8,128)(2,1)S(1)}, u32[]{:S(2)}, u32[]{:S(2)}) %collective-permute-start.28) | collective-permute-done | bytes 98336 | tf_op jit(solution)/shard_map/ppermute | solution.py:605
  132.9 1.9 %collective-permute-done.30 = bf16[2,192,128]{2,1,0:T(8,128)(2,1)S(1)} collective-permute-done((bf16[2,192,128]{2,1,0:T(8,128)(2,1)S(1)}, bf16[2,192,128]{2,1,0:T(8,128)(2,1)S(1)}, u32[]{:S(2)}, u32[]{:S(2)}) %collective-permute-start.30) | collective-permute-done | bytes 98336 | tf_op jit(solution)/shard_map/ppermute | solution.py:605
  135.3 0.9 collective-permute-start.35
  136.4 1.4 collective-permute-done.35
  137.9 0.8 collective-permute-start.36
  138.8 0.9 copy.82
  139.7 1.0 copy.83
  140.8 1.2 reshape.655
  142.0 0.8 reshape.656
  (190 shorter events, 14.7 us)
Async XLA Ops:
  3.6 9.2 %copy-start.22 = (bf16[192]{0:T(256)(128)(2,1)S(1)}, bf16[192]{0:T(256)(128)(2,1)}, u32[]{:S(2)}) copy-start(bf16[192]{0:T(256)(128)(2,1)} %param.22) | copy-start | bytes 1156
  3.6 9.2 %copy-start.12 = (bf16[3,3,12288]{2,1,0:T(4,128)(2,1)S(1)}, bf16[3,3,12288]{2,1,0:T(4,128)(2,1)}, u32[]{:S(2)}) copy-start(bf16[3,3,12288]{2,1,0:T(4,128)(2,1)} %param.17) | copy-start | bytes 663556
  3.8 15.8 %collective-permute-start.3 = (bf16[400,128]{1,0:T(8,128)(2,1)S(1)}, bf16[400,128]{1,0:T(8,128)(2,1)S(1)}, u32[]{:S(2)}, u32[]{:S(2)}) collective-permute-start(bf16[400,128]{1,0:T(8,128)(2,1)S(1)} %broadcast_select_fusion.8), channel_id=1, source_target_pairs={{0,17},{1,16},{2,1},{3,0},{16,19},{17,18},{18,3},{19,2},{4,21},{5,... | collective-permute-start | bytes 307208 | tf_op jit(solution)/shard_map/ppermute | solution.py:452
  8.0 11.6 %collective-permute-start.2 = (bf16[400,128]{1,0:T(8,128)(2,1)S(1)}, bf16[400,128]{1,0:T(8,128)(2,1)S(1)}, u32[]{:S(2)}, u32[]{:S(2)}) collective-permute-start(bf16[400,128]{1,0:T(8,128)(2,1)S(1)} %broadcast_select_fusion.9), channel_id=1, source_target_pairs={{0,16},{1,17},{2,0},{3,1},{16,18},{17,19},{18,2},{19,3},{4,20},{5,... | collective-permute-start | bytes 307208 | tf_op jit(solution)/shard_map/ppermute | solution.py:452
  9.0 8.3 %collective-permute-start.1 = (bf16[400,128]{1,0:T(8,128)(2,1)S(1)}, bf16[400,128]{1,0:T(8,128)(2,1)S(1)}, u32[]{:S(2)}, u32[]{:S(2)}) collective-permute-start(bf16[400,128]{1,0:T(8,128)(2,1)S(1)} %broadcast_select_fusion.10), channel_id=1, source_target_pairs={{0,1},{1,0},{2,17},{3,16},{16,3},{17,2},{18,19},{19,18},{4,5},{5,4... | collective-permute-start | bytes 307208 | tf_op jit(solution)/shard_map/ppermute | solution.py:452
  9.2 8.8 %collective-permute-start = (bf16[400,128]{1,0:T(8,128)(2,1)S(1)}, bf16[400,128]{1,0:T(8,128)(2,1)S(1)}, u32[]{:S(2)}, u32[]{:S(2)}) collective-permute-start(bf16[400,128]{1,0:T(8,128)(2,1)S(1)} %broadcast_select_fusion.11), channel_id=1, source_target_pairs={{0,0},{1,1},{2,16},{3,17},{16,2},{17,3},{18,18},{19,19},{4,4},{5,5... | collective-permute-start | bytes 307208 | tf_op jit(solution)/shard_map/ppermute | solution.py:452
  17.2 55.2 %copy-start = (bf16[208,1536]{1,0:T(8,128)(2,1)}, bf16[208,1536]{1,0:T(8,128)(2,1)S(1)}, u32[]{:S(2)}) copy-start(bf16[208,1536]{1,0:T(8,128)(2,1)S(1)} %pad_maximum_fusion.refs_0_.refs_4_.own2) | copy-start | bytes 1916932
  18.0 15.7 %collective-permute-start.4 = (bf16[208,768]{1,0:T(8,128)(2,1)S(1)}, bf16[208,768]{1,0:T(8,128)(2,1)S(1)}, u32[]{:S(2)}, u32[]{:S(2)}) collective-permute-start(bf16[208,768]{1,0:T(8,128)(2,1)S(1)} %pad_maximum_fusion.2.refs_0_.own1), channel_id=1, source_target_pairs={{0,3},{1,2},{2,1},{3,0},{16,18},{17,19},{18,16},{19,17},{4,7},{5,6... | collective-permute-start | bytes 958472 | tf_op jit(solution)/shard_map/ppermute | solution.py:38
  18.0 21.9 %collective-permute-start.6 = (bf16[208,768]{1,0:T(8,128)(2,1)S(1)}, bf16[208,768]{1,0:T(8,128)(2,1)S(1)}, u32[]{:S(2)}, u32[]{:S(2)}) collective-permute-start(bf16[208,768]{1,0:T(8,128)(2,1)S(1)} %pad_maximum_fusion.2.refs_0_.own1), channel_id=1, source_target_pairs={{0,1},{1,0},{2,3},{3,2},{4,5},{5,4},{6,7},{7,6},{8,9},{9,8},{10,11... | collective-permute-start | bytes 958472 | tf_op jit(solution)/shard_map/ppermute | solution.py:30
  19.7 14.1 %collective-permute-start.9 = (bf16[4,2,192,128]{3,2,1,0:T(8,128)(2,1)S(1)}, bf16[4,2,192,128]{3,2,1,0:T(8,128)(2,1)S(1)}, u32[]{:S(2)}, u32[]{:S(2)}) collective-permute-start(bf16[4,2,192,128]{3,2,1,0:T(8,128)(2,1)S(1)} %pad_maximum_fusion.1.refs_0_.x_ref), channel_id=1, source_target_pairs={{0,4},{4,0},{8,12},{12,8},{1,5},{5,1},{9,13},{13,9},{2,6},{6,2},{1... | collective-permute-start | bytes 1179656 | tf_op jit(solution)/shard_map/ppermute | solution.py:30
  21.0 14.9 %collective-permute-start.10 = (bf16[4,2,192,128]{3,2,1,0:T(8,128)(2,1)S(1)}, bf16[4,2,192,128]{3,2,1,0:T(8,128)(2,1)S(1)}, u32[]{:S(2)}, u32[]{:S(2)}) collective-permute-start(bf16[4,2,192,128]{3,2,1,0:T(8,128)(2,1)S(1)} %pad_maximum_fusion.1.refs_0_.x_ref), channel_id=1, source_target_pairs={{0,8},{4,12},{8,0},{12,4},{1,9},{5,13},{9,1},{13,5},{2,10},{6,14},... | collective-permute-start | bytes 1179656 | tf_op jit(solution)/shard_map/ppermute | solution.py:30
  22.2 16.3 %collective-permute-start.11 = (bf16[4,2,192,128]{3,2,1,0:T(8,128)(2,1)S(1)}, bf16[4,2,192,128]{3,2,1,0:T(8,128)(2,1)S(1)}, u32[]{:S(2)}, u32[]{:S(2)}) collective-permute-start(bf16[4,2,192,128]{3,2,1,0:T(8,128)(2,1)S(1)} %pad_maximum_fusion.1.refs_0_.x_ref), channel_id=1, source_target_pairs={{0,12},{4,8},{8,4},{12,0},{1,13},{5,9},{9,5},{13,1},{2,14},{6,10},... | collective-permute-start | bytes 1179656 | tf_op jit(solution)/shard_map/ppermute | solution.py:30
  33.7 6.2 %collective-permute-start.5 = (bf16[208,768]{1,0:T(8,128)(2,1)S(1)}, bf16[208,768]{1,0:T(8,128)(2,1)S(1)}, u32[]{:S(2)}, u32[]{:S(2)}) collective-permute-start(bf16[208,768]{1,0:T(8,128)(2,1)S(1)} %collective-permute-done.4.refs_1_), channel_id=1, source_target_pairs={{0,16},{16,0},{1,17},{17,1},{2,18},{18,2},{3,19},{19,3},{4,20},{20... | collective-permute-start | bytes 958472 | tf_op jit(solution)/shard_map/ppermute | solution.py:30
  33.9 30.6 %collective-permute-start.7 = (bf16[208,1536]{1,0:T(8,128)(2,1)S(1)}, bf16[208,1536]{1,0:T(8,128)(2,1)S(1)}, u32[]{:S(2)}, u32[]{:S(2)}) collective-permute-start(bf16[208,1536]{1,0:T(8,128)(2,1)S(1)} %pad_maximum_fusion.refs_0_.refs_4_.own2), channel_id=1, source_target_pairs={{0,3},{1,2},{2,1},{3,0},{16,18},{17,19},{18,16},{19,17},{4,7},{5,6... | collective-permute-start | bytes 1916936 | tf_op jit(solution)/shard_map/ppermute | solution.py:38
  39.9 18.7 %copy-start.2 = (bf16[832,512]{1,0:T(8,128)(2,1)}, bf16[832,512]{1,0:T(8,128)(2,1)S(1)}, u32[]{:S(2)}) copy-start(bf16[832,512]{1,0:T(8,128)(2,1)S(1)} %get-tuple-element.95.xn) | copy-start | bytes 2555908
  39.9 26.9 %collective-permute-start.8 = (bf16[208,1536]{1,0:T(8,128)(2,1)S(1)}, bf16[208,1536]{1,0:T(8,128)(2,1)S(1)}, u32[]{:S(2)}, u32[]{:S(2)}) collective-permute-start(bf16[208,1536]{1,0:T(8,128)(2,1)S(1)} %pad_maximum_fusion.refs_0_.refs_4_.own2), channel_id=1, source_target_pairs={{0,1},{1,0},{2,3},{3,2},{4,5},{5,4},{6,7},{7,6},{8,9},{9,8},{10,11... | collective-permute-start | bytes 1916936 | tf_op jit(solution)/shard_map/ppermute | solution.py:30
  41.9 3.8 %collective-permute-start.12 = (bf16[1,3,64,512]{3,2,1,0:T(8,128)(2,1)S(1)}, bf16[1,3,64,512]{3,2,1,0:T(8,128)(2,1)S(1)}, u32[]{:S(2)}, u32[]{:S(2)}) collective-permute-start(bf16[1,3,64,512]{3,2,1,0:T(8,128)(2,1)S(1)} %get-tuple-element.205), channel_id=1, source_target_pairs={{0,16},{16,0},{1,17},{17,1},{2,18},{18,2},{3,19},{19,3},{4,20},{20... | collective-permute-start | bytes 589832 | tf_op jit(solution)/shard_map/ppermute | solution.py:30
  44.6 1.4 collective-permute-start.13
  56.8 1.5 %collective-permute-start.14 = (bf16[1,3,64,512]{3,2,1,0:T(8,128)(2,1)S(1)}, bf16[1,3,64,512]{3,2,1,0:T(8,128)(2,1)S(1)}, u32[]{:S(2)}, u32[]{:S(2)}) collective-permute-start(bf16[1,3,64,512]{3,2,1,0:T(8,128)(2,1)S(1)} %get-tuple-element.203), channel_id=1, source_target_pairs={{0,16},{16,0},{1,17},{17,1},{2,18},{18,2},{3,19},{19,3},{4,20},{20... | collective-permute-start | bytes 589832 | tf_op jit(solution)/shard_map/ppermute | solution.py:30
  57.1 1.4 collective-permute-start.15
  64.5 14.0 %copy-start.4 = (bf16[208,1536]{1,0:T(8,128)(2,1)}, bf16[208,1536]{1,0:T(8,128)(2,1)S(1)}, u32[]{:S(2)}) copy-start(bf16[208,1536]{1,0:T(8,128)(2,1)S(1)} %collective-permute-done.7.refs_1_.refs_5_) | copy-start | bytes 1916932
  66.8 11.7 %copy-start.5 = (bf16[208,1536]{1,0:T(8,128)(2,1)}, bf16[208,1536]{1,0:T(8,128)(2,1)S(1)}, u32[]{:S(2)}) copy-start(bf16[208,1536]{1,0:T(8,128)(2,1)S(1)} %collective-permute-done.8.refs_3_.refs_7_) | copy-start | bytes 1916932
  66.8 5.6 %collective-permute-start.16 = (bf16[208,1536]{1,0:T(8,128)(2,1)S(1)}, bf16[208,1536]{1,0:T(8,128)(2,1)S(1)}, u32[]{:S(2)}, u32[]{:S(2)}) collective-permute-start(bf16[208,1536]{1,0:T(8,128)(2,1)S(1)} %collective-permute-done.7.refs_1_.refs_5_), channel_id=1, source_target_pairs={{0,16},{16,0},{1,17},{17,1},{2,18},{18,2},{3,19},{19,3},{4,20},{20... | collective-permute-start | bytes 1916936 | tf_op jit(solution)/shard_map/ppermute | solution.py:30
  68.7 2.2 %collective-permute-start.17 = (bf16[208,768]{1,0:T(8,128)(2,1)S(1)}, bf16[208,768]{1,0:T(8,128)(2,1)S(1)}, u32[]{:S(2)}, u32[]{:S(2)}) collective-permute-start(bf16[208,768]{1,0:T(8,128)(2,1)S(1)} %get-tuple-element.94), channel_id=1, source_target_pairs={{0,16},{16,0},{1,17},{17,1},{2,18},{18,2},{3,19},{19,3},{4,20},{20... | collective-permute-start | bytes 958472 | tf_op jit(solution)/shard_map/ppermute | solution.py:30
  68.7 14.4 %collective-permute-start.19 = (bf16[208,768]{1,0:T(8,128)(2,1)S(1)}, bf16[208,768]{1,0:T(8,128)(2,1)S(1)}, u32[]{:S(2)}, u32[]{:S(2)}) collective-permute-start(bf16[208,768]{1,0:T(8,128)(2,1)S(1)} %get-tuple-element.104), channel_id=1, source_target_pairs={{0,1},{1,0},{2,3},{3,2},{4,5},{5,4},{6,7},{7,6},{8,9},{9,8},{10,11... | collective-permute-start | bytes 958472 | tf_op jit(solution)/shard_map/ppermute | solution.py:30
  70.9 17.1 %collective-permute-start.18 = (bf16[208,768]{1,0:T(8,128)(2,1)S(1)}, bf16[208,768]{1,0:T(8,128)(2,1)S(1)}, u32[]{:S(2)}, u32[]{:S(2)}) collective-permute-start(bf16[208,768]{1,0:T(8,128)(2,1)S(1)} %shard_map.258), channel_id=1, source_target_pairs={{0,3},{1,2},{2,1},{3,0},{16,18},{17,19},{18,16},{19,17},{4,7},{5,6... | collective-permute-start | bytes 958472 | tf_op jit(solution)/shard_map/ppermute | solution.py:38
  72.4 6.1 %copy-start.6 = (bf16[208,1536]{1,0:T(8,128)(2,1)}, bf16[208,1536]{1,0:T(8,128)(2,1)S(1)}, u32[]{:S(2)}) copy-start(bf16[208,1536]{1,0:T(8,128)(2,1)S(1)} %collective-permute-done.16.refs_2_.refs_6_) | copy-start | bytes 1916932
  78.5 3.7 %collective-permute-start.23 = (bf16[208,512]{1,0:T(8,128)(2,1)S(1)}, bf16[208,512]{1,0:T(8,128)(2,1)S(1)}, u32[]{:S(2)}, u32[]{:S(2)}) collective-permute-start(bf16[208,512]{1,0:T(8,128)(2,1)S(1)} %get-tuple-element.193), channel_id=1, source_target_pairs={{0,16},{16,0},{1,17},{17,1},{2,18},{18,2},{3,19},{19,3},{4,20},{20... | collective-permute-start | bytes 638984 | tf_op jit(solution)/shard_map/ppermute | solution.py:30
  81.1 1.5 %collective-permute-start.24 = (bf16[208,512]{1,0:T(8,128)(2,1)S(1)}, bf16[208,512]{1,0:T(8,128)(2,1)S(1)}, u32[]{:S(2)}, u32[]{:S(2)}) collective-permute-start(bf16[208,512]{1,0:T(8,128)(2,1)S(1)} %get-tuple-element.192), channel_id=1, source_target_pairs={{0,16},{16,0},{1,17},{17,1},{2,18},{18,2},{3,19},{19,3},{4,20},{20... | collective-permute-start | bytes 638984 | tf_op jit(solution)/shard_map/ppermute | solution.py:30
  81.2 1.7 %collective-permute-start.25 = (bf16[208,512]{1,0:T(8,128)(2,1)S(1)}, bf16[208,512]{1,0:T(8,128)(2,1)S(1)}, u32[]{:S(2)}, u32[]{:S(2)}) collective-permute-start(bf16[208,512]{1,0:T(8,128)(2,1)S(1)} %get-tuple-element.191), channel_id=1, source_target_pairs={{0,16},{16,0},{1,17},{17,1},{2,18},{18,2},{3,19},{19,3},{4,20},{20... | collective-permute-start | bytes 638984 | tf_op jit(solution)/shard_map/ppermute | solution.py:30
  88.0 30.5 %collective-permute-start.26 = (bf16[208,1536]{1,0:T(8,128)(2,1)S(1)}, bf16[208,1536]{1,0:T(8,128)(2,1)S(1)}, u32[]{:S(2)}, u32[]{:S(2)}) collective-permute-start(bf16[208,1536]{1,0:T(8,128)(2,1)S(1)} %shard_map.262), channel_id=1, source_target_pairs={{0,3},{1,2},{2,1},{3,0},{16,18},{17,19},{18,16},{19,17},{4,7},{5,6... | collective-permute-start | bytes 1916936 | tf_op jit(solution)/shard_map/ppermute | solution.py:38
  88.0 30.7 %collective-permute-start.27 = (bf16[208,1536]{1,0:T(8,128)(2,1)S(1)}, bf16[208,1536]{1,0:T(8,128)(2,1)S(1)}, u32[]{:S(2)}, u32[]{:S(2)}) collective-permute-start(bf16[208,1536]{1,0:T(8,128)(2,1)S(1)} %get-tuple-element.117), channel_id=1, source_target_pairs={{0,1},{1,0},{2,3},{3,2},{4,5},{5,4},{6,7},{7,6},{8,9},{9,8},{10,11... | collective-permute-start | bytes 1916936 | tf_op jit(solution)/shard_map/ppermute | solution.py:30
  90.9 6.4 %copy-start.8 = (bf16[192,2,256]{2,1,0:T(2,128)(2,1)S(1)}, bf16[192,2,256]{2,1,0:T(2,128)(2,1)}, u32[]{:S(2)}) copy-start(bf16[192,2,256]{2,1,0:T(2,128)(2,1)} %param.29) | copy-start | bytes 589828
  90.9 27.8 %copy-start.7 = (f32[208,1536]{1,0:T(8,128)S(1)}, f32[208,1536]{1,0:T(8,128)}, u32[]{:S(2)}) copy-start(f32[208,1536]{1,0:T(8,128)} %get-tuple-element.123.own2) | copy-start | bytes 3833860
  96.4 23.7 %collective-permute-start.20 = (bf16[4,2,192,128]{3,2,1,0:T(8,128)(2,1)S(1)}, bf16[4,2,192,128]{3,2,1,0:T(8,128)(2,1)S(1)}, u32[]{:S(2)}, u32[]{:S(2)}) collective-permute-start(bf16[4,2,192,128]{3,2,1,0:T(8,128)(2,1)S(1)} %get-tuple-element.106), channel_id=1, source_target_pairs={{0,4},{4,0},{8,12},{12,8},{1,5},{5,1},{9,13},{13,9},{2,6},{6,2},{1... | collective-permute-start | bytes 1179656 | tf_op jit(solution)/shard_map/ppermute | solution.py:30
  97.4 23.2 %collective-permute-start.21 = (bf16[4,2,192,128]{3,2,1,0:T(8,128)(2,1)S(1)}, bf16[4,2,192,128]{3,2,1,0:T(8,128)(2,1)S(1)}, u32[]{:S(2)}, u32[]{:S(2)}) collective-permute-start(bf16[4,2,192,128]{3,2,1,0:T(8,128)(2,1)S(1)} %get-tuple-element.107), channel_id=1, source_target_pairs={{0,8},{4,12},{8,0},{12,4},{1,9},{5,13},{9,1},{13,5},{2,10},{6,14},... | collective-permute-start | bytes 1179656 | tf_op jit(solution)/shard_map/ppermute | solution.py:30
  98.6 22.0 %collective-permute-start.22 = (bf16[4,2,192,128]{3,2,1,0:T(8,128)(2,1)S(1)}, bf16[4,2,192,128]{3,2,1,0:T(8,128)(2,1)S(1)}, u32[]{:S(2)}, u32[]{:S(2)}) collective-permute-start(bf16[4,2,192,128]{3,2,1,0:T(8,128)(2,1)S(1)} %get-tuple-element.108), channel_id=1, source_target_pairs={{0,12},{4,8},{8,4},{12,0},{1,13},{5,9},{9,5},{13,1},{2,14},{6,10},... | collective-permute-start | bytes 1179656 | tf_op jit(solution)/shard_map/ppermute | solution.py:30
  119.5 7.3 %collective-permute-start.32 = (bf16[208,768]{1,0:T(8,128)(2,1)S(1)}, bf16[208,768]{1,0:T(8,128)(2,1)S(1)}, u32[]{:S(2)}, u32[]{:S(2)}) collective-permute-start(bf16[208,768]{1,0:T(8,128)(2,1)S(1)} %get-tuple-element.188), channel_id=1, source_target_pairs={{0,16},{16,0},{1,17},{17,1},{2,18},{18,2},{3,19},{19,3},{4,20},{20... | collective-permute-start | bytes 958472 | tf_op jit(solution)/shard_map/ppermute | solution.py:30
  119.9 6.8 %collective-permute-start.33 = (bf16[208,768]{1,0:T(8,128)(2,1)S(1)}, bf16[208,768]{1,0:T(8,128)(2,1)S(1)}, u32[]{:S(2)}, u32[]{:S(2)}) collective-permute-start(bf16[208,768]{1,0:T(8,128)(2,1)S(1)} %get-tuple-element.187), channel_id=1, source_target_pairs={{0,16},{16,0},{1,17},{17,1},{2,18},{18,2},{3,19},{19,3},{4,20},{20... | collective-permute-start | bytes 958472 | tf_op jit(solution)/shard_map/ppermute | solution.py:30
  120.1 8.7 %collective-permute-start.34 = (bf16[208,768]{1,0:T(8,128)(2,1)S(1)}, bf16[208,768]{1,0:T(8,128)(2,1)S(1)}, u32[]{:S(2)}, u32[]{:S(2)}) collective-permute-start(bf16[208,768]{1,0:T(8,128)(2,1)S(1)} %get-tuple-element.186), channel_id=1, source_target_pairs={{0,16},{16,0},{1,17},{17,1},{2,18},{18,2},{3,19},{19,3},{4,20},{20... | collective-permute-start | bytes 958472 | tf_op jit(solution)/shard_map/ppermute | solution.py:30
  121.7 13.1 %copy-start.1 = (bf16[208,1536]{1,0:T(8,128)(2,1)S(1)}, bf16[208,1536]{1,0:T(8,128)(2,1)}, u32[]{:S(2)}) copy-start(bf16[208,1536]{1,0:T(8,128)(2,1)} %copy-done) | copy-start | bytes 1916932
  121.7 11.2 %collective-permute-start.28 = (bf16[2,192,128]{2,1,0:T(8,128)(2,1)S(1)}, bf16[2,192,128]{2,1,0:T(8,128)(2,1)S(1)}, u32[]{:S(2)}, u32[]{:S(2)}) collective-permute-start(bf16[2,192,128]{2,1,0:T(8,128)(2,1)S(1)} %get-tuple-element.118), channel_id=1, source_target_pairs={{0,0},{1,1},{16,2},{17,3},{2,16},{3,17},{18,18},{19,19},{4,4},{5,5... | collective-permute-start | bytes 294920 | tf_op jit(solution)/shard_map/ppermute | solution.py:605
  124.6 8.3 %collective-permute-start.29 = (bf16[2,192,128]{2,1,0:T(8,128)(2,1)S(1)}, bf16[2,192,128]{2,1,0:T(8,128)(2,1)S(1)}, u32[]{:S(2)}, u32[]{:S(2)}) collective-permute-start(bf16[2,192,128]{2,1,0:T(8,128)(2,1)S(1)} %get-tuple-element.119), channel_id=1, source_target_pairs={{1,0},{0,1},{17,2},{16,3},{3,16},{2,17},{19,18},{18,19},{5,4},{4,5... | collective-permute-start | bytes 294920 | tf_op jit(solution)/shard_map/ppermute | solution.py:605
  126.8 8.0 %collective-permute-start.30 = (bf16[2,192,128]{2,1,0:T(8,128)(2,1)S(1)}, bf16[2,192,128]{2,1,0:T(8,128)(2,1)S(1)}, u32[]{:S(2)}, u32[]{:S(2)}) collective-permute-start(bf16[2,192,128]{2,1,0:T(8,128)(2,1)S(1)} %get-tuple-element.120), channel_id=1, source_target_pairs={{16,0},{17,1},{0,2},{1,3},{18,16},{19,17},{2,18},{3,19},{20,4},{21... | collective-permute-start | bytes 294920 | tf_op jit(solution)/shard_map/ppermute | solution.py:605
  126.8 8.0 %collective-permute-start.31 = (bf16[2,192,128]{2,1,0:T(8,128)(2,1)S(1)}, bf16[2,192,128]{2,1,0:T(8,128)(2,1)S(1)}, u32[]{:S(2)}, u32[]{:S(2)}) collective-permute-start(bf16[2,192,128]{2,1,0:T(8,128)(2,1)S(1)} %get-tuple-element.121), channel_id=1, source_target_pairs={{17,0},{16,1},{1,2},{0,3},{19,16},{18,17},{3,18},{2,19},{21,4},{20... | collective-permute-start | bytes 294920 | tf_op jit(solution)/shard_map/ppermute | solution.py:605
  135.3 3.4 %copy-start.9 = (bf16[192,2,256]{2,1,0:T(2,128)(2,1)S(1)}, bf16[192,2,256]{2,1,0:T(2,128)(2,1)}, u32[]{:S(2)}) copy-start(bf16[192,2,256]{2,1,0:T(2,128)(2,1)} %param.15) | copy-start | bytes 589828
  135.3 2.6 %collective-permute-start.35 = (f32[8,192]{1,0:T(8,128)S(1)}, f32[8,192]{1,0:T(8,128)S(1)}, u32[]{:S(2)}, u32[]{:S(2)}) collective-permute-start(f32[8,192]{1,0:T(8,128)S(1)} %shard_map.265), channel_id=1, source_target_pairs={{0,4},{4,0},{8,12},{12,8},{1,5},{5,1},{9,13},{13,9},{2,6},{6,2},{1... | collective-permute-start | bytes 18440 | tf_op jit(solution)/shard_map/ppermute | solution.py:30
  137.9 5.5 %collective-permute-start.36 = (f32[8,192]{1,0:T(8,128)S(1)}, f32[8,192]{1,0:T(8,128)S(1)}, u32[]{:S(2)}, u32[]{:S(2)}) collective-permute-start(f32[8,192]{1,0:T(8,128)S(1)} %add.183), channel_id=1, source_target_pairs={{0,8},{4,12},{8,0},{12,4},{1,9},{5,13},{9,1},{13,5},{2,10},{6,14},... | collective-permute-start | bytes 18440 | tf_op jit(solution)/shard_map/ppermute | solution.py:30
  (12 other events, 14.2 us)

commit v4 on v3

--- a/solution.py
+++ b/solution.py
@@ -346,8 +346,8 @@
         rows += [gain[:1], bias[:1]]
         at += 2 * half
     cols = slice(0, width)
-    rows.append(here[width:, cols].astype(f32)[4:5] + there0[width:, cols].astype(f32)[4:5])
-    out[...] = jnp.concatenate(rows + [jnp.zeros((3, width), f32)], axis=0)
+    shared = here[width:, cols].astype(f32)[4:5] + there0[width:, cols].astype(f32)[4:5]
+    out[...] = jnp.concatenate(rows + [shared, shared, jnp.zeros((2, width), f32)], axis=0)
 
 
 def final_kernel(scal, here, there0, there1, there2, scales, d_wq, d_wd, d_win, d_wout, d_bq, d_bf):
@@ -490,7 +490,7 @@
 
     head, tail = 2 * hw, 2 * part
     own1, own2 = in_order(halves1), in_order(halves2)
-    own1 = after(own1, got[:2])
+    own1 = after(own1, got[2:])
     near1, far1 = send_near(own1), send(own1, "col", 1)
     near2 = send_near(after(own2, [near1]))
     w1 = [own1, near1, send(near1, "dp", 1), far1]
@@ -586,9 +586,6 @@
     third = 2 * tail // 3
     got2 = [send(give2[:, j * third : (j + 1) * third], "dp", 1) for j in range(3)]
     low_near2 = call(pair_kernel, [shaped((block, 2 * tail), bf16)], [keep2, *got2])[0]
-    low_near2, far_sum2 = after([low_near2, far_sum2], [sum_near1, sum_far1])
-    sum_near2 = send_near(low_near2)
-    sum_far2 = send(far_sum2, "col", 1)
 
     strip = shaped((cols, 2, width, half_span), bf16)
     sums = call(
@@ -597,11 +594,14 @@
         [*w1, *w2, att_a, att_b, grads_a, grads_b, up_a, up_b, hid_a, hid_b],
         scalars,
     )
+    low_near2, far_sum2 = after([low_near2, far_sum2], [sum_near1, sum_far1, sums[0]])
+    sum_near2 = send_near(low_near2)
+    sum_far2 = send(far_sum2, "col", 1)
     sums = after(sums, [sum_near1, sum_far1])
     sums = [sums[0]] + [send(sums[j], "row", j) for j in range(1, rows)]
     piece = shaped((2, width, half_span), bf16)
     back = call(row_kernel, [piece] * cols, [mine, *sums], scalars)
-    back = after(back, [sum_near2, sum_far2])
+    back, sum_near2, sum_far2 = lax.optimization_barrier((back, sum_near2, sum_far2))
     back = [lax.ppermute(back[k], ("dp", "col"), spread_peers(k, True)) for k in range(4)]
     c_sum = jnp.sum(cotangent.astype(f32), axis=(1, 2))[None]
     total = call(
@@ -618,6 +618,8 @@
     small = call(small_kernel, [shaped((8, width), f32)], [total, *other, own1, own2])[0]
     small = small + send(small, "row", 1)
     small = small + send(small, "row", 2)
+    unit = jnp.ones_like(gain1)
+    small = small / jnp.stack([gain1, gain1, gain2, gain2, unit, unit, unit, unit])
     scales = jnp.pad(jnp.stack([ln1_gain, ln1_bias, ln2_gain, ln2_bias]), ((0, 4), (0, 0)))
     d_wq, d_wd, d_w_in, d_w_out, d_bq, d_bf = call(
         final_kernel,
@@ -648,14 +650,14 @@
         d_bq,
         d_wd.reshape(w_dense.shape),
         small[4],
-        small[0] / gain1,
-        small[1] / gain1,
-        small[2] / gain2,
-        small[3] / gain2,
+        small[0],
+        small[1],
+        small[2],
+        small[3],
         d_w_in,
         d_bf.reshape(ff),
         d_w_out,
-        small[4],
+        small[5],
     )
 
 

time: 146 us -> 143 us (0.979)
  starting transfers between devices: 40.5 us -> 37 us
  waiting for transfers between devices: 51.5 us -> 53.2 us
    ppermute x25, waiting for transfers between devices: 12.7 us -> 26.4 us  [send(): return lax.ppermute(x, axis, xor_peers(axis, shift))]
    ppermute x4, waiting for transfers between devices: 34.6 us -> 24.8 us  [send_near(): return lax.ppermute(x, ('dp', 'col'), pairs)]
    ppermute x25, starting transfers between devices: 21.3 us -> 16.1 us  [send(): return lax.ppermute(x, axis, xor_peers(axis, shift))]
    ppermute x4, waiting for transfers between devices: 3.54 us -> 1.89 us  [body(): lax.ppermute(back[k], ('dp', 'col'), spread_peers(k, True))]
    unnamed x52 -> x49, local copies, waits for them, and re-layouts: 4.57 us -> 3.95 us
  transfers between devices with their start and end apart: 37 -> 37, of which waited for: 19 -> 15; matrix products, arithmetic and copies ran while one was open for 7% -> 7% of each run, Pallas kernels for 23% -> 23%
where the time goes in v4:
time: 143 us
  waiting for transfers between devices  53.2 us (37%)
  starting transfers between devices  37 us (26%)
  Pallas kernels  33.7 us (24%)
  local copies, waits for them, and re-layouts  11.6 us (8%)
  between operations  4.21 us (3%)
  other arithmetic  3.39 us (2%)
    ppermute x25, waiting for transfers between devices, send(): return lax.ppermute(x, axis, xor_peers(axis, shift))  26.4 us
    ppermute x4, waiting for transfers between devices, send_near(): return lax.ppermute(x, ('dp', 'col'), pairs)  24.8 us
    pallas_call x11, Pallas kernels, call(): pl.pallas_call(kernel, out_shape=outs, in_specs=specs, out_specs=[pl.Bloc...  23.1 us
    ppermute x25, starting transfers between devices, send(): return lax.ppermute(x, axis, xor_peers(axis, shift))  16.1 us
    pallas_call x1, Pallas kernels, body(): pl.pallas_call(partial(attention_kernel, span), grid=(heads,), in_specs=[...  10.6 us
    ppermute x4, starting transfers between devices, body(): lax.ppermute(sent[k], ('dp', 'col'), spread_peers(k))  9.72 us
    ppermute x4, starting transfers between devices, body(): lax.ppermute(back[k], ('dp', 'col'), spread_peers(k, True))  6.76 us
    ppermute x4, starting transfers between devices, send_near(): return lax.ppermute(x, ('dp', 'col'), pairs)  4.44 us
  transfers between devices with their start and end apart: 37, of which 15 were waited for; matrix products, arithmetic and copies ran while one was open for 7% of the time, Pallas kernels for 23%

profile of v4, /device:TPU:1, one launch (start us, length us, event | category | flops | bytes accessed | tf_op | source)
XLA Modules:
  0.0 143.0 jit_solution(4860519183073569233)
XLA Ops:
  0.6 0.8 fusion.23
  1.7 1.0 copy.64
  2.6 1.0 copy.66
  3.8 5.6 %collective-permute-start = (bf16[400,128]{1,0:T(8,128)(2,1)S(1)}, bf16[400,128]{1,0:T(8,128)(2,1)S(1)}, u32[]{:S(2)}, u32[]{:S(2)}) collective-permute-start(bf16[400,128]{1,0:T(8,128)(2,1)S(1)} %broadcast_select_fusion.11), channel_id=1, source_target_pairs={{0,0},{1,1},{2,16},{3,17},{16,2},{17,3},{18,18},{19,19},{4,4},{5,5... | collective-permute-start | bytes 307208 | tf_op jit(solution)/shard_map/ppermute | solution.py:452
  9.6 1.2 collective-permute-start.3
  10.8 2.9 %collective-permute-start.1 = (bf16[400,128]{1,0:T(8,128)(2,1)S(1)}, bf16[400,128]{1,0:T(8,128)(2,1)S(1)}, u32[]{:S(2)}, u32[]{:S(2)}) collective-permute-start(bf16[400,128]{1,0:T(8,128)(2,1)S(1)} %broadcast_select_fusion.10), channel_id=1, source_target_pairs={{0,1},{1,0},{2,17},{3,16},{16,3},{17,2},{18,19},{19,18},{4,5},{5,4... | collective-permute-start | bytes 307208 | tf_op jit(solution)/shard_map/ppermute | solution.py:452
  18.4 1.3 collective-permute-start.10
  19.7 1.2 collective-permute-start.11
  21.1 2.1 %collective-permute-start.4 = (bf16[208,768]{1,0:T(8,128)(2,1)S(1)}, bf16[208,768]{1,0:T(8,128)(2,1)S(1)}, u32[]{:S(2)}, u32[]{:S(2)}) collective-permute-start(bf16[208,768]{1,0:T(8,128)(2,1)S(1)} %pad_maximum_fusion.2.refs_0_.own1), channel_id=1, source_target_pairs={{0,3},{1,2},{2,1},{3,0},{16,18},{17,19},{18,16},{19,17},{4,7},{5,6... | collective-permute-start | bytes 958472 | tf_op jit(solution)/shard_map/ppermute | solution.py:38
  26.7 10.0 %collective-permute-done.4.refs_1_ = bf16[208,768]{1,0:T(8,128)(2,1)S(1)} collective-permute-done((bf16[208,768]{1,0:T(8,128)(2,1)S(1)}, bf16[208,768]{1,0:T(8,128)(2,1)S(1)}, u32[]{:S(2)}, u32[]{:S(2)}) %collective-permute-start.4) | collective-permute-done | bytes 319520 | tf_op jit(solution)/shard_map/ppermute | solution.py:38
  36.9 1.1 collective-permute-done.10.refs_2_
  38.0 2.3 %collective-permute-start.7 = (bf16[208,1536]{1,0:T(8,128)(2,1)S(1)}, bf16[208,1536]{1,0:T(8,128)(2,1)S(1)}, u32[]{:S(2)}, u32[]{:S(2)}) collective-permute-start(bf16[208,1536]{1,0:T(8,128)(2,1)S(1)} %pad_maximum_fusion.refs_0_.refs_4_.own2), channel_id=1, source_target_pairs={{0,3},{1,2},{2,1},{3,0},{16,18},{17,19},{18,16},{19,17},{4,7},{5,6... | collective-permute-start | bytes 1916936 | tf_op jit(solution)/shard_map/ppermute | solution.py:38
  40.3 1.3 shard_map.254
  41.6 1.8 %shard_map.255 = (bf16[3,64,512]{2,1,0:T(8,128)(2,1)S(1)}, bf16[2,3,64,512]{3,2,1,0:T(8,128)(2,1)S(1)}, bf16[3,64,512]{2,1,0:T(8,128)(2,1)S(1)}) custom-call(s32[3]{0:T(128)S(1)} %pad_add_fusion.2.scal, f32[4,8,512]{2,1,0:T(8,128)S(1)} %pad_maximum_fusion.11.tables, bf16[832,512]{1,0:T(8,128)(2,1)S(1)} %get-tuple-element.97.xn, ...), custom_call_target="tpu_custom_call" | custom-call | tf_op jit(solution)/shard_map/pallas_call | solution.py:92
  44.5 0.7 collective-permute-done.12.k_other
  45.6 10.6 %shard_map.256 = (bf16[3,64,512]{2,1,0:T(8,128)(2,1)S(1)}, f32[3,64,512]{2,1,0:T(8,128)S(1)}, f32[2,3,64,512]{3,2,1,0:T(8,128)S(1)}, bf16[2,3,64,512]{3,2,1,0:T(8,128)(2,1)S(1)}) custom-call(s32[3]{0:T(128)S(1)} %pad_add_fusion.2.scal, s32[1,512]{1,0:T(1,128)S(1)} %compare_select_fusion.1.start, bf16[3,64,512]{2,1,0:T(8,128)(2,1)S(1)} %get-tuple-element.81.q_ref, ...), custom_call_target="tpu_custom_call" | custom-call | tf_op jit(solution)/shard_map/pallas_call | solution.py:532
  56.8 0.9 collective-permute-done.14.gk_other
  58.1 3.4 %shard_map.257 = (bf16[384,512]{1,0:T(8,128)(2,1)S(1)}, bf16[384,512]{1,0:T(8,128)(2,1)S(1)}, bf16[384,512]{1,0:T(8,128)(2,1)S(1)}, bf16[384,512]{1,0:T(8,128)(2...) custom-call(s32[3]{0:T(128)S(1)} %pad_add_fusion.2.scal, ...), custom_call_target="tpu_custom_call" | custom-call | tf_op jit(solution)/shard_map/pallas_call | solution.py:92
  61.4 6.1 %collective-permute-done.7.refs_1_.refs_5_ = bf16[208,1536]{1,0:T(8,128)(2,1)S(1)} collective-permute-done((bf16[208,1536]{1,0:T(8,128)(2,1)S(1)}, bf16[208,1536]{1,0:T(8,128)(2,1)S(1)}, u32[]{:S(2)}, u32[]{:S(2)}) %collective-permute-start.7) | collective-permute-done | bytes 639008 | tf_op jit(solution)/shard_map/ppermute | solution.py:38
  67.6 3.3 %collective-permute-done.8.refs_3_.refs_7_ = bf16[208,1536]{1,0:T(8,128)(2,1)S(1)} collective-permute-done((bf16[208,1536]{1,0:T(8,128)(2,1)S(1)}, bf16[208,1536]{1,0:T(8,128)(2,1)S(1)}, u32[]{:S(2)}, u32[]{:S(2)}) %collective-permute-start.8) | collective-permute-done | bytes 639008 | tf_op jit(solution)/shard_map/ppermute | solution.py:30
  70.9 0.8 collective-permute-start.16
  71.8 2.2 %collective-permute-done.17.refs_0_ = bf16[208,768]{1,0:T(8,128)(2,1)S(1)} collective-permute-done((bf16[208,768]{1,0:T(8,128)(2,1)S(1)}, bf16[208,768]{1,0:T(8,128)(2,1)S(1)}, u32[]{:S(2)}, u32[]{:S(2)}) %collective-permute-start.17) | collective-permute-done | bytes 319520 | tf_op jit(solution)/shard_map/ppermute | solution.py:30
  74.1 6.1 %shard_map.259 = (bf16[384,512]{1,0:T(8,128)(2,1)S(1)}, bf16[384,512]{1,0:T(8,128)(2,1)S(1)}, bf16[384,512]{1,0:T(8,128)(2,1)S(1)}, bf16[384,512]{1,0:T(8,128)(2...) custom-call(s32[3]{0:T(128)S(1)} %pad_add_fusion.2.scal, ...), custom_call_target="tpu_custom_call" | custom-call | tf_op jit(solution)/shard_map/pallas_call | solution.py:92
  80.3 1.9 %collective-permute-start.23 = (bf16[208,512]{1,0:T(8,128)(2,1)S(1)}, bf16[208,512]{1,0:T(8,128)(2,1)S(1)}, u32[]{:S(2)}, u32[]{:S(2)}) collective-permute-start(bf16[208,512]{1,0:T(8,128)(2,1)S(1)} %get-tuple-element.197), channel_id=1, source_target_pairs={{0,16},{16,0},{1,17},{17,1},{2,18},{18,2},{3,19},{19,3},{4,20},{20... | collective-permute-start | bytes 638984 | tf_op jit(solution)/shard_map/ppermute | solution.py:30
  82.7 5.4 %shard_map.260 = (bf16[4,2,192,128]{3,2,1,0:T(8,128)(2,1)S(1)}, bf16[4,2,192,128]{3,2,1,0:T(8,128)(2,1)S(1)}, bf16[4,2,192,128]{3,2,1,0:T(8,128)(2,1)S(1)}, bf16[4,2,192,128]{3,2,1,0:T(8,128)(2,1)S(1)}) custom-call(s32[3]{0:T(128)S(1)} %pad_add_fusion.2.scal, bf16[208,768]{1,0:T(8,128)(2,1)S(1)} %pad_maximum_fusion.2.refs_0_.own1, ...), custom_call_target="tpu_custom_call" | custom-call | tf_op jit(solution)/shard_map/pallas_call | solution.py:92
  88.3 2.1 %collective-permute-done.18.near1 = bf16[208,768]{1,0:T(8,128)(2,1)S(1)} collective-permute-done((bf16[208,768]{1,0:T(8,128)(2,1)S(1)}, bf16[208,768]{1,0:T(8,128)(2,1)S(1)}, u32[]{:S(2)}, u32[]{:S(2)}) %collective-permute-start.18) | collective-permute-done | bytes 319520 | tf_op jit(solution)/shard_map/ppermute | solution.py:38
  90.4 1.5 %collective-permute-start.27 = (bf16[208,1536]{1,0:T(8,128)(2,1)S(1)}, bf16[208,1536]{1,0:T(8,128)(2,1)S(1)}, u32[]{:S(2)}, u32[]{:S(2)}) collective-permute-start(bf16[208,1536]{1,0:T(8,128)(2,1)S(1)} %get-tuple-element.119), channel_id=1, source_target_pairs={{0,1},{1,0},{2,3},{3,2},{4,5},{5,4},{6,7},{7,6},{8,9},{9,8},{10,11... | collective-permute-start | bytes 1916936 | tf_op jit(solution)/shard_map/ppermute | solution.py:30
  91.9 1.2 collective-permute-start.20
  93.1 1.2 collective-permute-start.21
  94.7 8.1 %collective-permute-done.20.refs_1_ = bf16[4,2,192,128]{3,2,1,0:T(8,128)(2,1)S(1)} collective-permute-done((bf16[4,2,192,128]{3,2,1,0:T(8,128)(2,1)S(1)}, bf16[4,2,192,128]{3,2,1,0:T(8,128)(2,1)S(1)}, u32[]{:S(2)}, u32[]{:S(2)}) %collective-permute-start.20) | collective-permute-done | bytes 393248 | tf_op jit(solution)/shard_map/ppermute | solution.py:30
  102.8 8.3 %collective-permute-done.21.refs_2_ = bf16[4,2,192,128]{3,2,1,0:T(8,128)(2,1)S(1)} collective-permute-done((bf16[4,2,192,128]{3,2,1,0:T(8,128)(2,1)S(1)}, bf16[4,2,192,128]{3,2,1,0:T(8,128)(2,1)S(1)}, u32[]{:S(2)}, u32[]{:S(2)}) %collective-permute-start.21) | collective-permute-done | bytes 393248 | tf_op jit(solution)/shard_map/ppermute | solution.py:30
  111.1 1.1 collective-permute-done.22.refs_3_
  112.3 1.1 shard_map.261
  113.4 6.6 %collective-permute-done.26.near2 = bf16[208,1536]{1,0:T(8,128)(2,1)S(1)} collective-permute-done((bf16[208,1536]{1,0:T(8,128)(2,1)S(1)}, bf16[208,1536]{1,0:T(8,128)(2,1)S(1)}, u32[]{:S(2)}, u32[]{:S(2)}) %collective-permute-start.26) | collective-permute-done | bytes 639008 | tf_op jit(solution)/shard_map/ppermute | solution.py:38
  120.0 0.7 shard_map.263.here
  120.7 1.0 fusion.42
  121.7 1.0 collective-permute-start.32
  123.3 2.6 %collective-permute-start.28 = (bf16[2,192,128]{2,1,0:T(8,128)(2,1)S(1)}, bf16[2,192,128]{2,1,0:T(8,128)(2,1)S(1)}, u32[]{:S(2)}, u32[]{:S(2)}) collective-permute-start(bf16[2,192,128]{2,1,0:T(8,128)(2,1)S(1)} %get-tuple-element.120), channel_id=1, source_target_pairs={{0,0},{1,1},{16,2},{17,3},{2,16},{3,17},{18,18},{19,19},{4,4},{5,5... | collective-permute-start | bytes 294920 | tf_op jit(solution)/shard_map/ppermute | solution.py:605
  125.9 1.8 %collective-permute-start.29 = (bf16[2,192,128]{2,1,0:T(8,128)(2,1)S(1)}, bf16[2,192,128]{2,1,0:T(8,128)(2,1)S(1)}, u32[]{:S(2)}, u32[]{:S(2)}) collective-permute-start(bf16[2,192,128]{2,1,0:T(8,128)(2,1)S(1)} %get-tuple-element.121), channel_id=1, source_target_pairs={{1,0},{0,1},{17,2},{16,3},{3,16},{2,17},{19,18},{18,19},{5,4},{4,5... | collective-permute-start | bytes 294920 | tf_op jit(solution)/shard_map/ppermute | solution.py:605
  127.7 2.4 %collective-permute-start.31 = (bf16[2,192,128]{2,1,0:T(8,128)(2,1)S(1)}, bf16[2,192,128]{2,1,0:T(8,128)(2,1)S(1)}, u32[]{:S(2)}, u32[]{:S(2)}) collective-permute-start(bf16[2,192,128]{2,1,0:T(8,128)(2,1)S(1)} %get-tuple-element.123), channel_id=1, source_target_pairs={{17,0},{16,1},{1,2},{0,3},{19,16},{18,17},{3,18},{2,19},{21,4},{20... | collective-permute-start | bytes 294920 | tf_op jit(solution)/shard_map/ppermute | solution.py:605
  130.6 1.2 collective-permute-start.35
  131.9 2.4 %shard_map.264 = (f32[3,3,192,64]{3,2,1,0:T(8,128)S(1)}, f32[3,192,64]{2,1,0:T(8,128)S(1)}, f32[192,768]{1,0:T(8,128)}, f32[192,768]{1,0:T(8,128)}, f32[3,192]{1,0:T(4,128)}, /*index=5*/f32[1,768]{1,0:T(1,128)S(1)}) custom-call(s32[3]{0:T(128)S(1)} %pad_add_fusion.2.scal, bf16[208,2304]{1,0:T(8,128)(2,1)S(1)} %shard_map.263.here, ...), custom_call_target="tpu_custom_call" | custom-call | tf_op jit(solution)/shard_map/pallas_call | solution.py:92
  134.3 1.9 %collective-permute-done.30 = bf16[2,192,128]{2,1,0:T(8,128)(2,1)S(1)} collective-permute-done((bf16[2,192,128]{2,1,0:T(8,128)(2,1)S(1)}, bf16[2,192,128]{2,1,0:T(8,128)(2,1)S(1)}, u32[]{:S(2)}, u32[]{:S(2)}) %collective-permute-start.30) | collective-permute-done | bytes 98336 | tf_op jit(solution)/shard_map/ppermute | solution.py:605
  136.4 1.3 collective-permute-start.36
  137.8 1.1 copy.83
  138.9 0.9 copy.82
  139.8 1.2 reshape.655
  141.0 0.8 reshape.656
  (187 shorter events, 12.4 us)
Async XLA Ops:
  3.6 10.2 %copy-start.12 = (bf16[3,3,12288]{2,1,0:T(4,128)(2,1)S(1)}, bf16[3,3,12288]{2,1,0:T(4,128)(2,1)}, u32[]{:S(2)}) copy-start(bf16[3,3,12288]{2,1,0:T(4,128)(2,1)} %param.17) | copy-start | bytes 663556
  3.8 14.5 %collective-permute-start = (bf16[400,128]{1,0:T(8,128)(2,1)S(1)}, bf16[400,128]{1,0:T(8,128)(2,1)S(1)}, u32[]{:S(2)}, u32[]{:S(2)}) collective-permute-start(bf16[400,128]{1,0:T(8,128)(2,1)S(1)} %broadcast_select_fusion.11), channel_id=1, source_target_pairs={{0,0},{1,1},{2,16},{3,17},{16,2},{17,3},{18,18},{19,19},{4,4},{5,5... | collective-permute-start | bytes 307208 | tf_op jit(solution)/shard_map/ppermute | solution.py:452
  9.4 8.8 %collective-permute-start.2 = (bf16[400,128]{1,0:T(8,128)(2,1)S(1)}, bf16[400,128]{1,0:T(8,128)(2,1)S(1)}, u32[]{:S(2)}, u32[]{:S(2)}) collective-permute-start(bf16[400,128]{1,0:T(8,128)(2,1)S(1)} %broadcast_select_fusion.9), channel_id=1, source_target_pairs={{0,16},{1,17},{2,0},{3,1},{16,18},{17,19},{18,2},{19,3},{4,20},{5,... | collective-permute-start | bytes 307208 | tf_op jit(solution)/shard_map/ppermute | solution.py:452
  9.6 8.7 %collective-permute-start.3 = (bf16[400,128]{1,0:T(8,128)(2,1)S(1)}, bf16[400,128]{1,0:T(8,128)(2,1)S(1)}, u32[]{:S(2)}, u32[]{:S(2)}) collective-permute-start(bf16[400,128]{1,0:T(8,128)(2,1)S(1)} %broadcast_select_fusion.8), channel_id=1, source_target_pairs={{0,17},{1,16},{2,1},{3,0},{16,19},{17,18},{18,3},{19,2},{4,21},{5,... | collective-permute-start | bytes 307208 | tf_op jit(solution)/shard_map/ppermute | solution.py:452
  10.8 4.1 %copy-start.19 = (bf16[192]{0:T(256)(128)(2,1)S(1)}, bf16[192]{0:T(256)(128)(2,1)}, u32[]{:S(2)}) copy-start(bf16[192]{0:T(256)(128)(2,1)} %param.22) | copy-start | bytes 1156
  10.8 7.5 %collective-permute-start.1 = (bf16[400,128]{1,0:T(8,128)(2,1)S(1)}, bf16[400,128]{1,0:T(8,128)(2,1)S(1)}, u32[]{:S(2)}, u32[]{:S(2)}) collective-permute-start(bf16[400,128]{1,0:T(8,128)(2,1)S(1)} %broadcast_select_fusion.10), channel_id=1, source_target_pairs={{0,1},{1,0},{2,17},{3,16},{16,3},{17,2},{18,19},{19,18},{4,5},{5,4... | collective-permute-start | bytes 307208 | tf_op jit(solution)/shard_map/ppermute | solution.py:452
  18.1 56.0 %copy-start = (bf16[208,1536]{1,0:T(8,128)(2,1)}, bf16[208,1536]{1,0:T(8,128)(2,1)S(1)}, u32[]{:S(2)}) copy-start(bf16[208,1536]{1,0:T(8,128)(2,1)S(1)} %pad_maximum_fusion.refs_0_.refs_4_.own2) | copy-start | bytes 1916932
  18.4 19.6 %collective-permute-start.10 = (bf16[4,2,192,128]{3,2,1,0:T(8,128)(2,1)S(1)}, bf16[4,2,192,128]{3,2,1,0:T(8,128)(2,1)S(1)}, u32[]{:S(2)}, u32[]{:S(2)}) collective-permute-start(bf16[4,2,192,128]{3,2,1,0:T(8,128)(2,1)S(1)} %pad_maximum_fusion.1.refs_0_.x_ref), channel_id=1, source_target_pairs={{0,8},{4,12},{8,0},{12,4},{1,9},{5,13},{9,1},{13,5},{2,10},{6,14},... | collective-permute-start | bytes 1179656 | tf_op jit(solution)/shard_map/ppermute | solution.py:30
  19.7 20.6 %collective-permute-start.11 = (bf16[4,2,192,128]{3,2,1,0:T(8,128)(2,1)S(1)}, bf16[4,2,192,128]{3,2,1,0:T(8,128)(2,1)S(1)}, u32[]{:S(2)}, u32[]{:S(2)}) collective-permute-start(bf16[4,2,192,128]{3,2,1,0:T(8,128)(2,1)S(1)} %pad_maximum_fusion.1.refs_0_.x_ref), channel_id=1, source_target_pairs={{0,12},{4,8},{8,4},{12,0},{1,13},{5,9},{9,5},{13,1},{2,14},{6,10},... | collective-permute-start | bytes 1179656 | tf_op jit(solution)/shard_map/ppermute | solution.py:30
  20.8 19.4 %collective-permute-start.9 = (bf16[4,2,192,128]{3,2,1,0:T(8,128)(2,1)S(1)}, bf16[4,2,192,128]{3,2,1,0:T(8,128)(2,1)S(1)}, u32[]{:S(2)}, u32[]{:S(2)}) collective-permute-start(bf16[4,2,192,128]{3,2,1,0:T(8,128)(2,1)S(1)} %pad_maximum_fusion.1.refs_0_.x_ref), channel_id=1, source_target_pairs={{0,4},{4,0},{8,12},{12,8},{1,5},{5,1},{9,13},{13,9},{2,6},{6,2},{1... | collective-permute-start | bytes 1179656 | tf_op jit(solution)/shard_map/ppermute | solution.py:30
  21.1 15.6 %collective-permute-start.4 = (bf16[208,768]{1,0:T(8,128)(2,1)S(1)}, bf16[208,768]{1,0:T(8,128)(2,1)S(1)}, u32[]{:S(2)}, u32[]{:S(2)}) collective-permute-start(bf16[208,768]{1,0:T(8,128)(2,1)S(1)} %pad_maximum_fusion.2.refs_0_.own1), channel_id=1, source_target_pairs={{0,3},{1,2},{2,1},{3,0},{16,18},{17,19},{18,16},{19,17},{4,7},{5,6... | collective-permute-start | bytes 958472 | tf_op jit(solution)/shard_map/ppermute | solution.py:38
  23.2 18.4 %collective-permute-start.6 = (bf16[208,768]{1,0:T(8,128)(2,1)S(1)}, bf16[208,768]{1,0:T(8,128)(2,1)S(1)}, u32[]{:S(2)}, u32[]{:S(2)}) collective-permute-start(bf16[208,768]{1,0:T(8,128)(2,1)S(1)} %pad_maximum_fusion.2.refs_0_.own1), channel_id=1, source_target_pairs={{0,1},{1,0},{2,3},{3,2},{4,5},{5,4},{6,7},{7,6},{8,9},{9,8},{10,11... | collective-permute-start | bytes 958472 | tf_op jit(solution)/shard_map/ppermute | solution.py:30
  36.7 4.9 %collective-permute-start.5 = (bf16[208,768]{1,0:T(8,128)(2,1)S(1)}, bf16[208,768]{1,0:T(8,128)(2,1)S(1)}, u32[]{:S(2)}, u32[]{:S(2)}) collective-permute-start(bf16[208,768]{1,0:T(8,128)(2,1)S(1)} %collective-permute-done.4.refs_1_), channel_id=1, source_target_pairs={{0,16},{16,0},{1,17},{17,1},{2,18},{18,2},{3,19},{19,3},{4,20},{20... | collective-permute-start | bytes 958472 | tf_op jit(solution)/shard_map/ppermute | solution.py:30
  38.0 29.6 %collective-permute-start.7 = (bf16[208,1536]{1,0:T(8,128)(2,1)S(1)}, bf16[208,1536]{1,0:T(8,128)(2,1)S(1)}, u32[]{:S(2)}, u32[]{:S(2)}) collective-permute-start(bf16[208,1536]{1,0:T(8,128)(2,1)S(1)} %pad_maximum_fusion.refs_0_.refs_4_.own2), channel_id=1, source_target_pairs={{0,3},{1,2},{2,1},{3,0},{16,18},{17,19},{18,16},{19,17},{4,7},{5,6... | collective-permute-start | bytes 1916936 | tf_op jit(solution)/shard_map/ppermute | solution.py:38
  41.6 16.5 %copy-start.2 = (bf16[832,512]{1,0:T(8,128)(2,1)}, bf16[832,512]{1,0:T(8,128)(2,1)S(1)}, u32[]{:S(2)}) copy-start(bf16[832,512]{1,0:T(8,128)(2,1)S(1)} %get-tuple-element.97.xn) | copy-start | bytes 2555908
  43.5 1.7 %collective-permute-start.12 = (bf16[1,3,64,512]{3,2,1,0:T(8,128)(2,1)S(1)}, bf16[1,3,64,512]{3,2,1,0:T(8,128)(2,1)S(1)}, u32[]{:S(2)}, u32[]{:S(2)}) collective-permute-start(bf16[1,3,64,512]{3,2,1,0:T(8,128)(2,1)S(1)} %get-tuple-element.209), channel_id=1, source_target_pairs={{0,16},{16,0},{1,17},{17,1},{2,18},{18,2},{3,19},{19,3},{4,20},{20... | collective-permute-start | bytes 589832 | tf_op jit(solution)/shard_map/ppermute | solution.py:30
  44.1 1.4 %collective-permute-start.13 = (bf16[1,3,64,512]{3,2,1,0:T(8,128)(2,1)S(1)}, bf16[1,3,64,512]{3,2,1,0:T(8,128)(2,1)S(1)}, u32[]{:S(2)}, u32[]{:S(2)}) collective-permute-start(bf16[1,3,64,512]{3,2,1,0:T(8,128)(2,1)S(1)} %get-tuple-element.208), channel_id=1, source_target_pairs={{0,16},{16,0},{1,17},{17,1},{2,18},{18,2},{3,19},{19,3},{4,20},{20... | collective-permute-start | bytes 589832 | tf_op jit(solution)/shard_map/ppermute | solution.py:30
  44.2 26.7 %collective-permute-start.8 = (bf16[208,1536]{1,0:T(8,128)(2,1)S(1)}, bf16[208,1536]{1,0:T(8,128)(2,1)S(1)}, u32[]{:S(2)}, u32[]{:S(2)}) collective-permute-start(bf16[208,1536]{1,0:T(8,128)(2,1)S(1)} %pad_maximum_fusion.refs_0_.refs_4_.own2), channel_id=1, source_target_pairs={{0,1},{1,0},{2,3},{3,2},{4,5},{5,4},{6,7},{7,6},{8,9},{9,8},{10,11... | collective-permute-start | bytes 1916936 | tf_op jit(solution)/shard_map/ppermute | solution.py:30
  56.3 1.5 %collective-permute-start.14 = (bf16[1,3,64,512]{3,2,1,0:T(8,128)(2,1)S(1)}, bf16[1,3,64,512]{3,2,1,0:T(8,128)(2,1)S(1)}, u32[]{:S(2)}, u32[]{:S(2)}) collective-permute-start(bf16[1,3,64,512]{3,2,1,0:T(8,128)(2,1)S(1)} %get-tuple-element.207), channel_id=1, source_target_pairs={{0,16},{16,0},{1,17},{17,1},{2,18},{18,2},{3,19},{19,3},{4,20},{20... | collective-permute-start | bytes 589832 | tf_op jit(solution)/shard_map/ppermute | solution.py:30
  56.6 1.4 %collective-permute-start.15 = (bf16[1,3,64,512]{3,2,1,0:T(8,128)(2,1)S(1)}, bf16[1,3,64,512]{3,2,1,0:T(8,128)(2,1)S(1)}, u32[]{:S(2)}, u32[]{:S(2)}) collective-permute-start(bf16[1,3,64,512]{3,2,1,0:T(8,128)(2,1)S(1)} %get-tuple-element.206), channel_id=1, source_target_pairs={{0,16},{16,0},{1,17},{17,1},{2,18},{18,2},{3,19},{19,3},{4,20},{20... | collective-permute-start | bytes 589832 | tf_op jit(solution)/shard_map/ppermute | solution.py:30
  67.6 12.7 %copy-start.4 = (bf16[208,1536]{1,0:T(8,128)(2,1)}, bf16[208,1536]{1,0:T(8,128)(2,1)S(1)}, u32[]{:S(2)}) copy-start(bf16[208,1536]{1,0:T(8,128)(2,1)S(1)} %collective-permute-done.7.refs_1_.refs_5_) | copy-start | bytes 1916932
  70.9 9.3 %copy-start.5 = (bf16[208,1536]{1,0:T(8,128)(2,1)}, bf16[208,1536]{1,0:T(8,128)(2,1)S(1)}, u32[]{:S(2)}) copy-start(bf16[208,1536]{1,0:T(8,128)(2,1)S(1)} %collective-permute-done.8.refs_3_.refs_7_) | copy-start | bytes 1916932
  70.9 3.1 %collective-permute-start.16 = (bf16[208,1536]{1,0:T(8,128)(2,1)S(1)}, bf16[208,1536]{1,0:T(8,128)(2,1)S(1)}, u32[]{:S(2)}, u32[]{:S(2)}) collective-permute-start(bf16[208,1536]{1,0:T(8,128)(2,1)S(1)} %collective-permute-done.7.refs_1_.refs_5_), channel_id=1, source_target_pairs={{0,16},{16,0},{1,17},{17,1},{2,18},{18,2},{3,19},{19,3},{4,20},{20... | collective-permute-start | bytes 1916936 | tf_op jit(solution)/shard_map/ppermute | solution.py:30
  71.8 2.2 %collective-permute-start.17 = (bf16[208,768]{1,0:T(8,128)(2,1)S(1)}, bf16[208,768]{1,0:T(8,128)(2,1)S(1)}, u32[]{:S(2)}, u32[]{:S(2)}) collective-permute-start(bf16[208,768]{1,0:T(8,128)(2,1)S(1)} %get-tuple-element.96), channel_id=1, source_target_pairs={{0,16},{16,0},{1,17},{17,1},{2,18},{18,2},{3,19},{19,3},{4,20},{20... | collective-permute-start | bytes 958472 | tf_op jit(solution)/shard_map/ppermute | solution.py:30
  71.8 16.6 %collective-permute-start.19 = (bf16[208,768]{1,0:T(8,128)(2,1)S(1)}, bf16[208,768]{1,0:T(8,128)(2,1)S(1)}, u32[]{:S(2)}, u32[]{:S(2)}) collective-permute-start(bf16[208,768]{1,0:T(8,128)(2,1)S(1)} %get-tuple-element.106), channel_id=1, source_target_pairs={{0,1},{1,0},{2,3},{3,2},{4,5},{5,4},{6,7},{7,6},{8,9},{9,8},{10,11... | collective-permute-start | bytes 958472 | tf_op jit(solution)/shard_map/ppermute | solution.py:30
  74.0 16.5 %collective-permute-start.18 = (bf16[208,768]{1,0:T(8,128)(2,1)S(1)}, bf16[208,768]{1,0:T(8,128)(2,1)S(1)}, u32[]{:S(2)}, u32[]{:S(2)}) collective-permute-start(bf16[208,768]{1,0:T(8,128)(2,1)S(1)} %shard_map.258), channel_id=1, source_target_pairs={{0,3},{1,2},{2,1},{3,0},{16,18},{17,19},{18,16},{19,17},{4,7},{5,6... | collective-permute-start | bytes 958472 | tf_op jit(solution)/shard_map/ppermute | solution.py:38
  74.1 6.2 %copy-start.6 = (bf16[208,1536]{1,0:T(8,128)(2,1)}, bf16[208,1536]{1,0:T(8,128)(2,1)S(1)}, u32[]{:S(2)}) copy-start(bf16[208,1536]{1,0:T(8,128)(2,1)S(1)} %collective-permute-done.16.refs_2_.refs_6_) | copy-start | bytes 1916932
  80.3 7.8 %collective-permute-start.23 = (bf16[208,512]{1,0:T(8,128)(2,1)S(1)}, bf16[208,512]{1,0:T(8,128)(2,1)S(1)}, u32[]{:S(2)}, u32[]{:S(2)}) collective-permute-start(bf16[208,512]{1,0:T(8,128)(2,1)S(1)} %get-tuple-element.197), channel_id=1, source_target_pairs={{0,16},{16,0},{1,17},{17,1},{2,18},{18,2},{3,19},{19,3},{4,20},{20... | collective-permute-start | bytes 638984 | tf_op jit(solution)/shard_map/ppermute | solution.py:30
  82.2 5.9 %collective-permute-start.24 = (bf16[208,512]{1,0:T(8,128)(2,1)S(1)}, bf16[208,512]{1,0:T(8,128)(2,1)S(1)}, u32[]{:S(2)}, u32[]{:S(2)}) collective-permute-start(bf16[208,512]{1,0:T(8,128)(2,1)S(1)} %get-tuple-element.196), channel_id=1, source_target_pairs={{0,16},{16,0},{1,17},{17,1},{2,18},{18,2},{3,19},{19,3},{4,20},{20... | collective-permute-start | bytes 638984 | tf_op jit(solution)/shard_map/ppermute | solution.py:30
  82.3 5.8 %collective-permute-start.25 = (bf16[208,512]{1,0:T(8,128)(2,1)S(1)}, bf16[208,512]{1,0:T(8,128)(2,1)S(1)}, u32[]{:S(2)}, u32[]{:S(2)}) collective-permute-start(bf16[208,512]{1,0:T(8,128)(2,1)S(1)} %get-tuple-element.195), channel_id=1, source_target_pairs={{0,16},{16,0},{1,17},{17,1},{2,18},{18,2},{3,19},{19,3},{4,20},{20... | collective-permute-start | bytes 638984 | tf_op jit(solution)/shard_map/ppermute | solution.py:30
  88.1 6.5 %copy-start.8 = (bf16[192,2,256]{2,1,0:T(2,128)(2,1)S(1)}, bf16[192,2,256]{2,1,0:T(2,128)(2,1)}, u32[]{:S(2)}) copy-start(bf16[192,2,256]{2,1,0:T(2,128)(2,1)} %param.29) | copy-start | bytes 589828
  88.3 31.7 %copy-start.7 = (f32[208,1536]{1,0:T(8,128)S(1)}, f32[208,1536]{1,0:T(8,128)}, u32[]{:S(2)}) copy-start(f32[208,1536]{1,0:T(8,128)} %get-tuple-element.127.own2) | copy-start | bytes 3833860
  90.4 29.5 %collective-permute-start.26 = (bf16[208,1536]{1,0:T(8,128)(2,1)S(1)}, bf16[208,1536]{1,0:T(8,128)(2,1)S(1)}, u32[]{:S(2)}, u32[]{:S(2)}) collective-permute-start(bf16[208,1536]{1,0:T(8,128)(2,1)S(1)} %shard_map.262), channel_id=1, source_target_pairs={{0,3},{1,2},{2,1},{3,0},{16,18},{17,19},{18,16},{19,17},{4,7},{5,6... | collective-permute-start | bytes 1916936 | tf_op jit(solution)/shard_map/ppermute | solution.py:38
  90.4 29.5 %collective-permute-start.27 = (bf16[208,1536]{1,0:T(8,128)(2,1)S(1)}, bf16[208,1536]{1,0:T(8,128)(2,1)S(1)}, u32[]{:S(2)}, u32[]{:S(2)}) collective-permute-start(bf16[208,1536]{1,0:T(8,128)(2,1)S(1)} %get-tuple-element.119), channel_id=1, source_target_pairs={{0,1},{1,0},{2,3},{3,2},{4,5},{5,4},{6,7},{7,6},{8,9},{9,8},{10,11... | collective-permute-start | bytes 1916936 | tf_op jit(solution)/shard_map/ppermute | solution.py:30
  91.9 10.9 %collective-permute-start.20 = (bf16[4,2,192,128]{3,2,1,0:T(8,128)(2,1)S(1)}, bf16[4,2,192,128]{3,2,1,0:T(8,128)(2,1)S(1)}, u32[]{:S(2)}, u32[]{:S(2)}) collective-permute-start(bf16[4,2,192,128]{3,2,1,0:T(8,128)(2,1)S(1)} %get-tuple-element.108), channel_id=1, source_target_pairs={{0,4},{4,0},{8,12},{12,8},{1,5},{5,1},{9,13},{13,9},{2,6},{6,2},{1... | collective-permute-start | bytes 1179656 | tf_op jit(solution)/shard_map/ppermute | solution.py:30
  93.1 18.0 %collective-permute-start.21 = (bf16[4,2,192,128]{3,2,1,0:T(8,128)(2,1)S(1)}, bf16[4,2,192,128]{3,2,1,0:T(8,128)(2,1)S(1)}, u32[]{:S(2)}, u32[]{:S(2)}) collective-permute-start(bf16[4,2,192,128]{3,2,1,0:T(8,128)(2,1)S(1)} %get-tuple-element.109), channel_id=1, source_target_pairs={{0,8},{4,12},{8,0},{12,4},{1,9},{5,13},{9,1},{13,5},{2,10},{6,14},... | collective-permute-start | bytes 1179656 | tf_op jit(solution)/shard_map/ppermute | solution.py:30
  94.4 17.9 %collective-permute-start.22 = (bf16[4,2,192,128]{3,2,1,0:T(8,128)(2,1)S(1)}, bf16[4,2,192,128]{3,2,1,0:T(8,128)(2,1)S(1)}, u32[]{:S(2)}, u32[]{:S(2)}) collective-permute-start(bf16[4,2,192,128]{3,2,1,0:T(8,128)(2,1)S(1)} %get-tuple-element.110), channel_id=1, source_target_pairs={{0,12},{4,8},{8,4},{12,0},{1,13},{5,9},{9,5},{13,1},{2,14},{6,10},... | collective-permute-start | bytes 1179656 | tf_op jit(solution)/shard_map/ppermute | solution.py:30
  120.7 2.6 %copy-start.16 = (bf16[192]{0:T(256)(128)(2,1)S(1)}, bf16[192]{0:T(256)(128)(2,1)}, u32[]{:S(2)}) copy-start(bf16[192]{0:T(256)(128)(2,1)} %param.28) | copy-start | bytes 1156
  120.7 9.4 %copy-start.1 = (bf16[208,1536]{1,0:T(8,128)(2,1)S(1)}, bf16[208,1536]{1,0:T(8,128)(2,1)}, u32[]{:S(2)}) copy-start(bf16[208,1536]{1,0:T(8,128)(2,1)} %copy-done) | copy-start | bytes 1916932
  121.7 6.0 %collective-permute-start.32 = (bf16[208,768]{1,0:T(8,128)(2,1)}, bf16[208,768]{1,0:T(8,128)(2,1)S(1)}, u32[]{:S(2)}, u32[]{:S(2)}) collective-permute-start(bf16[208,768]{1,0:T(8,128)(2,1)} %get-tuple-element.192), channel_id=1, source_target_pairs={{0,16},{16,0},{1,17},{17,1},{2,18},{18,2},{3,19},{19,3},{4,20},{20... | collective-permute-start | bytes 958472 | tf_op jit(solution)/shard_map/ppermute | solution.py:30
  122.7 5.0 %collective-permute-start.33 = (bf16[208,768]{1,0:T(8,128)(2,1)}, bf16[208,768]{1,0:T(8,128)(2,1)S(1)}, u32[]{:S(2)}, u32[]{:S(2)}) collective-permute-start(bf16[208,768]{1,0:T(8,128)(2,1)} %get-tuple-element.191), channel_id=1, source_target_pairs={{0,16},{16,0},{1,17},{17,1},{2,18},{18,2},{3,19},{19,3},{4,20},{20... | collective-permute-start | bytes 958472 | tf_op jit(solution)/shard_map/ppermute | solution.py:30
  122.7 7.4 %collective-permute-start.34 = (bf16[208,768]{1,0:T(8,128)(2,1)}, bf16[208,768]{1,0:T(8,128)(2,1)S(1)}, u32[]{:S(2)}, u32[]{:S(2)}) collective-permute-start(bf16[208,768]{1,0:T(8,128)(2,1)} %get-tuple-element.190), channel_id=1, source_target_pairs={{0,16},{16,0},{1,17},{17,1},{2,18},{18,2},{3,19},{19,3},{4,20},{20... | collective-permute-start | bytes 958472 | tf_op jit(solution)/shard_map/ppermute | solution.py:30
  123.3 11.0 %collective-permute-start.28 = (bf16[2,192,128]{2,1,0:T(8,128)(2,1)S(1)}, bf16[2,192,128]{2,1,0:T(8,128)(2,1)S(1)}, u32[]{:S(2)}, u32[]{:S(2)}) collective-permute-start(bf16[2,192,128]{2,1,0:T(8,128)(2,1)S(1)} %get-tuple-element.120), channel_id=1, source_target_pairs={{0,0},{1,1},{16,2},{17,3},{2,16},{3,17},{18,18},{19,19},{4,4},{5,5... | collective-permute-start | bytes 294920 | tf_op jit(solution)/shard_map/ppermute | solution.py:605
  125.9 8.4 %collective-permute-start.29 = (bf16[2,192,128]{2,1,0:T(8,128)(2,1)S(1)}, bf16[2,192,128]{2,1,0:T(8,128)(2,1)S(1)}, u32[]{:S(2)}, u32[]{:S(2)}) collective-permute-start(bf16[2,192,128]{2,1,0:T(8,128)(2,1)S(1)} %get-tuple-element.121), channel_id=1, source_target_pairs={{1,0},{0,1},{17,2},{16,3},{3,16},{2,17},{19,18},{18,19},{5,4},{4,5... | collective-permute-start | bytes 294920 | tf_op jit(solution)/shard_map/ppermute | solution.py:605
  127.7 8.5 %collective-permute-start.30 = (bf16[2,192,128]{2,1,0:T(8,128)(2,1)S(1)}, bf16[2,192,128]{2,1,0:T(8,128)(2,1)S(1)}, u32[]{:S(2)}, u32[]{:S(2)}) collective-permute-start(bf16[2,192,128]{2,1,0:T(8,128)(2,1)S(1)} %get-tuple-element.122), channel_id=1, source_target_pairs={{16,0},{17,1},{0,2},{1,3},{18,16},{19,17},{2,18},{3,19},{20,4},{21... | collective-permute-start | bytes 294920 | tf_op jit(solution)/shard_map/ppermute | solution.py:605
  127.7 8.5 %collective-permute-start.31 = (bf16[2,192,128]{2,1,0:T(8,128)(2,1)S(1)}, bf16[2,192,128]{2,1,0:T(8,128)(2,1)S(1)}, u32[]{:S(2)}, u32[]{:S(2)}) collective-permute-start(bf16[2,192,128]{2,1,0:T(8,128)(2,1)S(1)} %get-tuple-element.123), channel_id=1, source_target_pairs={{17,0},{16,1},{1,2},{0,3},{19,16},{18,17},{3,18},{2,19},{21,4},{20... | collective-permute-start | bytes 294920 | tf_op jit(solution)/shard_map/ppermute | solution.py:605
  130.6 5.7 %collective-permute-start.35 = (f32[8,192]{1,0:T(8,128)S(1)}, f32[8,192]{1,0:T(8,128)S(1)}, u32[]{:S(2)}, u32[]{:S(2)}) collective-permute-start(f32[8,192]{1,0:T(8,128)S(1)} %shard_map.265), channel_id=1, source_target_pairs={{0,4},{4,0},{8,12},{12,8},{1,5},{5,1},{9,13},{13,9},{2,6},{6,2},{1... | collective-permute-start | bytes 18440 | tf_op jit(solution)/shard_map/ppermute | solution.py:30
  136.4 6.0 %collective-permute-start.36 = (f32[8,192]{1,0:T(8,128)S(1)}, f32[8,192]{1,0:T(8,128)S(1)}, u32[]{:S(2)}, u32[]{:S(2)}) collective-permute-start(f32[8,192]{1,0:T(8,128)S(1)} %add.183), channel_id=1, source_target_pairs={{0,8},{4,12},{8,0},{12,4},{1,9},{5,13},{9,1},{13,5},{2,10},{6,14},... | collective-permute-start | bytes 18440 | tf_op jit(solution)/shard_map/ppermute | solution.py:30
  (11 other events, 15.4 us)

commit v5 on v4

--- a/solution.py
+++ b/solution.py
@@ -84,7 +84,7 @@
     return jnp.concatenate([columns.astype(bf16), rows], axis=0)
 
 
-def call(kernel, outs, args, scalars=None, cost=0):
+def call(kernel, outs, args, scalars=None, scratch=()):
     specs = [pl.BlockSpec(memory_space=pltpu.VMEM) for _ in args]
     if scalars is not None:
         specs = [pl.BlockSpec(memory_space=pltpu.SMEM)] + specs
@@ -95,7 +95,8 @@
         in_specs=specs,
         out_specs=[pl.BlockSpec(memory_space=pltpu.VMEM) for _ in outs],
         compiler_params=pltpu.CompilerParams(vmem_limit_bytes=48 * 2**20),
-        cost_estimate=pl.CostEstimate(flops=cost, bytes_accessed=0, transcendentals=0),
+        scratch_shapes=list(scratch),
+        cost_estimate=pl.CostEstimate(flops=0, bytes_accessed=0, transcendentals=0),
     )(*args)
 
 
@@ -290,21 +291,19 @@
 
 
 def back_kernel(scal, *refs):
-    w1, w2, acts, outs = refs[:4], refs[4:8], refs[8:16], refs[16:]
+    w1, w2, acts, outs, held = refs[:4], refs[4:8], refs[8:16], refs[16:-1], refs[-1]
     part = acts[4].shape[0]
-    rows, (_, _, width, span) = len(outs), outs[0].shape
+    _, _, width, span = outs[0].shape
     row, core = scal[0], scal[1]
     for i, to in enumerate((0, 3 - core, 2 + core, 1)):
         for way in range(2):
             side = slice((1 - way) * part, (2 - way) * part)
-            total = sum(dot10(weight(w1, i, u), acts[2 * way + u][...]) for u in range(2))
+            used = slice(2 * 128 * (1 - way), acts[0].shape[0])
+            total = sum(dot10(weight(w1, i, u)[:, used], acts[2 * way + u][used, :]) for u in range(2))
             total += sum(dot10(weight(w2, i, u)[:, side], acts[4 + 2 * way + u][...]) for u in range(2))
-            total = total[:width].astype(bf16)
+            held[way] = total[:width].astype(bf16)
             for j, out in enumerate(outs):
-                value = total[:, :span]
-                for rr in range(1, rows):
-                    value = jnp.where((row ^ j) == rr, total[:, rr * span : (rr + 1) * span], value)
-                out[to, way] = value
+                out[to, way] = held[way, :, pl.ds(pl.multiple_of((row ^ j) * span, span), span)]
 
 
 def pair_kernel(keep, *refs):
@@ -593,6 +592,7 @@
         [strip] * rows,
         [*w1, *w2, att_a, att_b, grads_a, grads_b, up_a, up_b, hid_a, hid_b],
         scalars,
+        scratch=[pltpu.VMEM((2, width, count), bf16)],
     )
     low_near2, far_sum2 = after([low_near2, far_sum2], [sum_near1, sum_far1, sums[0]])
     sum_near2 = send_near(low_near2)

time: 143 us -> 143 us (level)
  no operation moved by 1% of the time
where the time goes in v5:
time: 143 us
  waiting for transfers between devices  53.5 us (37%)
  starting transfers between devices  37 us (26%)
  Pallas kernels  33.5 us (23%)
  local copies, waits for them, and re-layouts  11.6 us (8%)
  between operations  4.21 us (3%)
  other arithmetic  3.39 us (2%)
    ppermute x25, waiting for transfers between devices, send(): return lax.ppermute(x, axis, xor_peers(axis, shift))  26.5 us
    ppermute x4, waiting for transfers between devices, send_near(): return lax.ppermute(x, ('dp', 'col'), pairs)  25.1 us
    pallas_call x11, Pallas kernels, call(): pl.pallas_call(kernel, out_shape=outs, in_specs=specs, out_specs=[pl.Bloc...  22.8 us
    ppermute x25, starting transfers between devices, send(): return lax.ppermute(x, axis, xor_peers(axis, shift))  16 us
    pallas_call x1, Pallas kernels, body(): pl.pallas_call(partial(attention_kernel, span), grid=(heads,), in_specs=[...  10.6 us
    ppermute x4, starting transfers between devices, body(): lax.ppermute(sent[k], ('dp', 'col'), spread_peers(k))  9.72 us
    ppermute x4, starting transfers between devices, body(): lax.ppermute(back[k], ('dp', 'col'), spread_peers(k, True))  6.76 us
    ppermute x4, starting transfers between devices, send_near(): return lax.ppermute(x, ('dp', 'col'), pairs)  4.44 us
  transfers between devices with their start and end apart: 37, of which 15 were waited for; matrix products, arithmetic and copies ran while one was open for 7% of the time, Pallas kernels for 23%

profile of v5, /device:TPU:1, one launch (start us, length us, event | category | flops | bytes accessed | tf_op | source)
XLA Modules:
  0.0 143.0 jit_solution(10618768794686530833)
XLA Ops:
  0.6 0.8 fusion.23
  1.7 1.0 copy.64
  2.6 1.0 copy.66
  3.8 5.6 %collective-permute-start = (bf16[400,128]{1,0:T(8,128)(2,1)S(1)}, bf16[400,128]{1,0:T(8,128)(2,1)S(1)}, u32[]{:S(2)}, u32[]{:S(2)}) collective-permute-start(bf16[400,128]{1,0:T(8,128)(2,1)S(1)} %broadcast_select_fusion.11), channel_id=1, source_target_pairs={{0,0},{1,1},{2,16},{3,17},{16,2},{17,3},{18,18},{19,19},{4,4},{5,5... | collective-permute-start | bytes 307208 | tf_op jit(solution)/shard_map/ppermute | solution.py:451
  9.6 1.2 collective-permute-start.3
  10.8 2.9 %collective-permute-start.1 = (bf16[400,128]{1,0:T(8,128)(2,1)S(1)}, bf16[400,128]{1,0:T(8,128)(2,1)S(1)}, u32[]{:S(2)}, u32[]{:S(2)}) collective-permute-start(bf16[400,128]{1,0:T(8,128)(2,1)S(1)} %broadcast_select_fusion.10), channel_id=1, source_target_pairs={{0,1},{1,0},{2,17},{3,16},{16,3},{17,2},{18,19},{19,18},{4,5},{5,4... | collective-permute-start | bytes 307208 | tf_op jit(solution)/shard_map/ppermute | solution.py:451
  18.4 1.3 collective-permute-start.10
  19.7 1.2 collective-permute-start.11
  21.1 2.1 %collective-permute-start.4 = (bf16[208,768]{1,0:T(8,128)(2,1)S(1)}, bf16[208,768]{1,0:T(8,128)(2,1)S(1)}, u32[]{:S(2)}, u32[]{:S(2)}) collective-permute-start(bf16[208,768]{1,0:T(8,128)(2,1)S(1)} %pad_maximum_fusion.2.refs_0_.own1), channel_id=1, source_target_pairs={{0,3},{1,2},{2,1},{3,0},{16,18},{17,19},{18,16},{19,17},{4,7},{5,6... | collective-permute-start | bytes 958472 | tf_op jit(solution)/shard_map/ppermute | solution.py:38
  26.7 10.0 %collective-permute-done.4.refs_1_ = bf16[208,768]{1,0:T(8,128)(2,1)S(1)} collective-permute-done((bf16[208,768]{1,0:T(8,128)(2,1)S(1)}, bf16[208,768]{1,0:T(8,128)(2,1)S(1)}, u32[]{:S(2)}, u32[]{:S(2)}) %collective-permute-start.4) | collective-permute-done | bytes 319520 | tf_op jit(solution)/shard_map/ppermute | solution.py:38
  36.9 1.1 collective-permute-done.10.refs_2_
  38.0 2.3 %collective-permute-start.7 = (bf16[208,1536]{1,0:T(8,128)(2,1)S(1)}, bf16[208,1536]{1,0:T(8,128)(2,1)S(1)}, u32[]{:S(2)}, u32[]{:S(2)}) collective-permute-start(bf16[208,1536]{1,0:T(8,128)(2,1)S(1)} %pad_maximum_fusion.refs_0_.refs_4_.own2), channel_id=1, source_target_pairs={{0,3},{1,2},{2,1},{3,0},{16,18},{17,19},{18,16},{19,17},{4,7},{5,6... | collective-permute-start | bytes 1916936 | tf_op jit(solution)/shard_map/ppermute | solution.py:38
  40.3 1.3 shard_map.254
  41.6 1.8 %shard_map.255 = (bf16[3,64,512]{2,1,0:T(8,128)(2,1)S(1)}, bf16[2,3,64,512]{3,2,1,0:T(8,128)(2,1)S(1)}, bf16[3,64,512]{2,1,0:T(8,128)(2,1)S(1)}) custom-call(s32[3]{0:T(128)S(1)} %pad_add_fusion.2.scal, f32[4,8,512]{2,1,0:T(8,128)S(1)} %pad_maximum_fusion.11.tables, bf16[832,512]{1,0:T(8,128)(2,1)S(1)} %get-tuple-element.97.xn, ...), custom_call_target="tpu_custom_call" | custom-call | tf_op jit(solution)/shard_map/pallas_call | solution.py:92
  44.5 0.7 collective-permute-done.12.k_other
  45.6 10.6 %shard_map.256 = (bf16[3,64,512]{2,1,0:T(8,128)(2,1)S(1)}, f32[3,64,512]{2,1,0:T(8,128)S(1)}, f32[2,3,64,512]{3,2,1,0:T(8,128)S(1)}, bf16[2,3,64,512]{3,2,1,0:T(8,128)(2,1)S(1)}) custom-call(s32[3]{0:T(128)S(1)} %pad_add_fusion.2.scal, s32[1,512]{1,0:T(1,128)S(1)} %compare_select_fusion.1.start, bf16[3,64,512]{2,1,0:T(8,128)(2,1)S(1)} %get-tuple-element.81.q_ref, ...), custom_call_target="tpu_custom_call" | custom-call | tf_op jit(solution)/shard_map/pallas_call | solution.py:531
  56.8 0.9 collective-permute-done.14.gk_other
  58.1 3.4 %shard_map.257 = (bf16[384,512]{1,0:T(8,128)(2,1)S(1)}, bf16[384,512]{1,0:T(8,128)(2,1)S(1)}, bf16[384,512]{1,0:T(8,128)(2,1)S(1)}, bf16[384,512]{1,0:T(8,128)(2...) custom-call(s32[3]{0:T(128)S(1)} %pad_add_fusion.2.scal, ...), custom_call_target="tpu_custom_call" | custom-call | tf_op jit(solution)/shard_map/pallas_call | solution.py:92
  61.4 6.1 %collective-permute-done.7.refs_1_.refs_5_ = bf16[208,1536]{1,0:T(8,128)(2,1)S(1)} collective-permute-done((bf16[208,1536]{1,0:T(8,128)(2,1)S(1)}, bf16[208,1536]{1,0:T(8,128)(2,1)S(1)}, u32[]{:S(2)}, u32[]{:S(2)}) %collective-permute-start.7) | collective-permute-done | bytes 639008 | tf_op jit(solution)/shard_map/ppermute | solution.py:38
  67.6 3.3 %collective-permute-done.8.refs_3_.refs_7_ = bf16[208,1536]{1,0:T(8,128)(2,1)S(1)} collective-permute-done((bf16[208,1536]{1,0:T(8,128)(2,1)S(1)}, bf16[208,1536]{1,0:T(8,128)(2,1)S(1)}, u32[]{:S(2)}, u32[]{:S(2)}) %collective-permute-start.8) | collective-permute-done | bytes 639008 | tf_op jit(solution)/shard_map/ppermute | solution.py:30
  70.9 0.8 collective-permute-start.16
  71.8 2.2 %collective-permute-done.17.refs_0_ = bf16[208,768]{1,0:T(8,128)(2,1)S(1)} collective-permute-done((bf16[208,768]{1,0:T(8,128)(2,1)S(1)}, bf16[208,768]{1,0:T(8,128)(2,1)S(1)}, u32[]{:S(2)}, u32[]{:S(2)}) %collective-permute-start.17) | collective-permute-done | bytes 319520 | tf_op jit(solution)/shard_map/ppermute | solution.py:30
  74.1 6.1 %shard_map.259 = (bf16[384,512]{1,0:T(8,128)(2,1)S(1)}, bf16[384,512]{1,0:T(8,128)(2,1)S(1)}, bf16[384,512]{1,0:T(8,128)(2,1)S(1)}, bf16[384,512]{1,0:T(8,128)(2...) custom-call(s32[3]{0:T(128)S(1)} %pad_add_fusion.2.scal, ...), custom_call_target="tpu_custom_call" | custom-call | tf_op jit(solution)/shard_map/pallas_call | solution.py:92
  80.3 1.9 %collective-permute-start.23 = (bf16[208,512]{1,0:T(8,128)(2,1)S(1)}, bf16[208,512]{1,0:T(8,128)(2,1)S(1)}, u32[]{:S(2)}, u32[]{:S(2)}) collective-permute-start(bf16[208,512]{1,0:T(8,128)(2,1)S(1)} %get-tuple-element.197), channel_id=1, source_target_pairs={{0,16},{16,0},{1,17},{17,1},{2,18},{18,2},{3,19},{19,3},{4,20},{20... | collective-permute-start | bytes 638984 | tf_op jit(solution)/shard_map/ppermute | solution.py:30
  82.7 5.1 %shard_map.260 = (bf16[4,2,192,128]{3,2,1,0:T(8,128)(2,1)S(1)}, bf16[4,2,192,128]{3,2,1,0:T(8,128)(2,1)S(1)}, bf16[4,2,192,128]{3,2,1,0:T(8,128)(2,1)S(1)}, bf16[4,2,192,128]{3,2,1,0:T(8,128)(2,1)S(1)}) custom-call(s32[3]{0:T(128)S(1)} %pad_add_fusion.2.scal, bf16[208,768]{1,0:T(8,128)(2,1)S(1)} %pad_maximum_fusion.2.refs_0_.own1, ...), custom_call_target="tpu_custom_call" | custom-call | tf_op jit(solution)/shard_map/pallas_call | solution.py:92
  88.1 2.4 %collective-permute-done.18.near1 = bf16[208,768]{1,0:T(8,128)(2,1)S(1)} collective-permute-done((bf16[208,768]{1,0:T(8,128)(2,1)S(1)}, bf16[208,768]{1,0:T(8,128)(2,1)S(1)}, u32[]{:S(2)}, u32[]{:S(2)}) %collective-permute-start.18) | collective-permute-done | bytes 319520 | tf_op jit(solution)/shard_map/ppermute | solution.py:38
  90.4 1.5 %collective-permute-start.27 = (bf16[208,1536]{1,0:T(8,128)(2,1)S(1)}, bf16[208,1536]{1,0:T(8,128)(2,1)S(1)}, u32[]{:S(2)}, u32[]{:S(2)}) collective-permute-start(bf16[208,1536]{1,0:T(8,128)(2,1)S(1)} %get-tuple-element.119), channel_id=1, source_target_pairs={{0,1},{1,0},{2,3},{3,2},{4,5},{5,4},{6,7},{7,6},{8,9},{9,8},{10,11... | collective-permute-start | bytes 1916936 | tf_op jit(solution)/shard_map/ppermute | solution.py:30
  91.9 1.2 collective-permute-start.20
  93.1 1.2 collective-permute-start.21
  94.7 8.1 %collective-permute-done.20.refs_1_ = bf16[4,2,192,128]{3,2,1,0:T(8,128)(2,1)S(1)} collective-permute-done((bf16[4,2,192,128]{3,2,1,0:T(8,128)(2,1)S(1)}, bf16[4,2,192,128]{3,2,1,0:T(8,128)(2,1)S(1)}, u32[]{:S(2)}, u32[]{:S(2)}) %collective-permute-start.20) | collective-permute-done | bytes 393248 | tf_op jit(solution)/shard_map/ppermute | solution.py:30
  102.8 8.3 %collective-permute-done.21.refs_2_ = bf16[4,2,192,128]{3,2,1,0:T(8,128)(2,1)S(1)} collective-permute-done((bf16[4,2,192,128]{3,2,1,0:T(8,128)(2,1)S(1)}, bf16[4,2,192,128]{3,2,1,0:T(8,128)(2,1)S(1)}, u32[]{:S(2)}, u32[]{:S(2)}) %collective-permute-start.21) | collective-permute-done | bytes 393248 | tf_op jit(solution)/shard_map/ppermute | solution.py:30
  111.1 1.1 collective-permute-done.22.refs_3_
  112.3 1.1 shard_map.261
  113.4 6.6 %collective-permute-done.26.near2 = bf16[208,1536]{1,0:T(8,128)(2,1)S(1)} collective-permute-done((bf16[208,1536]{1,0:T(8,128)(2,1)S(1)}, bf16[208,1536]{1,0:T(8,128)(2,1)S(1)}, u32[]{:S(2)}, u32[]{:S(2)}) %collective-permute-start.26) | collective-permute-done | bytes 639008 | tf_op jit(solution)/shard_map/ppermute | solution.py:38
  120.0 0.7 shard_map.263.here
  120.8 1.0 fusion.42
  121.7 0.9 collective-permute-start.32
  123.3 2.6 %collective-permute-start.28 = (bf16[2,192,128]{2,1,0:T(8,128)(2,1)S(1)}, bf16[2,192,128]{2,1,0:T(8,128)(2,1)S(1)}, u32[]{:S(2)}, u32[]{:S(2)}) collective-permute-start(bf16[2,192,128]{2,1,0:T(8,128)(2,1)S(1)} %get-tuple-element.120), channel_id=1, source_target_pairs={{0,0},{1,1},{16,2},{17,3},{2,16},{3,17},{18,18},{19,19},{4,4},{5,5... | collective-permute-start | bytes 294920 | tf_op jit(solution)/shard_map/ppermute | solution.py:605
  125.9 1.8 %collective-permute-start.29 = (bf16[2,192,128]{2,1,0:T(8,128)(2,1)S(1)}, bf16[2,192,128]{2,1,0:T(8,128)(2,1)S(1)}, u32[]{:S(2)}, u32[]{:S(2)}) collective-permute-start(bf16[2,192,128]{2,1,0:T(8,128)(2,1)S(1)} %get-tuple-element.121), channel_id=1, source_target_pairs={{1,0},{0,1},{17,2},{16,3},{3,16},{2,17},{19,18},{18,19},{5,4},{4,5... | collective-permute-start | bytes 294920 | tf_op jit(solution)/shard_map/ppermute | solution.py:605
  127.7 2.4 %collective-permute-start.31 = (bf16[2,192,128]{2,1,0:T(8,128)(2,1)S(1)}, bf16[2,192,128]{2,1,0:T(8,128)(2,1)S(1)}, u32[]{:S(2)}, u32[]{:S(2)}) collective-permute-start(bf16[2,192,128]{2,1,0:T(8,128)(2,1)S(1)} %get-tuple-element.123), channel_id=1, source_target_pairs={{17,0},{16,1},{1,2},{0,3},{19,16},{18,17},{3,18},{2,19},{21,4},{20... | collective-permute-start | bytes 294920 | tf_op jit(solution)/shard_map/ppermute | solution.py:605
  130.6 1.2 collective-permute-start.35
  131.9 2.4 %shard_map.264 = (f32[3,3,192,64]{3,2,1,0:T(8,128)S(1)}, f32[3,192,64]{2,1,0:T(8,128)S(1)}, f32[192,768]{1,0:T(8,128)}, f32[192,768]{1,0:T(8,128)}, f32[3,192]{1,0:T(4,128)}, /*index=5*/f32[1,768]{1,0:T(1,128)S(1)}) custom-call(s32[3]{0:T(128)S(1)} %pad_add_fusion.2.scal, bf16[208,2304]{1,0:T(8,128)(2,1)S(1)} %shard_map.263.here, ...), custom_call_target="tpu_custom_call" | custom-call | tf_op jit(solution)/shard_map/pallas_call | solution.py:92
  134.3 1.9 %collective-permute-done.30 = bf16[2,192,128]{2,1,0:T(8,128)(2,1)S(1)} collective-permute-done((bf16[2,192,128]{2,1,0:T(8,128)(2,1)S(1)}, bf16[2,192,128]{2,1,0:T(8,128)(2,1)S(1)}, u32[]{:S(2)}, u32[]{:S(2)}) %collective-permute-start.30) | collective-permute-done | bytes 98336 | tf_op jit(solution)/shard_map/ppermute | solution.py:605
  136.4 1.3 collective-permute-start.36
  137.8 1.1 copy.83
  138.9 0.9 copy.82
  139.8 1.2 reshape.655
  141.0 0.8 reshape.656
  (187 shorter events, 12.4 us)
Async XLA Ops:
  3.6 10.2 %copy-start.12 = (bf16[3,3,12288]{2,1,0:T(4,128)(2,1)S(1)}, bf16[3,3,12288]{2,1,0:T(4,128)(2,1)}, u32[]{:S(2)}) copy-start(bf16[3,3,12288]{2,1,0:T(4,128)(2,1)} %param.17) | copy-start | bytes 663556
  3.8 14.5 %collective-permute-start = (bf16[400,128]{1,0:T(8,128)(2,1)S(1)}, bf16[400,128]{1,0:T(8,128)(2,1)S(1)}, u32[]{:S(2)}, u32[]{:S(2)}) collective-permute-start(bf16[400,128]{1,0:T(8,128)(2,1)S(1)} %broadcast_select_fusion.11), channel_id=1, source_target_pairs={{0,0},{1,1},{2,16},{3,17},{16,2},{17,3},{18,18},{19,19},{4,4},{5,5... | collective-permute-start | bytes 307208 | tf_op jit(solution)/shard_map/ppermute | solution.py:451
  9.4 8.8 %collective-permute-start.2 = (bf16[400,128]{1,0:T(8,128)(2,1)S(1)}, bf16[400,128]{1,0:T(8,128)(2,1)S(1)}, u32[]{:S(2)}, u32[]{:S(2)}) collective-permute-start(bf16[400,128]{1,0:T(8,128)(2,1)S(1)} %broadcast_select_fusion.9), channel_id=1, source_target_pairs={{0,16},{1,17},{2,0},{3,1},{16,18},{17,19},{18,2},{19,3},{4,20},{5,... | collective-permute-start | bytes 307208 | tf_op jit(solution)/shard_map/ppermute | solution.py:451
  9.6 8.7 %collective-permute-start.3 = (bf16[400,128]{1,0:T(8,128)(2,1)S(1)}, bf16[400,128]{1,0:T(8,128)(2,1)S(1)}, u32[]{:S(2)}, u32[]{:S(2)}) collective-permute-start(bf16[400,128]{1,0:T(8,128)(2,1)S(1)} %broadcast_select_fusion.8), channel_id=1, source_target_pairs={{0,17},{1,16},{2,1},{3,0},{16,19},{17,18},{18,3},{19,2},{4,21},{5,... | collective-permute-start | bytes 307208 | tf_op jit(solution)/shard_map/ppermute | solution.py:451
  10.8 4.1 %copy-start.19 = (bf16[192]{0:T(256)(128)(2,1)S(1)}, bf16[192]{0:T(256)(128)(2,1)}, u32[]{:S(2)}) copy-start(bf16[192]{0:T(256)(128)(2,1)} %param.22) | copy-start | bytes 1156
  10.8 7.5 %collective-permute-start.1 = (bf16[400,128]{1,0:T(8,128)(2,1)S(1)}, bf16[400,128]{1,0:T(8,128)(2,1)S(1)}, u32[]{:S(2)}, u32[]{:S(2)}) collective-permute-start(bf16[400,128]{1,0:T(8,128)(2,1)S(1)} %broadcast_select_fusion.10), channel_id=1, source_target_pairs={{0,1},{1,0},{2,17},{3,16},{16,3},{17,2},{18,19},{19,18},{4,5},{5,4... | collective-permute-start | bytes 307208 | tf_op jit(solution)/shard_map/ppermute | solution.py:451
  18.1 56.0 %copy-start = (bf16[208,1536]{1,0:T(8,128)(2,1)}, bf16[208,1536]{1,0:T(8,128)(2,1)S(1)}, u32[]{:S(2)}) copy-start(bf16[208,1536]{1,0:T(8,128)(2,1)S(1)} %pad_maximum_fusion.refs_0_.refs_4_.own2) | copy-start | bytes 1916932
  18.4 19.6 %collective-permute-start.10 = (bf16[4,2,192,128]{3,2,1,0:T(8,128)(2,1)S(1)}, bf16[4,2,192,128]{3,2,1,0:T(8,128)(2,1)S(1)}, u32[]{:S(2)}, u32[]{:S(2)}) collective-permute-start(bf16[4,2,192,128]{3,2,1,0:T(8,128)(2,1)S(1)} %pad_maximum_fusion.1.refs_0_.x_ref), channel_id=1, source_target_pairs={{0,8},{4,12},{8,0},{12,4},{1,9},{5,13},{9,1},{13,5},{2,10},{6,14},... | collective-permute-start | bytes 1179656 | tf_op jit(solution)/shard_map/ppermute | solution.py:30
  19.7 20.6 %collective-permute-start.11 = (bf16[4,2,192,128]{3,2,1,0:T(8,128)(2,1)S(1)}, bf16[4,2,192,128]{3,2,1,0:T(8,128)(2,1)S(1)}, u32[]{:S(2)}, u32[]{:S(2)}) collective-permute-start(bf16[4,2,192,128]{3,2,1,0:T(8,128)(2,1)S(1)} %pad_maximum_fusion.1.refs_0_.x_ref), channel_id=1, source_target_pairs={{0,12},{4,8},{8,4},{12,0},{1,13},{5,9},{9,5},{13,1},{2,14},{6,10},... | collective-permute-start | bytes 1179656 | tf_op jit(solution)/shard_map/ppermute | solution.py:30
  20.8 19.4 %collective-permute-start.9 = (bf16[4,2,192,128]{3,2,1,0:T(8,128)(2,1)S(1)}, bf16[4,2,192,128]{3,2,1,0:T(8,128)(2,1)S(1)}, u32[]{:S(2)}, u32[]{:S(2)}) collective-permute-start(bf16[4,2,192,128]{3,2,1,0:T(8,128)(2,1)S(1)} %pad_maximum_fusion.1.refs_0_.x_ref), channel_id=1, source_target_pairs={{0,4},{4,0},{8,12},{12,8},{1,5},{5,1},{9,13},{13,9},{2,6},{6,2},{1... | collective-permute-start | bytes 1179656 | tf_op jit(solution)/shard_map/ppermute | solution.py:30
  21.1 15.6 %collective-permute-start.4 = (bf16[208,768]{1,0:T(8,128)(2,1)S(1)}, bf16[208,768]{1,0:T(8,128)(2,1)S(1)}, u32[]{:S(2)}, u32[]{:S(2)}) collective-permute-start(bf16[208,768]{1,0:T(8,128)(2,1)S(1)} %pad_maximum_fusion.2.refs_0_.own1), channel_id=1, source_target_pairs={{0,3},{1,2},{2,1},{3,0},{16,18},{17,19},{18,16},{19,17},{4,7},{5,6... | collective-permute-start | bytes 958472 | tf_op jit(solution)/shard_map/ppermute | solution.py:38
  23.2 18.4 %collective-permute-start.6 = (bf16[208,768]{1,0:T(8,128)(2,1)S(1)}, bf16[208,768]{1,0:T(8,128)(2,1)S(1)}, u32[]{:S(2)}, u32[]{:S(2)}) collective-permute-start(bf16[208,768]{1,0:T(8,128)(2,1)S(1)} %pad_maximum_fusion.2.refs_0_.own1), channel_id=1, source_target_pairs={{0,1},{1,0},{2,3},{3,2},{4,5},{5,4},{6,7},{7,6},{8,9},{9,8},{10,11... | collective-permute-start | bytes 958472 | tf_op jit(solution)/shard_map/ppermute | solution.py:30
  36.7 4.9 %collective-permute-start.5 = (bf16[208,768]{1,0:T(8,128)(2,1)S(1)}, bf16[208,768]{1,0:T(8,128)(2,1)S(1)}, u32[]{:S(2)}, u32[]{:S(2)}) collective-permute-start(bf16[208,768]{1,0:T(8,128)(2,1)S(1)} %collective-permute-done.4.refs_1_), channel_id=1, source_target_pairs={{0,16},{16,0},{1,17},{17,1},{2,18},{18,2},{3,19},{19,3},{4,20},{20... | collective-permute-start | bytes 958472 | tf_op jit(solution)/shard_map/ppermute | solution.py:30
  38.0 29.6 %collective-permute-start.7 = (bf16[208,1536]{1,0:T(8,128)(2,1)S(1)}, bf16[208,1536]{1,0:T(8,128)(2,1)S(1)}, u32[]{:S(2)}, u32[]{:S(2)}) collective-permute-start(bf16[208,1536]{1,0:T(8,128)(2,1)S(1)} %pad_maximum_fusion.refs_0_.refs_4_.own2), channel_id=1, source_target_pairs={{0,3},{1,2},{2,1},{3,0},{16,18},{17,19},{18,16},{19,17},{4,7},{5,6... | collective-permute-start | bytes 1916936 | tf_op jit(solution)/shard_map/ppermute | solution.py:38
  41.6 16.5 %copy-start.2 = (bf16[832,512]{1,0:T(8,128)(2,1)}, bf16[832,512]{1,0:T(8,128)(2,1)S(1)}, u32[]{:S(2)}) copy-start(bf16[832,512]{1,0:T(8,128)(2,1)S(1)} %get-tuple-element.97.xn) | copy-start | bytes 2555908
  43.5 1.7 %collective-permute-start.12 = (bf16[1,3,64,512]{3,2,1,0:T(8,128)(2,1)S(1)}, bf16[1,3,64,512]{3,2,1,0:T(8,128)(2,1)S(1)}, u32[]{:S(2)}, u32[]{:S(2)}) collective-permute-start(bf16[1,3,64,512]{3,2,1,0:T(8,128)(2,1)S(1)} %get-tuple-element.209), channel_id=1, source_target_pairs={{0,16},{16,0},{1,17},{17,1},{2,18},{18,2},{3,19},{19,3},{4,20},{20... | collective-permute-start | bytes 589832 | tf_op jit(solution)/shard_map/ppermute | solution.py:30
  44.1 1.4 %collective-permute-start.13 = (bf16[1,3,64,512]{3,2,1,0:T(8,128)(2,1)S(1)}, bf16[1,3,64,512]{3,2,1,0:T(8,128)(2,1)S(1)}, u32[]{:S(2)}, u32[]{:S(2)}) collective-permute-start(bf16[1,3,64,512]{3,2,1,0:T(8,128)(2,1)S(1)} %get-tuple-element.208), channel_id=1, source_target_pairs={{0,16},{16,0},{1,17},{17,1},{2,18},{18,2},{3,19},{19,3},{4,20},{20... | collective-permute-start | bytes 589832 | tf_op jit(solution)/shard_map/ppermute | solution.py:30
  44.2 26.7 %collective-permute-start.8 = (bf16[208,1536]{1,0:T(8,128)(2,1)S(1)}, bf16[208,1536]{1,0:T(8,128)(2,1)S(1)}, u32[]{:S(2)}, u32[]{:S(2)}) collective-permute-start(bf16[208,1536]{1,0:T(8,128)(2,1)S(1)} %pad_maximum_fusion.refs_0_.refs_4_.own2), channel_id=1, source_target_pairs={{0,1},{1,0},{2,3},{3,2},{4,5},{5,4},{6,7},{7,6},{8,9},{9,8},{10,11... | collective-permute-start | bytes 1916936 | tf_op jit(solution)/shard_map/ppermute | solution.py:30
  56.3 1.5 %collective-permute-start.14 = (bf16[1,3,64,512]{3,2,1,0:T(8,128)(2,1)S(1)}, bf16[1,3,64,512]{3,2,1,0:T(8,128)(2,1)S(1)}, u32[]{:S(2)}, u32[]{:S(2)}) collective-permute-start(bf16[1,3,64,512]{3,2,1,0:T(8,128)(2,1)S(1)} %get-tuple-element.207), channel_id=1, source_target_pairs={{0,16},{16,0},{1,17},{17,1},{2,18},{18,2},{3,19},{19,3},{4,20},{20... | collective-permute-start | bytes 589832 | tf_op jit(solution)/shard_map/ppermute | solution.py:30
  56.6 1.4 %collective-permute-start.15 = (bf16[1,3,64,512]{3,2,1,0:T(8,128)(2,1)S(1)}, bf16[1,3,64,512]{3,2,1,0:T(8,128)(2,1)S(1)}, u32[]{:S(2)}, u32[]{:S(2)}) collective-permute-start(bf16[1,3,64,512]{3,2,1,0:T(8,128)(2,1)S(1)} %get-tuple-element.206), channel_id=1, source_target_pairs={{0,16},{16,0},{1,17},{17,1},{2,18},{18,2},{3,19},{19,3},{4,20},{20... | collective-permute-start | bytes 589832 | tf_op jit(solution)/shard_map/ppermute | solution.py:30
  67.6 12.7 %copy-start.4 = (bf16[208,1536]{1,0:T(8,128)(2,1)}, bf16[208,1536]{1,0:T(8,128)(2,1)S(1)}, u32[]{:S(2)}) copy-start(bf16[208,1536]{1,0:T(8,128)(2,1)S(1)} %collective-permute-done.7.refs_1_.refs_5_) | copy-start | bytes 1916932
  70.9 9.3 %copy-start.5 = (bf16[208,1536]{1,0:T(8,128)(2,1)}, bf16[208,1536]{1,0:T(8,128)(2,1)S(1)}, u32[]{:S(2)}) copy-start(bf16[208,1536]{1,0:T(8,128)(2,1)S(1)} %collective-permute-done.8.refs_3_.refs_7_) | copy-start | bytes 1916932
  70.9 3.1 %collective-permute-start.16 = (bf16[208,1536]{1,0:T(8,128)(2,1)S(1)}, bf16[208,1536]{1,0:T(8,128)(2,1)S(1)}, u32[]{:S(2)}, u32[]{:S(2)}) collective-permute-start(bf16[208,1536]{1,0:T(8,128)(2,1)S(1)} %collective-permute-done.7.refs_1_.refs_5_), channel_id=1, source_target_pairs={{0,16},{16,0},{1,17},{17,1},{2,18},{18,2},{3,19},{19,3},{4,20},{20... | collective-permute-start | bytes 1916936 | tf_op jit(solution)/shard_map/ppermute | solution.py:30
  71.8 2.2 %collective-permute-start.17 = (bf16[208,768]{1,0:T(8,128)(2,1)S(1)}, bf16[208,768]{1,0:T(8,128)(2,1)S(1)}, u32[]{:S(2)}, u32[]{:S(2)}) collective-permute-start(bf16[208,768]{1,0:T(8,128)(2,1)S(1)} %get-tuple-element.96), channel_id=1, source_target_pairs={{0,16},{16,0},{1,17},{17,1},{2,18},{18,2},{3,19},{19,3},{4,20},{20... | collective-permute-start | bytes 958472 | tf_op jit(solution)/shard_map/ppermute | solution.py:30
  71.8 16.3 %collective-permute-start.19 = (bf16[208,768]{1,0:T(8,128)(2,1)S(1)}, bf16[208,768]{1,0:T(8,128)(2,1)S(1)}, u32[]{:S(2)}, u32[]{:S(2)}) collective-permute-start(bf16[208,768]{1,0:T(8,128)(2,1)S(1)} %get-tuple-element.106), channel_id=1, source_target_pairs={{0,1},{1,0},{2,3},{3,2},{4,5},{5,4},{6,7},{7,6},{8,9},{9,8},{10,11... | collective-permute-start | bytes 958472 | tf_op jit(solution)/shard_map/ppermute | solution.py:30
  74.0 16.5 %collective-permute-start.18 = (bf16[208,768]{1,0:T(8,128)(2,1)S(1)}, bf16[208,768]{1,0:T(8,128)(2,1)S(1)}, u32[]{:S(2)}, u32[]{:S(2)}) collective-permute-start(bf16[208,768]{1,0:T(8,128)(2,1)S(1)} %shard_map.258), channel_id=1, source_target_pairs={{0,3},{1,2},{2,1},{3,0},{16,18},{17,19},{18,16},{19,17},{4,7},{5,6... | collective-permute-start | bytes 958472 | tf_op jit(solution)/shard_map/ppermute | solution.py:38
  74.1 6.2 %copy-start.6 = (bf16[208,1536]{1,0:T(8,128)(2,1)}, bf16[208,1536]{1,0:T(8,128)(2,1)S(1)}, u32[]{:S(2)}) copy-start(bf16[208,1536]{1,0:T(8,128)(2,1)S(1)} %collective-permute-done.16.refs_2_.refs_6_) | copy-start | bytes 1916932
  80.3 7.5 %collective-permute-start.23 = (bf16[208,512]{1,0:T(8,128)(2,1)S(1)}, bf16[208,512]{1,0:T(8,128)(2,1)S(1)}, u32[]{:S(2)}, u32[]{:S(2)}) collective-permute-start(bf16[208,512]{1,0:T(8,128)(2,1)S(1)} %get-tuple-element.197), channel_id=1, source_target_pairs={{0,16},{16,0},{1,17},{17,1},{2,18},{18,2},{3,19},{19,3},{4,20},{20... | collective-permute-start | bytes 638984 | tf_op jit(solution)/shard_map/ppermute | solution.py:30
  82.2 5.7 %collective-permute-start.24 = (bf16[208,512]{1,0:T(8,128)(2,1)S(1)}, bf16[208,512]{1,0:T(8,128)(2,1)S(1)}, u32[]{:S(2)}, u32[]{:S(2)}) collective-permute-start(bf16[208,512]{1,0:T(8,128)(2,1)S(1)} %get-tuple-element.196), channel_id=1, source_target_pairs={{0,16},{16,0},{1,17},{17,1},{2,18},{18,2},{3,19},{19,3},{4,20},{20... | collective-permute-start | bytes 638984 | tf_op jit(solution)/shard_map/ppermute | solution.py:30
  82.3 5.6 %collective-permute-start.25 = (bf16[208,512]{1,0:T(8,128)(2,1)S(1)}, bf16[208,512]{1,0:T(8,128)(2,1)S(1)}, u32[]{:S(2)}, u32[]{:S(2)}) collective-permute-start(bf16[208,512]{1,0:T(8,128)(2,1)S(1)} %get-tuple-element.195), channel_id=1, source_target_pairs={{0,16},{16,0},{1,17},{17,1},{2,18},{18,2},{3,19},{19,3},{4,20},{20... | collective-permute-start | bytes 638984 | tf_op jit(solution)/shard_map/ppermute | solution.py:30
  87.8 6.8 %copy-start.8 = (bf16[192,2,256]{2,1,0:T(2,128)(2,1)S(1)}, bf16[192,2,256]{2,1,0:T(2,128)(2,1)}, u32[]{:S(2)}) copy-start(bf16[192,2,256]{2,1,0:T(2,128)(2,1)} %param.29) | copy-start | bytes 589828
  88.0 32.0 %copy-start.7 = (f32[208,1536]{1,0:T(8,128)S(1)}, f32[208,1536]{1,0:T(8,128)}, u32[]{:S(2)}) copy-start(f32[208,1536]{1,0:T(8,128)} %get-tuple-element.127.own2) | copy-start | bytes 3833860
  90.4 29.5 %collective-permute-start.26 = (bf16[208,1536]{1,0:T(8,128)(2,1)S(1)}, bf16[208,1536]{1,0:T(8,128)(2,1)S(1)}, u32[]{:S(2)}, u32[]{:S(2)}) collective-permute-start(bf16[208,1536]{1,0:T(8,128)(2,1)S(1)} %shard_map.262), channel_id=1, source_target_pairs={{0,3},{1,2},{2,1},{3,0},{16,18},{17,19},{18,16},{19,17},{4,7},{5,6... | collective-permute-start | bytes 1916936 | tf_op jit(solution)/shard_map/ppermute | solution.py:38
  90.4 29.6 %collective-permute-start.27 = (bf16[208,1536]{1,0:T(8,128)(2,1)S(1)}, bf16[208,1536]{1,0:T(8,128)(2,1)S(1)}, u32[]{:S(2)}, u32[]{:S(2)}) collective-permute-start(bf16[208,1536]{1,0:T(8,128)(2,1)S(1)} %get-tuple-element.119), channel_id=1, source_target_pairs={{0,1},{1,0},{2,3},{3,2},{4,5},{5,4},{6,7},{7,6},{8,9},{9,8},{10,11... | collective-permute-start | bytes 1916936 | tf_op jit(solution)/shard_map/ppermute | solution.py:30
  91.9 10.9 %collective-permute-start.20 = (bf16[4,2,192,128]{3,2,1,0:T(8,128)(2,1)S(1)}, bf16[4,2,192,128]{3,2,1,0:T(8,128)(2,1)S(1)}, u32[]{:S(2)}, u32[]{:S(2)}) collective-permute-start(bf16[4,2,192,128]{3,2,1,0:T(8,128)(2,1)S(1)} %get-tuple-element.108), channel_id=1, source_target_pairs={{0,4},{4,0},{8,12},{12,8},{1,5},{5,1},{9,13},{13,9},{2,6},{6,2},{1... | collective-permute-start | bytes 1179656 | tf_op jit(solution)/shard_map/ppermute | solution.py:30
  93.1 18.0 %collective-permute-start.21 = (bf16[4,2,192,128]{3,2,1,0:T(8,128)(2,1)S(1)}, bf16[4,2,192,128]{3,2,1,0:T(8,128)(2,1)S(1)}, u32[]{:S(2)}, u32[]{:S(2)}) collective-permute-start(bf16[4,2,192,128]{3,2,1,0:T(8,128)(2,1)S(1)} %get-tuple-element.109), channel_id=1, source_target_pairs={{0,8},{4,12},{8,0},{12,4},{1,9},{5,13},{9,1},{13,5},{2,10},{6,14},... | collective-permute-start | bytes 1179656 | tf_op jit(solution)/shard_map/ppermute | solution.py:30
  94.4 17.9 %collective-permute-start.22 = (bf16[4,2,192,128]{3,2,1,0:T(8,128)(2,1)S(1)}, bf16[4,2,192,128]{3,2,1,0:T(8,128)(2,1)S(1)}, u32[]{:S(2)}, u32[]{:S(2)}) collective-permute-start(bf16[4,2,192,128]{3,2,1,0:T(8,128)(2,1)S(1)} %get-tuple-element.110), channel_id=1, source_target_pairs={{0,12},{4,8},{8,4},{12,0},{1,13},{5,9},{9,5},{13,1},{2,14},{6,10},... | collective-permute-start | bytes 1179656 | tf_op jit(solution)/shard_map/ppermute | solution.py:30
  120.7 2.5 %copy-start.16 = (bf16[192]{0:T(256)(128)(2,1)S(1)}, bf16[192]{0:T(256)(128)(2,1)}, u32[]{:S(2)}) copy-start(bf16[192]{0:T(256)(128)(2,1)} %param.28) | copy-start | bytes 1156
  120.8 9.3 %copy-start.1 = (bf16[208,1536]{1,0:T(8,128)(2,1)S(1)}, bf16[208,1536]{1,0:T(8,128)(2,1)}, u32[]{:S(2)}) copy-start(bf16[208,1536]{1,0:T(8,128)(2,1)} %copy-done) | copy-start | bytes 1916932
  121.7 5.9 %collective-permute-start.32 = (bf16[208,768]{1,0:T(8,128)(2,1)}, bf16[208,768]{1,0:T(8,128)(2,1)S(1)}, u32[]{:S(2)}, u32[]{:S(2)}) collective-permute-start(bf16[208,768]{1,0:T(8,128)(2,1)} %get-tuple-element.192), channel_id=1, source_target_pairs={{0,16},{16,0},{1,17},{17,1},{2,18},{18,2},{3,19},{19,3},{4,20},{20... | collective-permute-start | bytes 958472 | tf_op jit(solution)/shard_map/ppermute | solution.py:30
  122.7 5.0 %collective-permute-start.33 = (bf16[208,768]{1,0:T(8,128)(2,1)}, bf16[208,768]{1,0:T(8,128)(2,1)S(1)}, u32[]{:S(2)}, u32[]{:S(2)}) collective-permute-start(bf16[208,768]{1,0:T(8,128)(2,1)} %get-tuple-element.191), channel_id=1, source_target_pairs={{0,16},{16,0},{1,17},{17,1},{2,18},{18,2},{3,19},{19,3},{4,20},{20... | collective-permute-start | bytes 958472 | tf_op jit(solution)/shard_map/ppermute | solution.py:30
  122.7 7.4 %collective-permute-start.34 = (bf16[208,768]{1,0:T(8,128)(2,1)}, bf16[208,768]{1,0:T(8,128)(2,1)S(1)}, u32[]{:S(2)}, u32[]{:S(2)}) collective-permute-start(bf16[208,768]{1,0:T(8,128)(2,1)} %get-tuple-element.190), channel_id=1, source_target_pairs={{0,16},{16,0},{1,17},{17,1},{2,18},{18,2},{3,19},{19,3},{4,20},{20... | collective-permute-start | bytes 958472 | tf_op jit(solution)/shard_map/ppermute | solution.py:30
  123.3 11.0 %collective-permute-start.28 = (bf16[2,192,128]{2,1,0:T(8,128)(2,1)S(1)}, bf16[2,192,128]{2,1,0:T(8,128)(2,1)S(1)}, u32[]{:S(2)}, u32[]{:S(2)}) collective-permute-start(bf16[2,192,128]{2,1,0:T(8,128)(2,1)S(1)} %get-tuple-element.120), channel_id=1, source_target_pairs={{0,0},{1,1},{16,2},{17,3},{2,16},{3,17},{18,18},{19,19},{4,4},{5,5... | collective-permute-start | bytes 294920 | tf_op jit(solution)/shard_map/ppermute | solution.py:605
  125.9 8.4 %collective-permute-start.29 = (bf16[2,192,128]{2,1,0:T(8,128)(2,1)S(1)}, bf16[2,192,128]{2,1,0:T(8,128)(2,1)S(1)}, u32[]{:S(2)}, u32[]{:S(2)}) collective-permute-start(bf16[2,192,128]{2,1,0:T(8,128)(2,1)S(1)} %get-tuple-element.121), channel_id=1, source_target_pairs={{1,0},{0,1},{17,2},{16,3},{3,16},{2,17},{19,18},{18,19},{5,4},{4,5... | collective-permute-start | bytes 294920 | tf_op jit(solution)/shard_map/ppermute | solution.py:605
  127.7 8.5 %collective-permute-start.30 = (bf16[2,192,128]{2,1,0:T(8,128)(2,1)S(1)}, bf16[2,192,128]{2,1,0:T(8,128)(2,1)S(1)}, u32[]{:S(2)}, u32[]{:S(2)}) collective-permute-start(bf16[2,192,128]{2,1,0:T(8,128)(2,1)S(1)} %get-tuple-element.122), channel_id=1, source_target_pairs={{16,0},{17,1},{0,2},{1,3},{18,16},{19,17},{2,18},{3,19},{20,4},{21... | collective-permute-start | bytes 294920 | tf_op jit(solution)/shard_map/ppermute | solution.py:605
  127.7 8.5 %collective-permute-start.31 = (bf16[2,192,128]{2,1,0:T(8,128)(2,1)S(1)}, bf16[2,192,128]{2,1,0:T(8,128)(2,1)S(1)}, u32[]{:S(2)}, u32[]{:S(2)}) collective-permute-start(bf16[2,192,128]{2,1,0:T(8,128)(2,1)S(1)} %get-tuple-element.123), channel_id=1, source_target_pairs={{17,0},{16,1},{1,2},{0,3},{19,16},{18,17},{3,18},{2,19},{21,4},{20... | collective-permute-start | bytes 294920 | tf_op jit(solution)/shard_map/ppermute | solution.py:605
  130.6 5.7 %collective-permute-start.35 = (f32[8,192]{1,0:T(8,128)S(1)}, f32[8,192]{1,0:T(8,128)S(1)}, u32[]{:S(2)}, u32[]{:S(2)}) collective-permute-start(f32[8,192]{1,0:T(8,128)S(1)} %shard_map.265), channel_id=1, source_target_pairs={{0,4},{4,0},{8,12},{12,8},{1,5},{5,1},{9,13},{13,9},{2,6},{6,2},{1... | collective-permute-start | bytes 18440 | tf_op jit(solution)/shard_map/ppermute | solution.py:30
  136.4 6.0 %collective-permute-start.36 = (f32[8,192]{1,0:T(8,128)S(1)}, f32[8,192]{1,0:T(8,128)S(1)}, u32[]{:S(2)}, u32[]{:S(2)}) collective-permute-start(f32[8,192]{1,0:T(8,128)S(1)} %add.183), channel_id=1, source_target_pairs={{0,8},{4,12},{8,0},{12,4},{1,9},{5,13},{9,1},{13,5},{2,10},{6,14},... | collective-permute-start | bytes 18440 | tf_op jit(solution)/shard_map/ppermute | solution.py:30
  (11 other events, 15.4 us)
